TPU v7x, 32 devices: a whole 2x2x4 slice. The times are simulated.
32 devices in a mesh: ctx: 2 (over x), tp: 4 (over y, core), rep: 4 (over z).
Axes of the slice: x: 2, y: 2, z: 4, core: 2. Of those that a mesh axis runs over, the one named last changes fastest.
Arguments:
- spikes: int32 [8, 512, 3584], P('rep', 'ctx'), may hold values from 0 to 4
- dec_spikes: int32 [4, 8, 3584], P(None, 'rep'), may hold values from 0 to 4
- thresholds: int32 [3584], replicated, may hold values from 1 to 3
- in_scale: float32 [3584], replicated, may hold values from 0.3 to 3
- qkv_weight: bfloat16 [3, 3584, 2048], P(None, ('ctx', 'rep'), 'tp'), may hold values from -0.09375 to 0.09375
- out_weight: bfloat16 [2048, 3584], P('tp', ('ctx', 'rep')), may hold values from -0.1875 to 0.1875
- head_gain: float32 [16, 128], P('tp'), may hold values from 0.5 to 2
- prior_state: float32 [8, 16, 128, 128], P('rep', 'tp'), may hold values from -256 to 256
- lengths: int32 [8], P('rep'), may hold values from 128 to 512, as said below
Outputs:
- block_out: bfloat16 [8, 512, 3584], P('rep', 'ctx', 'tp')
- decode_out: bfloat16 [4, 8, 3584], P(None, 'rep', 'tp')
Inputs may be any that keep to these rules, and one draw needn't show every extreme that they name: `lengths`: one request in every draw has a full block of 512 prompt positions.
All inputs are finite; a program needn't handle non-finite values.
Results may differ from a plain program's by a relative error of at most 0.012.
Values may be sent and summed in bfloat16 or wider, within the bound.
No kernel may reach another device: no remote copies, remote signals or barrier semaphores. Data moves between devices by JAX's collectives and lax.ppermute only.
A program may use at most 128 MiB of HBM per device.

v0:
```python
import jax
import jax.numpy as jnp
from jax import lax
from jax.sharding import PartitionSpec as P


def carried_in(value, axis, combine, identity):
    peers, here = (lax.axis_size(axis), lax.axis_index(axis))
    everything = lax.all_gather(value, axis)
    start = jnp.broadcast_to(jnp.asarray(identity, value.dtype), value.shape)

    def turn(k, before):
        reached = k < here
        new = combine(before, everything[k])
        return jnp.where(reached, new, before)

    return lax.fori_loop(0, peers, turn, start)


def normalize(value_rows, gain):
    mean = jnp.mean(value_rows * value_rows, axis=-1, keepdims=True)
    return (value_rows * lax.rsqrt(mean + 1e-06) * gain).astype(jnp.bfloat16)


def local(
    spikes,
    dec_spikes,
    thresholds,
    in_scale,
    qkv_weight,
    out_weight,
    head_gain,
    prior_state,
    lengths,
):
    groups, block, width = spikes.shape
    steps = dec_spikes.shape[0]
    heads, head = head_gain.shape
    inner = heads * head
    prompt_rows = groups * block
    topmost_precision = lax.Precision.HIGHEST
    context_position = lax.axis_index("ctx")
    tokens_x = (jnp.where(spikes >= thresholds, spikes, 0).astype(jnp.float32) * in_scale).astype(
        jnp.bfloat16
    )
    dec_x = (
        jnp.where(dec_spikes >= thresholds, dec_spikes, 0).astype(jnp.float32) * in_scale
    ).astype(jnp.bfloat16)
    rows_all = jnp.concatenate(
        [tokens_x.reshape(prompt_rows, width), dec_x.reshape(steps * groups, width)], 0
    )
    full = lax.all_gather(qkv_weight, ("ctx", "rep"), axis=1, tiled=True)
    projected = jnp.einsum("rd,cde->rce", rows_all, full, preferred_element_type=jnp.float32)
    projected = projected.astype(jnp.bfloat16)
    prompt = projected[:prompt_rows].reshape(groups, block, 3, heads, head)
    decoded = projected[prompt_rows:].reshape(steps, groups, 3, heads, head)
    query = prompt[:, :, 0]
    value_rows = prompt[:, :, 2]
    positions = context_position * block + jnp.arange(block)
    live = positions[None, :] < lengths[:, None]
    keys = jnp.where(live[:, :, None, None], prompt[:, :, 1], jnp.zeros_like(prompt[:, :, 1]))
    block_state = jnp.einsum(
        "gthk,gthv->ghkv", keys, value_rows, preferred_element_type=jnp.float32
    )
    before = carried_in(
        block_state, "ctx", lambda earlier, later: earlier + later, jnp.zeros_like(block_state)
    )
    carried = (prior_state + before).astype(jnp.bfloat16)
    inter = jnp.einsum("gthk,ghkv->gthv", query, carried, preferred_element_type=jnp.float32)
    scores = jnp.einsum("gthk,gshk->ghts", query, keys, preferred_element_type=jnp.float32)
    causal = jnp.arange(block)[:, None] >= jnp.arange(block)[None, :]
    weights = jnp.where(causal, scores, 0.0).astype(jnp.bfloat16)
    intra = jnp.einsum("ghts,gshv->gthv", weights, value_rows, preferred_element_type=jnp.float32)
    hidden = normalize(inter + intra, head_gain).reshape(prompt_rows, inner)
    dec_query = decoded[:, :, 0].astype(jnp.float32)
    dec_keys = decoded[:, :, 1].astype(jnp.float32)
    dec_values = decoded[:, :, 2].astype(jnp.float32)
    state_readouts = []
    memory_state = prior_state + lax.psum(block_state, "ctx")
    for decode_step_body in range(steps):
        memory_state = memory_state + jnp.einsum(
            "ghk,ghv->ghkv",
            dec_keys[decode_step_body],
            dec_values[decode_step_body],
            precision=topmost_precision,
        )
        state_readouts.append(
            jnp.einsum(
                "ghk,ghkv->ghv",
                dec_query[decode_step_body],
                memory_state,
                precision=topmost_precision,
            )
        )
    dec_hidden = normalize(jnp.stack(state_readouts), head_gain).reshape(steps * groups, inner)
    hidden_all = jnp.concatenate([hidden, dec_hidden], 0)
    columns = width // lax.axis_size("tp")
    residual = lax.dynamic_slice_in_dim(rows_all, lax.axis_index("tp") * columns, columns, 1)
    terms = jnp.dot(
        hidden_all,
        lax.all_gather(out_weight, ("ctx", "rep"), axis=1, tiled=True),
        preferred_element_type=jnp.float32,
    )
    summed = lax.psum_scatter(terms, "tp", scatter_dimension=1, tiled=True)
    result = (residual.astype(jnp.float32) + summed).astype(jnp.bfloat16)
    block_out = result[:prompt_rows].reshape(groups, block, columns)
    decode_out = result[prompt_rows:].reshape(steps, groups, columns)
    return (block_out, decode_out)


def solution(mesh):
    return jax.shard_map(
        local,
        mesh=mesh,
        in_specs=(
            P("rep", "ctx", None),
            P(None, "rep", None),
            P(),
            P(),
            P(None, ("ctx", "rep"), "tp"),
            P("tp", ("ctx", "rep")),
            P("tp", None),
            P("rep", "tp", None, None),
            P("rep"),
        ),
        out_specs=(P("rep", "ctx", "tp"), P(None, "rep", "tp")),
        check_vma=False,
    )
```

profile of v0, /device:TPU:0, one launch (start us, length us, event | category | flops | bytes accessed | tf_op | source)
XLA Modules:
  0.0 388.7 jit_solution(5561676269352590739)
XLA Ops:
  7.2 0.7 all-gather.5.cloned.1.call-update
  7.9 1.0 fusion.48
  9.0 0.7 broadcast_compare_fusion
  9.7 6.1 %fusion.2 = bf16[2,256,3584]{2,1,0:T(8,128)(2,1)} fusion(s32[2,256,3584]{2,1,0:T(8,128)} %param.11, f32[3584]{0:T(1024)} %param.14, s32[3584]{0:T(1024)} %param.13), kind=kLoop, calls=%fused_computation.4 | loop fusion | flops 9175040 | bytes 11038720 | tf_op jit(solution)/shard_map/convert_element_type | solution.py:43
  15.8 154.3 %all-gather.5.cloned.1.call-done = bf16[3,3584,512]{2,1,0:T(8,128)(2,1)} async-done(((bf16[3,448,512]{2,1,0:T(8,128)(2,1)}), bf16[3,3584,512]{2,1,0:T(8,128)(2,1)}) %all-gather.5.cloned.1.call-update) | async-done | bytes 11010064 | tf_op jit(solution)/shard_map/all_gather | solution.py:52
  170.1 10.7 %fusion.7 = bf16[520,3,512]{2,0,1:T(8,128)(2,1)} fusion(bf16[3,3584,512]{2,1,0:T(8,128)(2,1)} %all-gather.5.cloned.1.call-done, bf16[8,3584]{1,0:T(8,128)(2,1)S(1)} %reshape.138, bf16[512,3584]{1,0:T(8,128)(2,1)} %bitcast.123), kind=kOutput, calls=%fused_computation.13 | convolution fusion | flops 5733478400 | bytes 16334848 | tf_op jit(solution)/shard_map/rd,cde->rce/dot_general | solution.py:53
  180.9 1.5 slice.103
  182.4 0.4 reshape.139
  182.8 0.5 fusion.69
  183.4 0.8 copy-done.1
  184.3 1.2 fusion.25
  185.6 19.6 %all-gather.9.cloned.1.call-done = f32[4,4,128,128]{3,2,1,0:T(8,128)} async-done(((f32[2,4,128,128]{3,2,1,0:T(8,128)}), f32[4,4,128,128]{3,2,1,0:T(8,128)}) %all-gather.9.cloned.1.call-update) | async-done | bytes 1048592 | tf_op jit(solution)/shard_map/all_gather | solution.py:9
  205.3 0.7 all-reduce.2.cloned.1.call-update
  206.0 0.5 all-gather.7.cloned.1.call-update
  206.6 1.3 slice.107
  208.0 0.7 reshape.141
  208.8 2.6 while.14
  208.8 1.3 add_select_fusion.2
  210.1 1.2 add_select_fusion.2
  211.4 1.3 fusion.26
  212.7 2.2 multiply_reduce_fusion
  215.5 22.1 %all-reduce.2.cloned.1.call-done = f32[2,4,128,128]{3,2,1,0:T(8,128)} async-done(((f32[2,4,128,128]{3,2,1,0:T(8,128)}), f32[2,4,128,128]{3,2,1,0:T(8,128)}) %all-reduce.2.cloned.1.call-update) | async-done | bytes 524304 | tf_op jit(solution)/shard_map/psum | solution.py:79
  237.6 1.2 multiply_add_fusion.2
  239.2 0.5 fusion.24
  239.6 0.6 fusion.27
  240.2 0.7 fusion.21
  241.2 65.4 %all-gather.7.cloned.1.call-done = bf16[512,3584]{0,1:T(8,128)(2,1)} async-done(((bf16[512,448]{0,1:T(8,128)(2,1)}), bf16[512,3584]{0,1:T(8,128)(2,1)}) %all-gather.7.cloned.1.call-update) | async-done | bytes 3670032 | tf_op jit(solution)/shard_map/all_gather | solution.py:101
  306.6 7.2 %fusion.16 = f32[520,3584]{1,0:T(8,128)} fusion(bf16[512,3584]{0,1:T(8,128)(2,1)} %all-gather.7.cloned.1.call-done, bf16[8,512]{1,0:T(8,128)(2,1)S(1)} %fusion.49, bf16[512,512]{1,0:T(8,128)(2,1)S(1)} %bitcast.128), kind=kOutput, calls=%fused_computation.22 | convolution fusion | flops 1909473280 | bytes 11657216 | tf_op jit(solution)/shard_map/dot_general | solution.py:99
  313.8 64.9 %reduce-scatter.2.cloned.1.call-done = f32[520,896]{1,0:T(8,128)} async-done(((f32[520,3584]{1,0:T(8,128)}), f32[520,896]{1,0:T(8,128)}) %reduce-scatter.2.cloned.1.call-update) | async-done | bytes 1863696 | tf_op jit(solution)/shard_map/reduce_scatter | solution.py:104
  378.6 1.9 add_convert_fusion
  380.5 1.0 slice.120
  381.5 0.6 reshape.151
  (31 shorter events, 1.5 us)
Async XLA Ops:
  7.2 163.0 %all-gather.5.cloned.1.call-start = ((), (), s32[]{:S(2)}) async-start(), calls=%async_computation.1 | async-start | bytes 12386304 | tf_op jit(solution)/shard_map/all_gather | solution.py:52
  7.9 197.4 %all-gather.9.cloned.1.call-start = ((), (), s32[]{:S(2)}) async-start(), calls=%async_computation.5 | async-start | bytes 1572864 | tf_op jit(solution)/shard_map/all_gather | solution.py:9
  183.3 0.8 copy-start.1
  183.4 1.0 copy-start.3
  205.2 32.3 %all-reduce.2.cloned.1.call-start = ((), (), s32[]{:S(2)}) async-start(), calls=%async_computation.2 | async-start | bytes 1048576 | tf_op jit(solution)/shard_map/psum | solution.py:79
  206.0 100.6 %all-gather.7.cloned.1.call-start = ((), (), s32[]{:S(2)}) async-start(), calls=%async_computation.3 | async-start | bytes 4128768 | tf_op jit(solution)/shard_map/all_gather | solution.py:101
  206.5 172.1 %reduce-scatter.2.cloned.1.call-start = ((), (), s32[]{:S(2)}) async-start(), calls=%async_computation.4 | async-start | bytes 9318400 | tf_op jit(solution)/shard_map/reduce_scatter | solution.py:104
  208.7 2.6 copy-start
  208.8 3.9 %copy-start.2 = (bf16[2,256,1,4,128]{4,3,1,0,2:T(4,128)(2,1)S(1)}, bf16[2,256,1,4,128]{4,3,1,0,2:T(4,128)(2,1)}, u32[]{:S(2)}) copy-start(bf16[2,256,1,4,128]{4,3,1,0,2:T(4,128)(2,1)} %copy-done.1) | copy-start | bytes 1572868
  211.4 3.6 copy-start.4
Sparse Core Ops, SparseCore 0:
  10.1 159.9 all-gather.4
  185.7 19.4 all-gather.8
  208.9 28.5 all-reduce.1
  239.7 66.8 all-gather.6
  313.9 64.7 reduce-scatter.1
where the time goes:
time: 389 us
  waiting for transfers between devices  328 us (84%)
  matrix products  24.8 us (6%)
  between operations  14 us (4%)
  other arithmetic  13.9 us (4%)
  local copies, waits for them, and re-layouts  7.55 us (2%)
    all_gather x1, waiting for transfers between devices, local(): full = lax.all_gather(qkv_weight, ('ctx', 'rep'), axis=1, tiled=True)  154 us
    all_gather x1, waiting for transfers between devices, local(): lax.all_gather(out_weight, ('ctx', 'rep'), axis=1, tiled=True)  65.4 us
    reduce_scatter x1, waiting for transfers between devices, local(): summed = lax.psum_scatter(terms, 'tp', scatter_dimension=1, tiled=True)  64.9 us
    psum x1, waiting for transfers between devices, local(): memory_state = prior_state + lax.psum(block_state, 'ctx')  22.1 us
    all_gather x1, waiting for transfers between devices, carried_in(): everything = lax.all_gather(value, axis)  19.6 us
    dot_general x1, matrix products, local(): jnp.einsum('rd,cde->rce', rows_all, full, preferred_element_type=jnp.floa...  10.7 us
  transfers between devices with their start and end apart: 5, of which 5 were waited for; matrix products, arithmetic and copies ran while one was open for 5% of the time, Pallas kernels for 0%

commit v1 on v0

--- a/solution.py
+++ b/solution.py
@@ -1,6 +1,8 @@
 import jax
 import jax.numpy as jnp
 from jax import lax
+from jax.experimental import pallas as pl
+from jax.experimental.pallas import tpu as pltpu
 from jax.sharding import PartitionSpec as P
 
 
@@ -22,7 +24,7 @@
     return (value_rows * lax.rsqrt(mean + 1e-06) * gain).astype(jnp.bfloat16)
 
 
-def local(
+def local_any(
     spikes,
     dec_spikes,
     thresholds,
@@ -108,9 +110,382 @@
     return (block_out, decode_out)
 
 
+AXES = ("ctx", "tp", "rep")
+VMEM_LIMIT = 60 * 1024 * 1024
+DEC_PAD = 16
+
+
+def fits(mesh):
+    shape = dict(mesh.shape)
+    return (shape["ctx"], shape["tp"], shape["rep"]) == (2, 4, 4)
+
+
+def move(value, target):
+    sizes = [lax.axis_size(name) for name in AXES]
+    pairs = []
+    for c in range(sizes[0]):
+        for t in range(sizes[1]):
+            for r in range(sizes[2]):
+                to = target(c, t, r)
+                if to is not None:
+                    at = (c * sizes[1] + t) * sizes[2] + r
+                    pairs.append((at, (to[0] * sizes[1] + to[1]) * sizes[2] + to[2]))
+    return lax.ppermute(value, AXES, pairs)
+
+
+def to_ctx(c, t, r):
+    return (1 - c, t, r)
+
+
+def to_core(c, t, r):
+    return (c, t ^ 1, r)
+
+
+def to_y(c, t, r):
+    return (c, t ^ 2, r)
+
+
+def to_diagonal(c, t, r):
+    return (1 - c, t ^ 2, r)
+
+
+def to_pair(c, t, r):
+    return (c, t, r ^ 1)
+
+
+def mid_swap(c, t, r):
+    return (c, t, 3 - r) if r in (1, 2) else None
+
+
+def mid_to_end(c, t, r):
+    return (c, t, r ^ 1) if r in (1, 2) else None
+
+
+def params():
+    return pltpu.CompilerParams(vmem_limit_bytes=VMEM_LIMIT)
+
+
+def whole(shape):
+    return pl.BlockSpec(shape, lambda *_: (0,) * len(shape))
+
+
+def embed_kernel(parts, spikes_ref, thresholds_ref, scale_ref, out_ref):
+    counts = spikes_ref[...]
+    gated = jnp.where(counts >= thresholds_ref[...], counts, 0)
+    x = (gated.astype(jnp.float32) * scale_ref[...]).astype(jnp.bfloat16)
+    width = x.shape[1] // (2 * parts)
+    for z in range(parts):
+        first = x[:, z * width : (z + 1) * width]
+        second = x[:, (parts + z) * width : (parts + z + 1) * width]
+        out_ref[z] = jnp.concatenate([first, second], axis=1)
+
+
+def embed(spikes, thresholds, scale, parts, tile):
+    rows, width = spikes.shape
+    return pl.pallas_call(
+        lambda *refs: embed_kernel(parts, *refs),
+        grid=(rows // tile,),
+        in_specs=[
+            pl.BlockSpec((tile, width), lambda i: (i, 0)),
+            whole((1, width)),
+            whole((1, width)),
+        ],
+        out_specs=pl.BlockSpec((parts, tile, width // parts), lambda i: (0, i, 0)),
+        out_shape=jax.ShapeDtypeStruct((parts, rows, width // parts), jnp.bfloat16),
+        compiler_params=params(),
+        name="embed",
+    )(spikes, thresholds[None], scale[None])
+
+
+def weights_of(scalars, mine, other, index):
+    if len(mine) == 2:
+        flag = scalars[1] == 1
+        own = jnp.where(flag, mine[1][index], mine[0][index])
+        far = jnp.where(flag, other[1][index], other[0][index])
+    else:
+        own, far = mine[0][index], other[0][index]
+    first = scalars[0] == 0
+    return jnp.concatenate([jnp.where(first, own, far), jnp.where(first, far, own)], axis=0)
+
+
+def row_blocks(x_refs):
+    at = 0
+    for ref in x_refs:
+        rows = ref.shape[1]
+        yield ref, at, rows
+        at += rows
+
+
+def project_kernel(candidates, has_sum, scalars, *refs):
+    x_refs = refs[:4]
+    mine = refs[4 : 4 + candidates]
+    other = refs[4 + candidates : 4 + 2 * candidates]
+    out_ref = refs[-1]
+    sum_ref = refs[-2] if has_sum else None
+    for index in range(3):
+        weight = weights_of(scalars, mine, other, index)
+        columns = slice(index * weight.shape[1], (index + 1) * weight.shape[1])
+        for ref, at, rows in row_blocks(x_refs):
+            term = jnp.dot(ref[0], weight, preferred_element_type=jnp.float32)
+            if has_sum:
+                term = sum_ref[at : at + rows, columns] + term
+            out_ref[at : at + rows, columns] = term
+
+
+def part_spec(array, step):
+    block = (1,) + array.shape[1:]
+    return pl.BlockSpec(block, lambda i, scalars: (scalars[3 + step], 0, 0))
+
+
+def project(scalars, step, xs, mine, other, summed):
+    rows = sum(x.shape[1] for x in xs)
+    columns = 3 * mine[0].shape[2]
+    operands = [*xs, *mine, *other]
+    in_specs = [part_spec(x, step) for x in xs]
+    in_specs += [whole(w.shape) for w in (*mine, *other)]
+    if summed is not None:
+        operands.append(summed)
+        in_specs.append(whole(summed.shape))
+    return pl.pallas_call(
+        lambda *refs: project_kernel(len(mine), summed is not None, *refs),
+        grid_spec=pltpu.PrefetchScalarGridSpec(
+            num_scalar_prefetch=1,
+            grid=(1,),
+            in_specs=in_specs,
+            out_specs=whole((rows, columns)),
+        ),
+        out_shape=jax.ShapeDtypeStruct((rows, columns), jnp.float32),
+        compiler_params=params(),
+        cost_estimate=pl.CostEstimate(
+            flops=2 * rows * columns * xs[0].shape[2], bytes_accessed=8 * rows * columns, transcendentals=0
+        ),
+        name="project",
+    )(scalars, *operands)
+
+
+def attend_kernel(
+    dims, scalars, own_x, first_x, second_x, dec_x, m0, m1, o0, o1, sum_ref, prior_ref, gain_ref, lengths, near_ref, far_ref, qkv
+):
+    groups, block, heads, head, steps = dims
+    for index in range(3):
+        weight = weights_of(scalars, (m0, m1), (o0, o1), index)
+        columns = slice(index * weight.shape[1], (index + 1) * weight.shape[1])
+        for ref, at, rows in row_blocks((own_x, first_x, second_x, dec_x)):
+            term = jnp.dot(ref[0], weight, preferred_element_type=jnp.float32)
+            qkv[at : at + rows, columns] = (sum_ref[at : at + rows, columns] + term).astype(jnp.bfloat16)
+    here = scalars[0]
+    parity = scalars[2]
+    wide = heads * head
+    prompt = 2 * groups * block
+    causal = lax.broadcasted_iota(jnp.int32, (block, block), 0) >= lax.broadcasted_iota(jnp.int32, (block, block), 1)
+    position = lax.broadcasted_iota(jnp.int32, (block, head), 0)
+    row = lax.broadcasted_iota(jnp.int32, (DEC_PAD, DEC_PAD), 0)
+    column = lax.broadcasted_iota(jnp.int32, (DEC_PAD, DEC_PAD), 1)
+    reach = (row % groups == column % groups) & (column <= row)
+    exact = lax.Precision.HIGHEST
+    inner = (((0,), (0,)), ((), ()))
+    across = (((1,), (1,)), ((), ()))
+
+    def finish(value, gain):
+        mean = jnp.mean(value * value, axis=-1, keepdims=True)
+        return (value * lax.rsqrt(mean + 1e-06) * gain).astype(jnp.bfloat16)
+
+    for h in range(heads):
+        cols = [slice(i * wide + h * head, i * wide + (h + 1) * head) for i in range(3)]
+        gain = gain_ref[h : h + 1, :]
+        dq = qkv[prompt : prompt + DEC_PAD, cols[0]]
+        dk = qkv[prompt : prompt + DEC_PAD, cols[1]]
+        dv = qkv[prompt : prompt + DEC_PAD, cols[2]].astype(jnp.float32)
+        dq32 = dq.astype(jnp.float32)
+        pairs = lax.dot_general(dq, dk, across, preferred_element_type=jnp.float32)
+        read = jnp.dot(jnp.where(reach, pairs, 0.0), dv, precision=exact, preferred_element_type=jnp.float32)
+        dec_group = lax.broadcasted_iota(jnp.int32, (DEC_PAD, head), 0) % groups
+        for r in range(groups):
+            prior = prior_ref[r, h]
+            starts = (r * block, groups * block + pl.multiple_of((r ^ parity) * block, block))
+            run = (here, 1 - here)
+            keys, values, states = [], [], []
+            for start, b in zip(starts, run):
+                k = qkv[pl.ds(start, block), cols[1]]
+                live = b * block + position < lengths[r]
+                k = jnp.where(live, k, jnp.zeros_like(k))
+                v = qkv[pl.ds(start, block), cols[2]]
+                keys.append(k)
+                values.append(v)
+                states.append(lax.dot_general(k, v, inner, preferred_element_type=jnp.float32))
+            before = (jnp.where(here == 1, states[1], 0.0), jnp.where(here == 0, states[0], 0.0))
+            for side, out_ref in enumerate((near_ref, far_ref)):
+                q = qkv[pl.ds(starts[side], block), cols[0]]
+                carried = (prior + before[side]).astype(jnp.bfloat16)
+                scores = lax.dot_general(q, keys[side], across, preferred_element_type=jnp.float32)
+                weights = jnp.where(causal, scores, 0.0).astype(jnp.bfloat16)
+                attended = jnp.dot(q, carried, preferred_element_type=jnp.float32) + jnp.dot(
+                    weights, values[side], preferred_element_type=jnp.float32
+                )
+                out_ref[r * block : (r + 1) * block, h * head : (h + 1) * head] = finish(attended, gain)
+            state = prior + (states[0] + states[1])
+            inter = jnp.dot(dq32, state, precision=exact, preferred_element_type=jnp.float32)
+            read = read + jnp.where(dec_group == r, inter, 0.0)
+        done = finish(read, gain)
+        near_ref[groups * block :, h * head : (h + 1) * head] = done
+        far_ref[groups * block :, h * head : (h + 1) * head] = done
+
+
+def attend(scalars, xs, mine, other, summed, prior, gain, lengths, dims):
+    groups, block, heads, head, _ = dims
+    rows, columns = summed.shape
+    shape = (groups * block + DEC_PAD, heads * head)
+    in_specs = [part_spec(x, 3) for x in xs]
+    in_specs += [whole(w.shape) for w in (*mine, *other, summed)]
+    in_specs += [
+        pl.BlockSpec((groups, heads, head, head), lambda i, s: (0, s[0], 0, 0)),
+        whole(gain.shape),
+        pl.BlockSpec(memory_space=pltpu.SMEM),
+    ]
+    out = jax.ShapeDtypeStruct(shape, jnp.bfloat16)
+    return pl.pallas_call(
+        lambda *refs: attend_kernel(dims, *refs),
+        grid_spec=pltpu.PrefetchScalarGridSpec(
+            num_scalar_prefetch=1,
+            grid=(1,),
+            in_specs=in_specs,
+            out_specs=[whole(shape), whole(shape)],
+            scratch_shapes=[pltpu.VMEM((rows, columns), jnp.bfloat16)],
+        ),
+        out_shape=[out, out],
+        compiler_params=params(),
+        cost_estimate=pl.CostEstimate(
+            flops=2 * rows * columns * xs[0].shape[2] * 2, bytes_accessed=4 * rows * columns, transcendentals=0
+        ),
+        name="attend",
+    )(scalars, *xs, *mine, *other, summed, prior, gain, lengths)
+
+
+def combine_kernel(dims, scalars, *refs):
+    prompt, dec = dims
+    hidden, weights = refs[:8], refs[8:16]
+    res_ref, dec_res_ref, out_ref, dec_ref = refs[16:]
+    here_first = scalars[0] == 0
+    same = scalars[1] == 1
+    total = None
+    for i in range(4):
+        core, moved = i % 2, i // 2
+        def piece(j):
+            return jnp.where(same, hidden[core * 4 + j + 2 * moved][...], hidden[core * 4 + j + 2 * (1 - moved)][...])
+
+        near, far = piece(0), piece(1)
+        rows = jnp.concatenate([jnp.where(here_first, near, far), jnp.where(here_first, far, near)], axis=1)
+        weight = jnp.concatenate([weights[2 * i][...], weights[2 * i + 1][...]], axis=1)
+        term = jnp.dot(rows, weight, preferred_element_type=jnp.float32)
+        total = term if total is None else total + term
+    out_ref[...] = (res_ref[...].astype(jnp.float32) + total[:prompt]).astype(jnp.bfloat16)
+    dec_ref[...] = (dec_res_ref[...].astype(jnp.float32) + total[prompt : prompt + dec]).astype(jnp.bfloat16)
+
+
+def combine(scalars, hidden, weights, res, dec_res):
+    operands = [*hidden, *weights, res, dec_res]
+    return pl.pallas_call(
+        lambda *refs: combine_kernel((res.shape[0], dec_res.shape[0]), *refs),
+        grid_spec=pltpu.PrefetchScalarGridSpec(
+            num_scalar_prefetch=1,
+            grid=(1,),
+            in_specs=[whole(a.shape) for a in operands],
+            out_specs=[whole(res.shape), whole(dec_res.shape)],
+        ),
+        out_shape=[
+            jax.ShapeDtypeStruct(res.shape, jnp.bfloat16),
+            jax.ShapeDtypeStruct(dec_res.shape, jnp.bfloat16),
+        ],
+        compiler_params=params(),
+        name="combine",
+    )(scalars, *operands)
+
+
+def spread(value, is_end):
+    pair = move(value, to_pair)
+    third_mid = move(value, mid_swap)
+    fourth_mid = move(pair, mid_swap)
+    third_end = move(third_mid, mid_to_end)
+    fourth_end = move(fourth_mid, mid_to_end)
+    return (value,), (pair,), (third_mid, third_end), (fourth_mid, fourth_end)
+
+
+def local_grid(
+    spikes, dec_spikes, thresholds, in_scale, qkv_weight, out_weight, head_gain, prior_state, lengths
+):
+    groups, block, width = spikes.shape
+    steps = dec_spikes.shape[0]
+    all_heads, head = head_gain.shape
+    heads = all_heads // 2
+    wide = heads * head
+    planes = lax.axis_size("rep")
+    c, t, z = (lax.axis_index(name) for name in AXES)
+    parity = t % 2
+    y = t // 2
+    is_end = (z == 0) | (z == planes - 1)
+    end = is_end.astype(jnp.int32)
+    third = jnp.where(is_end, z ^ 2, z ^ 3)
+    fourth = jnp.where(is_end, z ^ 3, z ^ 2)
+    scalars = jnp.stack([c, end, parity, z, z ^ 1, third, fourth]).astype(jnp.int32)
+
+    kept = lax.dynamic_slice_in_dim(qkv_weight, c * wide, wide, 2)
+    given = lax.dynamic_slice_in_dim(qkv_weight, (1 - c) * wide, wide, 2)
+    other = move(given, to_ctx)
+    mine_parts = spread(kept, is_end)
+    other_parts = spread(other, is_end)
+
+    counts = spikes.reshape(groups * block, width)
+    dec_counts = dec_spikes.reshape(steps * groups, width)
+    dec_padded = jnp.pad(dec_counts, ((0, DEC_PAD - steps * groups), (0, 0)))
+    own_x = embed(counts, thresholds, in_scale, planes, block // 2)
+    dec_x = embed(dec_padded, thresholds, in_scale, planes, DEC_PAD)
+    first_x = move(lax.dynamic_slice_in_dim(own_x, parity * block, block, 1), to_ctx)
+    second_x = move(first_x, to_core)
+    xs = (own_x, first_x, second_x, dec_x)
+
+    def meet(c, t, r):
+        return (c, t, r) if c == t // 2 else (1 - c, t ^ 2, r)
+
+    out_block = move(out_weight, meet)
+    (o_own,), (o_pair,), o_third, o_fourth = spread(out_block, is_end)
+    o_third = jnp.where(is_end, o_third[1], o_third[0])
+    o_fourth = jnp.where(is_end, o_fourth[1], o_fourth[0])
+    z_even = z % 2 == 0
+    low = z < 2
+    near_half = (jnp.where(z_even, o_own, o_pair), jnp.where(z_even, o_pair, o_own))
+    far_half = (jnp.where(low, o_third, o_fourth), jnp.where(low, o_fourth, o_third))
+    near_mine = z // 2 == parity
+    used = [jnp.where(near_mine, a, b) for a, b in zip(near_half, far_half)]
+    passed = [jnp.where(near_mine, b, a) for a, b in zip(near_half, far_half)]
+    sibling = [move(p, to_core) for p in passed]
+    out_weights = used + sibling + [move(u, to_ctx) for u in used] + [move(s, to_ctx) for s in sibling]
+
+    summed = None
+    for step in range(3):
+        summed = project(scalars, step, xs, mine_parts[step], other_parts[step], summed)
+    gain = lax.dynamic_slice_in_dim(head_gain, c * heads, heads, 0)
+    near, far = attend(
+        scalars, xs, mine_parts[3], other_parts[3], summed, prior_state, gain, lengths, (groups, block, heads, head, steps)
+    )
+    mine = [near, move(far, to_ctx), move(near, to_y), move(far, to_diagonal)]
+    hidden = mine + [move(m, to_core) for m in mine]
+
+    columns = width // lax.axis_size("tp")
+
+    def gate(rows):
+        part = lax.dynamic_slice_in_dim(rows, t * columns, columns, 1)
+        level = lax.dynamic_slice_in_dim(thresholds, t * columns, columns, 0)
+        scale = lax.dynamic_slice_in_dim(in_scale, t * columns, columns, 0)
+        return (jnp.where(part >= level, part, 0).astype(jnp.float32) * scale).astype(jnp.bfloat16)
+
+    flags = jnp.stack([c, (c == y).astype(jnp.int32)]).astype(jnp.int32)
+    out, dec_out = combine(flags, hidden, out_weights, gate(counts), gate(dec_counts))
+    return out.reshape(groups, block, columns), dec_out.reshape(steps, groups, columns)
+
+
 def solution(mesh):
     return jax.shard_map(
-        local,
+        local_grid if fits(mesh) else local_any,
         mesh=mesh,
         in_specs=(
             P("rep", "ctx", None),

time: 389 us -> 252 us (0.65)
  waiting for transfers between devices: 328 us -> 106 us
  starting transfers between devices: 0.15 us -> 76.3 us
  Pallas kernels: 0 us -> 44.8 us
  matrix products: 24.8 us -> 0 us
  between operations: 14 us -> 0.9 us
  local copies, waits for them, and re-layouts: 7.55 us -> 15.5 us
  other arithmetic: 13.9 us -> 8.38 us
    all_gather x3 -> x0, waiting for transfers between devices: 239 us -> none  [the longest x1 154 us: local(): full = lax.all_gather(qkv_weight, ('ctx', 'rep'), axis=1, tiled=True)]
    ppermute x0 -> x32, waiting for transfers between devices: none -> 106 us  [move(): return lax.ppermute(value, AXES, pairs)]
    ppermute x0 -> x32, starting transfers between devices: none -> 76.3 us  [move(): return lax.ppermute(value, AXES, pairs)]
    reduce_scatter x1 -> x0, waiting for transfers between devices: 64.9 us -> none  [local(): summed = lax.psum_scatter(terms, 'tp', scatter_dimension=1, tiled=True)]
    pallas_call x0 -> x7, Pallas kernels: none -> 44.8 us  [the longest x3 21.3 us: project(): pl.pallas_call(lambda *refs: project_kernel(len(mine), summed is not None...]
    dot_general x9 -> x0, matrix products: 24.8 us -> none  [the longest x1 10.7 us: local(): jnp.einsum('rd,cde->rce', rows_all, full, preferred_element_type=jnp.floa...]
    psum x1 -> x0, waiting for transfers between devices: 22.1 us -> none  [local(): memory_state = prior_state + lax.psum(block_state, 'ctx')]
    dynamic_slice x0 -> x5, local copies, waits for them, and re-layouts: none -> 7.34 us  [the longest x1 2.89 us: local_grid(): lax.dynamic_slice_in_dim(own_x, parity * block, block, 1)]
  transfers between devices with their start and end apart: 5 -> 32, of which waited for: 5 -> 11; matrix products, arithmetic and copies ran while one was open for 5% -> 6% of each run, Pallas kernels for 0% -> 13%
where the time goes in v1:
time: 252 us; the launch traced here: 251 us
  waiting for transfers between devices  106 us (42%)
  starting transfers between devices  76.3 us (30%)
  Pallas kernels  44.8 us (18%)
  local copies, waits for them, and re-layouts  15.5 us (6%)
  other arithmetic  8.38 us (3%)
    ppermute x32, waiting for transfers between devices, move(): return lax.ppermute(value, AXES, pairs)  106 us
    ppermute x32, starting transfers between devices, move(): return lax.ppermute(value, AXES, pairs)  76.3 us
    pallas_call x3, Pallas kernels, project(): pl.pallas_call(lambda *refs: project_kernel(len(mine), summed is not None...  21.3 us
    pallas_call x1, Pallas kernels, attend(): pl.pallas_call(lambda *refs: attend_kernel(dims, *refs), grid_spec=pltpu....  8.64 us
    pallas_call x2, Pallas kernels, embed(): pl.pallas_call(lambda *refs: embed_kernel(parts, *refs), grid=(rows // ti...  7.68 us
    pallas_call x1, Pallas kernels, combine(): pl.pallas_call(lambda *refs: combine_kernel((res.shape[0], dec_res.shape[...  7.13 us
  transfers between devices with their start and end apart: 32, of which 11 were waited for; matrix products, arithmetic and copies ran while one was open for 6% of the time, Pallas kernels for 13%

profile of v1, /device:TPU:0, one launch (start us, length us, event | category | flops | bytes accessed | tf_op | source)
XLA Modules:
  0.0 251.4 jit_solution(3667144967347952356)
XLA Ops:
  3.3 6.0 %embed.2.refs_1_ = bf16[4,512,896]{2,1,0:T(8,128)(2,1)} custom-call(s32[512,3584]{1,0:T(8,128)} %bitcast.10, s32[1,3584]{1,0:T(1,128)} %broadcast_in_dim.20.refs_1_, f32[1,3584]{1,0:T(1,128)} %broadcast_in_dim.21.refs_2_), custom_call_target="tpu_custom_call" | custom-call | tf_op jit(solution)/shard_map/embed/pallas_call | solution.py:185
  9.3 2.9 %constant_dynamic-slice_fusion.3 = bf16[4,256,896]{2,1,0:T(8,128)(2,1)} fusion(bf16[4,512,896]{2,1,0:T(8,128)(2,1)} %embed.2.refs_1_, s32[]{:T(128)S(6)} %select_n.106), kind=kLoop, calls=%fused_computation.21 | loop fusion | bytes 3670020 | tf_op jit(solution)/shard_map/dynamic_slice | solution.py:442
  12.2 2.9 %collective-permute-start = (bf16[4,256,896]{2,1,0:T(8,128)(2,1)}, bf16[4,256,896]{2,1,0:T(8,128)(2,1)S(1)}, u32[]{:S(2)}, u32[]{:S(2)}) collective-permute-start(bf16[4,256,896]{2,1,0:T(8,128)(2,1)} %constant_dynamic-slice_fusion.3), channel_id=1, source_target_pairs={{0,16},{1,17},{2,18},{3,19},{4,20},{5,21},{6,22},{7,23},{8,24},{9,... | collective-permute-start | bytes 5505032 | tf_op jit(solution)/shard_map/ppermute | solution.py:133
  15.1 2.2 constant_dynamic-slice_fusion.1
  17.4 1.6 collective-permute-start.2
  20.5 1.7 collective-permute-start.20
  22.9 4.4 %collective-permute-start.21 = (bf16[512,448]{1,0:T(8,128)(2,1)S(1)}, bf16[512,448]{1,0:T(8,128)(2,1)}, u32[]{:S(2)}, u32[]{:S(2)}) collective-permute-start(bf16[512,448]{1,0:T(8,128)(2,1)S(1)} %collective-permute-done.20), channel_id=1, source_target_pairs={{0,1},{1,0},{2,3},{3,2},{4,5},{5,4},{6,7},{7,6},{8,9},{9,8},{10,11... | collective-permute-start | bytes 1376264 | tf_op jit(solution)/shard_map/ppermute | solution.py:133
  27.3 28.8 %collective-permute-done.refs_2_ = bf16[4,256,896]{2,1,0:T(8,128)(2,1)S(1)} collective-permute-done((bf16[4,256,896]{2,1,0:T(8,128)(2,1)}, bf16[4,256,896]{2,1,0:T(8,128)(2,1)S(1)}, u32[]{:S(2)}, u32[]{:S(2)}) %collective-permute-start) | collective-permute-done | bytes 1835040 | tf_op jit(solution)/shard_map/ppermute | solution.py:133
  57.6 13.4 %collective-permute-done.5.refs_6_ = bf16[3,448,256]{2,1,0:T(8,128)(2,1)} collective-permute-done((bf16[3,448,256]{2,1,0:T(8,128)(2,1)}, bf16[3,448,256]{2,1,0:T(8,128)(2,1)}, u32[]{:S(2)}, u32[]{:S(2)}) %collective-permute-start.5) | collective-permute-done | bytes 688160 | tf_op jit(solution)/shard_map/ppermute | solution.py:133
  72.5 4.2 %collective-permute-start.6 = (bf16[3,448,256]{2,1,0:T(8,128)(2,1)}, bf16[3,448,256]{2,1,0:T(8,128)(2,1)}, u32[]{:S(2)}, u32[]{:S(2)}) collective-permute-start(bf16[3,448,256]{2,1,0:T(8,128)(2,1)} %collective-permute-done.5.refs_6_), channel_id=1, source_target_pairs={{0,1},{1,0},{2,3},{3,2},{4,5},{5,4},{6,7},{7,6},{8,9},{9,8},{10,11... | collective-permute-start | bytes 2064392 | tf_op jit(solution)/shard_map/ppermute | solution.py:133
  78.2 1.5 collective-permute-start.11
  82.3 8.1 %collective-permute-done.6.refs_6_ = bf16[3,448,256]{2,1,0:T(8,128)(2,1)} collective-permute-done((bf16[3,448,256]{2,1,0:T(8,128)(2,1)}, bf16[3,448,256]{2,1,0:T(8,128)(2,1)}, u32[]{:S(2)}, u32[]{:S(2)}) %collective-permute-start.6) | collective-permute-done | bytes 688160 | tf_op jit(solution)/shard_map/ppermute | solution.py:133
  93.3 10.5 %collective-permute-done.23 = bf16[512,448]{1,0:T(8,128)(2,1)} collective-permute-done((bf16[512,448]{1,0:T(8,128)(2,1)}, bf16[512,448]{1,0:T(8,128)(2,1)}, u32[]{:S(2)}, u32[]{:S(2)}) %collective-permute-start.23) | collective-permute-done | bytes 458784 | tf_op jit(solution)/shard_map/ppermute | solution.py:133
  105.1 8.6 %collective-permute-done.25 = bf16[512,448]{1,0:T(8,128)(2,1)} collective-permute-done((bf16[512,448]{1,0:T(8,128)(2,1)}, bf16[512,448]{1,0:T(8,128)(2,1)}, u32[]{:S(2)}, u32[]{:S(2)}) %collective-permute-start.25) | collective-permute-done | bytes 458784 | tf_op jit(solution)/shard_map/ppermute | solution.py:133
  115.0 2.4 broadcast_select_fusion.6
  118.9 2.0 broadcast_select_fusion.7
  122.5 1.7 embed.3.refs_4_
  124.8 6.3 %project.3.refs_7_ = f32[1040,768]{1,0:T(8,128)} custom-call(s32[7]{0:T(128)} %stack.48.refs_0_, bf16[4,512,896]{2,1,0:T(8,128)(2,1)} %embed.2.refs_1_, bf16[4,256,896]{2,1,0:T(8,128)(2,1)} %copy-done.1, bf16[4,256,896]{2,1,0:T(8,128)(2,1)} %collective-permute-done.1.refs_3_, bf16[4,16,896]{2,1,0:T(8,128)(2,1)} %embed.3.refs_4_, ...), custom_call_target="tpu_custom_call" | custom-call | flops 1431306240 | bytes 6389760 | tf_op jit(solution)/shard_map/project/pallas_call | solution.py:249
  131.1 6.5 %collective-permute-done.10.refs_6_ = bf16[3,448,256]{2,1,0:T(8,128)(2,1)} collective-permute-done((bf16[3,448,256]{2,1,0:T(8,128)(2,1)}, bf16[3,448,256]{2,1,0:T(8,128)(2,1)}, u32[]{:S(2)}, u32[]{:S(2)}) %collective-permute-start.10) | collective-permute-done | bytes 688160 | tf_op jit(solution)/shard_map/ppermute | solution.py:133
  137.6 14.7 %collective-permute-done.4.refs_6_ = bf16[3,448,256]{2,1,0:T(8,128)(2,1)} collective-permute-done((bf16[3,448,256]{2,1,0:T(8,128)(2,1)}, bf16[3,448,256]{2,1,0:T(8,128)(2,1)}, u32[]{:S(2)}, u32[]{:S(2)}) %collective-permute-start.4) | collective-permute-done | bytes 688160 | tf_op jit(solution)/shard_map/ppermute | solution.py:133
  152.4 24.5 %collective-permute-start.28 = (bf16[512,448]{1,0:T(8,128)(2,1)S(1)}, bf16[512,448]{1,0:T(8,128)(2,1)S(1)}, u32[]{:S(2)}, u32[]{:S(2)}) collective-permute-start(bf16[512,448]{1,0:T(8,128)(2,1)S(1)} %get-tuple-element.15.refs_9_), channel_id=1, source_target_pairs={{0,16},{1,17},{2,18},{3,19},{4,20},{5,21},{6,22},{7,23},{8,24},{9,... | collective-permute-start | bytes 1376264 | tf_op jit(solution)/shard_map/ppermute | solution.py:133
  176.9 14.7 %collective-permute-start.29 = (bf16[512,448]{1,0:T(8,128)(2,1)S(1)}, bf16[512,448]{1,0:T(8,128)(2,1)S(1)}, u32[]{:S(2)}, u32[]{:S(2)}) collective-permute-start(bf16[512,448]{1,0:T(8,128)(2,1)S(1)} %get-tuple-element.14.refs_10_), channel_id=1, source_target_pairs={{0,16},{1,17},{2,18},{3,19},{4,20},{5,21},{6,22},{7,23},{8,24},{9,... | collective-permute-start | bytes 1376264 | tf_op jit(solution)/shard_map/ppermute | solution.py:133
  191.6 7.3 %project.4.refs_9_ = f32[1040,768]{1,0:T(8,128)} custom-call(s32[7]{0:T(128)} %stack.48.refs_0_, bf16[4,512,896]{2,1,0:T(8,128)(2,1)} %embed.2.refs_1_, bf16[4,256,896]{2,1,0:T(8,128)(2,1)} %copy-done.1, bf16[4,256,896]{2,1,0:T(8,128)(2,1)} %collective-permute-done.1.refs_3_, bf16[4,16,896]{2,1,0:T(8,128)(2,1)} %embed.3.refs_4_, ...), custom_call_target="tpu_custom_call" | custom-call | flops 1431306240 | bytes 6389760 | tf_op jit(solution)/shard_map/project/pallas_call | solution.py:249
  198.9 7.7 %project.5.refs_9_ = f32[1040,768]{1,0:T(8,128)} custom-call(s32[7]{0:T(128)} %stack.48.refs_0_, bf16[4,512,896]{2,1,0:T(8,128)(2,1)} %embed.2.refs_1_, bf16[4,256,896]{2,1,0:T(8,128)(2,1)} %copy-done.1, bf16[4,256,896]{2,1,0:T(8,128)(2,1)} %collective-permute-done.1.refs_3_, bf16[4,16,896]{2,1,0:T(8,128)(2,1)} %embed.3.refs_4_, ...), custom_call_target="tpu_custom_call" | custom-call | flops 1431306240 | bytes 6389760 | tf_op jit(solution)/shard_map/project/pallas_call | solution.py:249
  206.7 8.6 %attend.1 = (bf16[528,256]{1,0:T(8,128)(2,1)}, bf16[528,256]{1,0:T(8,128)(2,1)}) custom-call(s32[7]{0:T(128)} %stack.48.refs_0_, bf16[4,512,896]{2,1,0:T(8,128)(2,1)} %embed.2.refs_1_, bf16[4,256,896]{2,1,0:T(8,128)(2,1)} %copy-done.1, bf16[4,256,896]{2,1,0:T(8,128)(2,1)} %collective-permute-done.1.refs_3_, bf16[4,16,896]{2,1,0:T(8,128)(2,1)} %embed.3.refs_4_, ...), custom_call_target="tpu_custom_call" | custom-call | flops 2862612480 | bytes 3194880 | tf_op jit(solution)/shard_map/attend/pallas_call | solution.py:346
  215.3 2.0 collective-permute-start.13
  220.5 1.9 collective-permute-start.31
  223.0 3.5 %collective-permute-done.13.refs_2_ = bf16[528,256]{1,0:T(8,128)(2,1)} collective-permute-done((bf16[528,256]{1,0:T(8,128)(2,1)}, bf16[528,256]{1,0:T(8,128)(2,1)}, u32[]{:S(2)}, u32[]{:S(2)}) %collective-permute-start.13) | collective-permute-done | bytes 270368 | tf_op jit(solution)/shard_map/ppermute | solution.py:133
  227.8 3.5 %collective-permute-done.15.refs_4_ = bf16[528,256]{1,0:T(8,128)(2,1)S(1)} collective-permute-done((bf16[528,256]{1,0:T(8,128)(2,1)}, bf16[528,256]{1,0:T(8,128)(2,1)S(1)}, u32[]{:S(2)}, u32[]{:S(2)}) %collective-permute-start.15) | collective-permute-done | bytes 270368 | tf_op jit(solution)/shard_map/ppermute | solution.py:133
  231.8 2.7 %fusion.2.refs_17_ = bf16[512,896]{1,0:T(8,128)(2,1)} fusion(s32[512,3584]{1,0:T(8,128)} %bitcast.11, s32[]{:T(128)S(6)} %select_n.126, f32[896]{0:T(1024)S(1)} %dynamic_slice.32, s32[896]{0:T(1024)S(1)} %dynamic_slice.31), kind=kLoop, calls=%fused_computation.3 | loop fusion | flops 2293760 | bytes 2759684 | tf_op jit(solution)/shard_map/convert_element_type | solution.py:479
  234.6 6.6 %collective-permute-done.31.refs_16_ = bf16[512,448]{1,0:T(8,128)(2,1)S(1)} collective-permute-done((bf16[512,448]{1,0:T(8,128)(2,1)S(1)}, bf16[512,448]{1,0:T(8,128)(2,1)S(1)}, u32[]{:S(2)}, u32[]{:S(2)}) %collective-permute-start.31) | collective-permute-done | bytes 458784 | tf_op jit(solution)/shard_map/ppermute | solution.py:133
  243.0 7.1 %combine.1 = (bf16[512,896]{1,0:T(8,128)(2,1)}, bf16[8,896]{1,0:T(8,128)(2,1)}) custom-call(s32[2]{0:T(128)} %pad_add_fusion.refs_0_, bf16[528,256]{1,0:T(8,128)(2,1)} %get-tuple-element.6.refs_1_, bf16[528,256]{1,0:T(8,128)(2,1)} %collective-permute-done.13.refs_2_, bf16[528,256]{1,0:T(8,128)(2,1)} %collective-permute-done.14.refs_3_, ...), custom_call_target="tpu_custom_call" | custom-call | tf_op jit(solution)/shard_map/combine/pallas_call | solution.py:387
  (94 shorter events, 29.6 us)
Async XLA Ops:
  12.2 44.0 %collective-permute-start = (bf16[4,256,896]{2,1,0:T(8,128)(2,1)}, bf16[4,256,896]{2,1,0:T(8,128)(2,1)S(1)}, u32[]{:S(2)}, u32[]{:S(2)}) collective-permute-start(bf16[4,256,896]{2,1,0:T(8,128)(2,1)} %constant_dynamic-slice_fusion.3), channel_id=1, source_target_pairs={{0,16},{1,17},{2,18},{3,19},{4,20},{5,21},{6,22},{7,23},{8,24},{9,... | collective-permute-start | bytes 5505032 | tf_op jit(solution)/shard_map/ppermute | solution.py:133
  17.4 38.8 %collective-permute-start.2 = (bf16[3,448,256]{2,1,0:T(8,128)(2,1)S(1)}, bf16[3,448,256]{2,1,0:T(8,128)(2,1)}, u32[]{:S(2)}, u32[]{:S(2)}) collective-permute-start(bf16[3,448,256]{2,1,0:T(8,128)(2,1)S(1)} %get-tuple-element.17.refs_5_), channel_id=1, source_target_pairs={{0,1},{1,0},{2,3},{3,2},{4,5},{5,4},{6,7},{7,6},{8,9},{9,8},{10,11... | collective-permute-start | bytes 2064392 | tf_op jit(solution)/shard_map/ppermute | solution.py:133
  18.9 52.1 %collective-permute-start.5 = (bf16[3,448,256]{2,1,0:T(8,128)(2,1)}, bf16[3,448,256]{2,1,0:T(8,128)(2,1)}, u32[]{:S(2)}, u32[]{:S(2)}) collective-permute-start(bf16[3,448,256]{2,1,0:T(8,128)(2,1)} %get-tuple-element.16), channel_id=1, source_target_pairs={{0,16},{1,17},{2,18},{3,19},{4,20},{5,21},{6,22},{7,23},{8,24},{9,... | collective-permute-start | bytes 2064392 | tf_op jit(solution)/shard_map/ppermute | solution.py:133
  20.5 2.4 collective-permute-start.20
  22.2 50.4 %collective-permute-start.9 = (bf16[3,448,256]{2,1,0:T(8,128)(2,1)S(1)}, bf16[3,448,256]{2,1,0:T(8,128)(2,1)S(1)}, u32[]{:S(2)}, u32[]{:S(2)}) collective-permute-start(bf16[3,448,256]{2,1,0:T(8,128)(2,1)S(1)} %get-tuple-element.17.refs_5_), channel_id=1, source_target_pairs={{1,2},{2,1},{5,6},{6,5},{9,10},{10,9},{13,14},{14,13},{17,18},{18,... | collective-permute-start | bytes 2064392 | tf_op jit(solution)/shard_map/ppermute | solution.py:133
  22.9 53.8 %collective-permute-start.21 = (bf16[512,448]{1,0:T(8,128)(2,1)S(1)}, bf16[512,448]{1,0:T(8,128)(2,1)}, u32[]{:S(2)}, u32[]{:S(2)}) collective-permute-start(bf16[512,448]{1,0:T(8,128)(2,1)S(1)} %collective-permute-done.20), channel_id=1, source_target_pairs={{0,1},{1,0},{2,3},{3,2},{4,5},{5,4},{6,7},{7,6},{8,9},{9,8},{10,11... | collective-permute-start | bytes 1376264 | tf_op jit(solution)/shard_map/ppermute | solution.py:133
  56.2 64.8 %collective-permute-start.1 = (bf16[4,256,896]{2,1,0:T(8,128)(2,1)S(1)}, bf16[4,256,896]{2,1,0:T(8,128)(2,1)}, u32[]{:S(2)}, u32[]{:S(2)}) collective-permute-start(bf16[4,256,896]{2,1,0:T(8,128)(2,1)S(1)} %collective-permute-done.refs_2_), channel_id=1, source_target_pairs={{0,4},{1,5},{2,6},{3,7},{4,0},{5,1},{6,2},{7,3},{8,12},{9,13},{10,... | collective-permute-start | bytes 5505032 | tf_op jit(solution)/shard_map/ppermute | solution.py:133
  56.2 22.0 %collective-permute-start.22 = (bf16[512,448]{1,0:T(8,128)(2,1)S(1)}, bf16[512,448]{1,0:T(8,128)(2,1)}, u32[]{:S(2)}, u32[]{:S(2)}) collective-permute-start(bf16[512,448]{1,0:T(8,128)(2,1)S(1)} %collective-permute-done.20), channel_id=1, source_target_pairs={{1,2},{2,1},{5,6},{6,5},{9,10},{10,9},{13,14},{14,13},{17,18},{18,... | collective-permute-start | bytes 1376264 | tf_op jit(solution)/shard_map/ppermute | solution.py:133
  71.0 8.7 %collective-permute-start.3 = (bf16[3,448,256]{2,1,0:T(8,128)(2,1)}, bf16[3,448,256]{2,1,0:T(8,128)(2,1)}, u32[]{:S(2)}, u32[]{:S(2)}) collective-permute-start(bf16[3,448,256]{2,1,0:T(8,128)(2,1)} %collective-permute-done.2.refs_5_), channel_id=1, source_target_pairs={{1,2},{2,1},{5,6},{6,5},{9,10},{10,9},{13,14},{14,13},{17,18},{18,... | collective-permute-start | bytes 2064392 | tf_op jit(solution)/shard_map/ppermute | solution.py:133
  72.5 17.9 %collective-permute-start.6 = (bf16[3,448,256]{2,1,0:T(8,128)(2,1)}, bf16[3,448,256]{2,1,0:T(8,128)(2,1)}, u32[]{:S(2)}, u32[]{:S(2)}) collective-permute-start(bf16[3,448,256]{2,1,0:T(8,128)(2,1)} %collective-permute-done.5.refs_6_), channel_id=1, source_target_pairs={{0,1},{1,0},{2,3},{3,2},{4,5},{5,4},{6,7},{7,6},{8,9},{9,8},{10,11... | collective-permute-start | bytes 2064392 | tf_op jit(solution)/shard_map/ppermute | solution.py:133
  76.7 4.3 %collective-permute-start.24 = (bf16[512,448]{1,0:T(8,128)(2,1)}, bf16[512,448]{1,0:T(8,128)(2,1)}, u32[]{:S(2)}, u32[]{:S(2)}) collective-permute-start(bf16[512,448]{1,0:T(8,128)(2,1)} %collective-permute-done.21), channel_id=1, source_target_pairs={{1,2},{2,1},{5,6},{6,5},{9,10},{10,9},{13,14},{14,13},{17,18},{18,... | collective-permute-start | bytes 1376264 | tf_op jit(solution)/shard_map/ppermute | solution.py:133
  78.2 13.8 %collective-permute-start.11 = (bf16[3,448,256]{2,1,0:T(8,128)(2,1)}, bf16[3,448,256]{2,1,0:T(8,128)(2,1)}, u32[]{:S(2)}, u32[]{:S(2)}) collective-permute-start(bf16[3,448,256]{2,1,0:T(8,128)(2,1)} %collective-permute-done.5.refs_6_), channel_id=1, source_target_pairs={{1,2},{2,1},{5,6},{6,5},{9,10},{10,9},{13,14},{14,13},{17,18},{18,... | collective-permute-start | bytes 2064392 | tf_op jit(solution)/shard_map/ppermute | solution.py:133
  79.7 24.0 %collective-permute-start.23 = (bf16[512,448]{1,0:T(8,128)(2,1)}, bf16[512,448]{1,0:T(8,128)(2,1)}, u32[]{:S(2)}, u32[]{:S(2)}) collective-permute-start(bf16[512,448]{1,0:T(8,128)(2,1)} %collective-permute-done.22), channel_id=1, source_target_pairs={{1,0},{2,3},{5,4},{6,7},{9,8},{10,11},{13,12},{14,15},{17,16},{18,... | collective-permute-start | bytes 1376264 | tf_op jit(solution)/shard_map/ppermute | solution.py:133
  81.0 32.7 %collective-permute-start.25 = (bf16[512,448]{1,0:T(8,128)(2,1)}, bf16[512,448]{1,0:T(8,128)(2,1)}, u32[]{:S(2)}, u32[]{:S(2)}) collective-permute-start(bf16[512,448]{1,0:T(8,128)(2,1)} %collective-permute-done.24), channel_id=1, source_target_pairs={{1,0},{2,3},{5,4},{6,7},{9,8},{10,11},{13,12},{14,15},{17,16},{18,... | collective-permute-start | bytes 1376264 | tf_op jit(solution)/shard_map/ppermute | solution.py:133
  90.5 27.0 %collective-permute-start.7 = (bf16[3,448,256]{2,1,0:T(8,128)(2,1)}, bf16[3,448,256]{2,1,0:T(8,128)(2,1)}, u32[]{:S(2)}, u32[]{:S(2)}) collective-permute-start(bf16[3,448,256]{2,1,0:T(8,128)(2,1)} %collective-permute-done.6.refs_6_), channel_id=1, source_target_pairs={{1,2},{2,1},{5,6},{6,5},{9,10},{10,9},{13,14},{14,13},{17,18},{18,... | collective-permute-start | bytes 2064392 | tf_op jit(solution)/shard_map/ppermute | solution.py:133
  92.0 45.6 %collective-permute-start.10 = (bf16[3,448,256]{2,1,0:T(8,128)(2,1)}, bf16[3,448,256]{2,1,0:T(8,128)(2,1)}, u32[]{:S(2)}, u32[]{:S(2)}) collective-permute-start(bf16[3,448,256]{2,1,0:T(8,128)(2,1)} %copy-done.5), channel_id=1, source_target_pairs={{1,0},{2,3},{5,4},{6,7},{9,8},{10,11},{13,12},{14,15},{17,16},{18,... | collective-permute-start | bytes 2064392 | tf_op jit(solution)/shard_map/ppermute | solution.py:133
  103.8 48.6 %collective-permute-start.4 = (bf16[3,448,256]{2,1,0:T(8,128)(2,1)}, bf16[3,448,256]{2,1,0:T(8,128)(2,1)}, u32[]{:S(2)}, u32[]{:S(2)}) collective-permute-start(bf16[3,448,256]{2,1,0:T(8,128)(2,1)} %collective-permute-done.3.refs_5_), channel_id=1, source_target_pairs={{1,0},{2,3},{5,4},{6,7},{9,8},{10,11},{13,12},{14,15},{17,16},{18,... | collective-permute-start | bytes 2064392 | tf_op jit(solution)/shard_map/ppermute | solution.py:133
  113.7 63.2 %collective-permute-start.12 = (bf16[3,448,256]{2,1,0:T(8,128)(2,1)}, bf16[3,448,256]{2,1,0:T(8,128)(2,1)}, u32[]{:S(2)}, u32[]{:S(2)}) collective-permute-start(bf16[3,448,256]{2,1,0:T(8,128)(2,1)} %collective-permute-done.11.refs_7_), channel_id=1, source_target_pairs={{1,0},{2,3},{5,4},{6,7},{9,8},{10,11},{13,12},{14,15},{17,16},{18,... | collective-permute-start | bytes 2064392 | tf_op jit(solution)/shard_map/ppermute | solution.py:133
  117.4 89.3 %collective-permute-start.8 = (bf16[3,448,256]{2,1,0:T(8,128)(2,1)}, bf16[3,448,256]{2,1,0:T(8,128)(2,1)}, u32[]{:S(2)}, u32[]{:S(2)}) collective-permute-start(bf16[3,448,256]{2,1,0:T(8,128)(2,1)} %collective-permute-done.7.refs_7_), channel_id=1, source_target_pairs={{1,0},{2,3},{5,4},{6,7},{9,8},{10,11},{13,12},{14,15},{17,16},{18,... | collective-permute-start | bytes 2064392 | tf_op jit(solution)/shard_map/ppermute | solution.py:133
  120.9 85.7 %collective-permute-start.26 = (bf16[512,448]{1,0:T(8,128)(2,1)}, bf16[512,448]{1,0:T(8,128)(2,1)S(1)}, u32[]{:S(2)}, u32[]{:S(2)}) collective-permute-start(bf16[512,448]{1,0:T(8,128)(2,1)} %get-tuple-element.13), channel_id=1, source_target_pairs={{0,4},{1,5},{2,6},{3,7},{4,0},{5,1},{6,2},{7,3},{8,12},{9,13},{10,... | collective-permute-start | bytes 1376264 | tf_op jit(solution)/shard_map/ppermute | solution.py:133
  137.6 79.7 %collective-permute-start.27 = (bf16[512,448]{1,0:T(8,128)(2,1)S(1)}, bf16[512,448]{1,0:T(8,128)(2,1)S(1)}, u32[]{:S(2)}, u32[]{:S(2)}) collective-permute-start(bf16[512,448]{1,0:T(8,128)(2,1)S(1)} %copy-done.10), channel_id=1, source_target_pairs={{0,4},{1,5},{2,6},{3,7},{4,0},{5,1},{6,2},{7,3},{8,12},{9,13},{10,... | collective-permute-start | bytes 1376264 | tf_op jit(solution)/shard_map/ppermute | solution.py:133
  152.4 65.0 %collective-permute-start.28 = (bf16[512,448]{1,0:T(8,128)(2,1)S(1)}, bf16[512,448]{1,0:T(8,128)(2,1)S(1)}, u32[]{:S(2)}, u32[]{:S(2)}) collective-permute-start(bf16[512,448]{1,0:T(8,128)(2,1)S(1)} %get-tuple-element.15.refs_9_), channel_id=1, source_target_pairs={{0,16},{1,17},{2,18},{3,19},{4,20},{5,21},{6,22},{7,23},{8,24},{9,... | collective-permute-start | bytes 1376264 | tf_op jit(solution)/shard_map/ppermute | solution.py:133
  176.9 43.6 %collective-permute-start.29 = (bf16[512,448]{1,0:T(8,128)(2,1)S(1)}, bf16[512,448]{1,0:T(8,128)(2,1)S(1)}, u32[]{:S(2)}, u32[]{:S(2)}) collective-permute-start(bf16[512,448]{1,0:T(8,128)(2,1)S(1)} %get-tuple-element.14.refs_10_), channel_id=1, source_target_pairs={{0,16},{1,17},{2,18},{3,19},{4,20},{5,21},{6,22},{7,23},{8,24},{9,... | collective-permute-start | bytes 1376264 | tf_op jit(solution)/shard_map/ppermute | solution.py:133
  206.6 16.4 %collective-permute-start.30 = (bf16[512,448]{1,0:T(8,128)(2,1)S(1)}, bf16[512,448]{1,0:T(8,128)(2,1)}, u32[]{:S(2)}, u32[]{:S(2)}) collective-permute-start(bf16[512,448]{1,0:T(8,128)(2,1)S(1)} %collective-permute-done.26.refs_11_), channel_id=1, source_target_pairs={{0,16},{1,17},{2,18},{3,19},{4,20},{5,21},{6,22},{7,23},{8,24},{9,... | collective-permute-start | bytes 1376264 | tf_op jit(solution)/shard_map/ppermute | solution.py:133
  215.3 11.2 %collective-permute-start.13 = (bf16[528,256]{1,0:T(8,128)(2,1)}, bf16[528,256]{1,0:T(8,128)(2,1)}, u32[]{:S(2)}, u32[]{:S(2)}) collective-permute-start(bf16[528,256]{1,0:T(8,128)(2,1)} %get-tuple-element.7), channel_id=1, source_target_pairs={{0,16},{1,17},{2,18},{3,19},{4,20},{5,21},{6,22},{7,23},{8,24},{9,... | collective-permute-start | bytes 811016 | tf_op jit(solution)/shard_map/ppermute | solution.py:133
  217.4 10.4 %collective-permute-start.14 = (bf16[528,256]{1,0:T(8,128)(2,1)}, bf16[528,256]{1,0:T(8,128)(2,1)}, u32[]{:S(2)}, u32[]{:S(2)}) collective-permute-start(bf16[528,256]{1,0:T(8,128)(2,1)} %get-tuple-element.6.refs_1_), channel_id=1, source_target_pairs={{0,8},{1,9},{2,10},{3,11},{4,12},{5,13},{6,14},{7,15},{8,0},{9,1},... | collective-permute-start | bytes 811016 | tf_op jit(solution)/shard_map/ppermute | solution.py:133
  217.4 13.8 %collective-permute-start.15 = (bf16[528,256]{1,0:T(8,128)(2,1)}, bf16[528,256]{1,0:T(8,128)(2,1)S(1)}, u32[]{:S(2)}, u32[]{:S(2)}) collective-permute-start(bf16[528,256]{1,0:T(8,128)(2,1)} %get-tuple-element.7), channel_id=1, source_target_pairs={{0,24},{1,25},{2,26},{3,27},{4,28},{5,29},{6,30},{7,31},{8,16},{9,... | collective-permute-start | bytes 811016 | tf_op jit(solution)/shard_map/ppermute | solution.py:133
  220.5 20.7 %collective-permute-start.31 = (bf16[512,448]{1,0:T(8,128)(2,1)S(1)}, bf16[512,448]{1,0:T(8,128)(2,1)S(1)}, u32[]{:S(2)}, u32[]{:S(2)}) collective-permute-start(bf16[512,448]{1,0:T(8,128)(2,1)S(1)} %collective-permute-done.27.refs_12_), channel_id=1, source_target_pairs={{0,16},{1,17},{2,18},{3,19},{4,20},{5,21},{6,22},{7,23},{8,24},{9,... | collective-permute-start | bytes 1376264 | tf_op jit(solution)/shard_map/ppermute | solution.py:133
  223.0 18.2 %collective-permute-start.16 = (bf16[528,256]{1,0:T(8,128)(2,1)}, bf16[528,256]{1,0:T(8,128)(2,1)S(1)}, u32[]{:S(2)}, u32[]{:S(2)}) collective-permute-start(bf16[528,256]{1,0:T(8,128)(2,1)} %get-tuple-element.6.refs_1_), channel_id=1, source_target_pairs={{0,4},{1,5},{2,6},{3,7},{4,0},{5,1},{6,2},{7,3},{8,12},{9,13},{10,... | collective-permute-start | bytes 811016 | tf_op jit(solution)/shard_map/ppermute | solution.py:133
  226.5 14.7 %collective-permute-start.17 = (bf16[528,256]{1,0:T(8,128)(2,1)}, bf16[528,256]{1,0:T(8,128)(2,1)S(1)}, u32[]{:S(2)}, u32[]{:S(2)}) collective-permute-start(bf16[528,256]{1,0:T(8,128)(2,1)} %collective-permute-done.13.refs_2_), channel_id=1, source_target_pairs={{0,4},{1,5},{2,6},{3,7},{4,0},{5,1},{6,2},{7,3},{8,12},{9,13},{10,... | collective-permute-start | bytes 811016 | tf_op jit(solution)/shard_map/ppermute | solution.py:133
  227.7 13.5 %collective-permute-start.18 = (bf16[528,256]{1,0:T(8,128)(2,1)}, bf16[528,256]{1,0:T(8,128)(2,1)S(1)}, u32[]{:S(2)}, u32[]{:S(2)}) collective-permute-start(bf16[528,256]{1,0:T(8,128)(2,1)} %collective-permute-done.14.refs_3_), channel_id=1, source_target_pairs={{0,4},{1,5},{2,6},{3,7},{4,0},{5,1},{6,2},{7,3},{8,12},{9,13},{10,... | collective-permute-start | bytes 811016 | tf_op jit(solution)/shard_map/ppermute | solution.py:133
  231.2 10.0 %collective-permute-start.19 = (bf16[528,256]{1,0:T(8,128)(2,1)S(1)}, bf16[528,256]{1,0:T(8,128)(2,1)S(1)}, u32[]{:S(2)}, u32[]{:S(2)}) collective-permute-start(bf16[528,256]{1,0:T(8,128)(2,1)S(1)} %collective-permute-done.15.refs_4_), channel_id=1, source_target_pairs={{0,4},{1,5},{2,6},{3,7},{4,0},{5,1},{6,2},{7,3},{8,12},{9,13},{10,... | collective-permute-start | bytes 811016 | tf_op jit(solution)/shard_map/ppermute | solution.py:133
  (19 other events, 489.5 us)

commit v2 on v1

--- a/solution.py
+++ b/solution.py
@@ -120,7 +120,7 @@
     return (shape["ctx"], shape["tp"], shape["rep"]) == (2, 4, 4)
 
 
-def move(value, target):
+def move(value, target, name="move"):
     sizes = [lax.axis_size(name) for name in AXES]
     pairs = []
     for c in range(sizes[0]):
@@ -130,7 +130,12 @@
                 if to is not None:
                     at = (c * sizes[1] + t) * sizes[2] + r
                     pairs.append((at, (to[0] * sizes[1] + to[1]) * sizes[2] + to[2]))
-    return lax.ppermute(value, AXES, pairs)
+    with jax.named_scope(name):
+        return lax.ppermute(value, AXES, pairs)
+
+
+def after(value, *earlier):
+    return lax.optimization_barrier((value, *earlier))[0]
 
 
 def to_ctx(c, t, r):
@@ -169,10 +174,62 @@
     return pl.BlockSpec(shape, lambda *_: (0,) * len(shape))
 
 
+def split_kernel(scalars, kept_in, given_in, out_in, kept_ref, given_ref):
+    kinds = kept_in.shape[0]
+    kept_ref[:kinds] = kept_in[...]
+    given_ref[...] = given_in[...]
+    wide = kept_ref.shape[2]
+    for half in range(kept_ref.shape[0] - kinds):
+        kept_ref[kinds + half] = out_in[:, half * wide : (half + 1) * wide]
+
+
+def split(scalars, weight, out_weight):
+    kinds, rows, columns = weight.shape
+    wide = columns // 2
+    half = (kinds, rows, wide)
+    kept = (kinds + out_weight.shape[1] // wide, rows, wide)
+    return pl.pallas_call(
+        split_kernel,
+        grid_spec=pltpu.PrefetchScalarGridSpec(
+            num_scalar_prefetch=1,
+            grid=(1,),
+            in_specs=[
+                pl.BlockSpec(half, lambda i, s: (0, 0, s[0])),
+                pl.BlockSpec(half, lambda i, s: (0, 0, 1 - s[0])),
+                whole(out_weight.shape),
+            ],
+            out_specs=[whole(kept), whole(half)],
+        ),
+        out_shape=[jax.ShapeDtypeStruct(kept, weight.dtype), jax.ShapeDtypeStruct(half, weight.dtype)],
+        compiler_params=params(),
+        name="split",
+    )(scalars, weight, weight, out_weight)
+
+
 def embed_kernel(parts, spikes_ref, thresholds_ref, scale_ref, out_ref):
-    counts = spikes_ref[...]
-    gated = jnp.where(counts >= thresholds_ref[...], counts, 0)
-    x = (gated.astype(jnp.float32) * scale_ref[...]).astype(jnp.bfloat16)
+    place(parts, spikes_ref[...], thresholds_ref, scale_ref, out_ref)
+
+
+def embed_steps_kernel(parts, spikes_ref, thresholds_ref, scale_ref, out_ref):
+    steps, groups, width = spikes_ref.shape
+    rows = [spikes_ref[step] for step in range(steps)]
+    rows.append(jnp.zeros((DEC_PAD - steps * groups, width), spikes_ref.dtype))
+    place(parts, jnp.concatenate(rows, axis=0), thresholds_ref, scale_ref, out_ref)
+
+
+def embed_steps(spikes, thresholds, scale, parts):
+    width = spikes.shape[2]
+    return pl.pallas_call(
+        lambda *refs: embed_steps_kernel(parts, *refs),
+        out_shape=jax.ShapeDtypeStruct((parts, DEC_PAD, width // parts), jnp.bfloat16),
+        compiler_params=params(),
+        name="embed_steps",
+    )(spikes, thresholds, scale)
+
+
+def place(parts, counts, thresholds_ref, scale_ref, out_ref):
+    gated = jnp.where(counts >= thresholds_ref[...][None], counts, 0)
+    x = (gated.astype(jnp.float32) * scale_ref[...][None]).astype(jnp.bfloat16)
     width = x.shape[1] // (2 * parts)
     for z in range(parts):
         first = x[:, z * width : (z + 1) * width]
@@ -187,23 +244,21 @@
         grid=(rows // tile,),
         in_specs=[
             pl.BlockSpec((tile, width), lambda i: (i, 0)),
-            whole((1, width)),
-            whole((1, width)),
+            whole((width,)),
+            whole((width,)),
         ],
         out_specs=pl.BlockSpec((parts, tile, width // parts), lambda i: (0, i, 0)),
         out_shape=jax.ShapeDtypeStruct((parts, rows, width // parts), jnp.bfloat16),
         compiler_params=params(),
         name="embed",
-    )(spikes, thresholds[None], scale[None])
+    )(spikes, thresholds, scale)
 
 
 def weights_of(scalars, mine, other, index):
-    if len(mine) == 2:
-        flag = scalars[1] == 1
-        own = jnp.where(flag, mine[1][index], mine[0][index])
-        far = jnp.where(flag, other[1][index], other[0][index])
-    else:
-        own, far = mine[0][index], other[0][index]
+    def pick(refs):
+        return refs[0][index] if len(refs) == 1 else jnp.where(scalars[1] == 1, refs[1][index], refs[0][index])
+
+    own, far = pick(mine), pick(other)
     first = scalars[0] == 0
     return jnp.concatenate([jnp.where(first, own, far), jnp.where(first, far, own)], axis=0)
 
@@ -216,59 +271,55 @@
         at += rows
 
 
-def project_kernel(candidates, has_sum, scalars, *refs):
-    x_refs = refs[:4]
-    mine = refs[4 : 4 + candidates]
-    other = refs[4 + candidates : 4 + 2 * candidates]
-    out_ref = refs[-1]
-    sum_ref = refs[-2] if has_sum else None
-    for index in range(3):
-        weight = weights_of(scalars, mine, other, index)
-        columns = slice(index * weight.shape[1], (index + 1) * weight.shape[1])
-        for ref, at, rows in row_blocks(x_refs):
-            term = jnp.dot(ref[0], weight, preferred_element_type=jnp.float32)
-            if has_sum:
-                term = sum_ref[at : at + rows, columns] + term
-            out_ref[at : at + rows, columns] = term
+def project_kernel(steps, has_sum, scalars, *refs):
+    x_refs, out_ref = refs[:4], refs[-1]
+    mine, other = refs[4 : 4 + steps], refs[4 + steps : 4 + 2 * steps]
+    for step in range(steps):
+
+        @pl.when(pl.program_id(0) == step)
+        def _(step=step):
+            for index in range(3):
+                weight = weights_of(scalars, mine[step : step + 1], other[step : step + 1], index)
+                columns = slice(index * weight.shape[1], (index + 1) * weight.shape[1])
+                for ref, at, rows in row_blocks(x_refs):
+                    term = jnp.dot(ref[0], weight, preferred_element_type=jnp.float32)
+                    if step or has_sum:
+                        term = (out_ref if step else refs[-2])[at : at + rows, columns] + term
+                    out_ref[at : at + rows, columns] = term
 
 
 def part_spec(array, step):
     block = (1,) + array.shape[1:]
-    return pl.BlockSpec(block, lambda i, scalars: (scalars[3 + step], 0, 0))
-
-
-def project(scalars, step, xs, mine, other, summed):
+    return pl.BlockSpec(block, lambda i, scalars: (scalars[3 + step + i], 0, 0))
+
+
+def project(scalars, first, xs, mine, other, summed):
+    steps = len(mine)
     rows = sum(x.shape[1] for x in xs)
     columns = 3 * mine[0].shape[2]
-    operands = [*xs, *mine, *other]
-    in_specs = [part_spec(x, step) for x in xs]
-    in_specs += [whole(w.shape) for w in (*mine, *other)]
-    if summed is not None:
-        operands.append(summed)
-        in_specs.append(whole(summed.shape))
+    earlier = [] if summed is None else [summed]
     return pl.pallas_call(
-        lambda *refs: project_kernel(len(mine), summed is not None, *refs),
+        lambda *refs: project_kernel(steps, bool(earlier), *refs),
         grid_spec=pltpu.PrefetchScalarGridSpec(
             num_scalar_prefetch=1,
-            grid=(1,),
-            in_specs=in_specs,
+            grid=(steps,),
+            in_specs=[part_spec(x, first) for x in xs]
+            + [whole(other[0].shape) for _ in (*mine, *other)]
+            + [whole(sums.shape) for sums in earlier],
             out_specs=whole((rows, columns)),
         ),
         out_shape=jax.ShapeDtypeStruct((rows, columns), jnp.float32),
         compiler_params=params(),
-        cost_estimate=pl.CostEstimate(
-            flops=2 * rows * columns * xs[0].shape[2], bytes_accessed=8 * rows * columns, transcendentals=0
-        ),
         name="project",
-    )(scalars, *operands)
+    )(scalars, *xs, *mine, *other, *earlier)
 
 
 def attend_kernel(
-    dims, scalars, own_x, first_x, second_x, dec_x, m0, m1, o0, o1, sum_ref, prior_ref, gain_ref, lengths, near_ref, far_ref, qkv
+    dims, scalars, own_x, first_x, second_x, dec_x, mine, other0, other1, sum_ref, prior_ref, gain_ref, lengths, near_ref, far_ref, qkv
 ):
     groups, block, heads, head, steps = dims
     for index in range(3):
-        weight = weights_of(scalars, (m0, m1), (o0, o1), index)
+        weight = weights_of(scalars, (mine,), (other0, other1), index)
         columns = slice(index * weight.shape[1], (index + 1) * weight.shape[1])
         for ref, at, rows in row_blocks((own_x, first_x, second_x, dec_x)):
             term = jnp.dot(ref[0], weight, preferred_element_type=jnp.float32)
@@ -336,7 +387,7 @@
     rows, columns = summed.shape
     shape = (groups * block + DEC_PAD, heads * head)
     in_specs = [part_spec(x, 3) for x in xs]
-    in_specs += [whole(w.shape) for w in (*mine, *other, summed)]
+    in_specs += [whole(other[0].shape) for _ in (*mine, *other)] + [whole(summed.shape)]
     in_specs += [
         pl.BlockSpec((groups, heads, head, head), lambda i, s: (0, s[0], 0, 0)),
         whole(gain.shape),
@@ -361,36 +412,69 @@
     )(scalars, *xs, *mine, *other, summed, prior, gain, lengths)
 
 
-def combine_kernel(dims, scalars, *refs):
-    prompt, dec = dims
-    hidden, weights = refs[:8], refs[8:16]
-    res_ref, dec_res_ref, out_ref, dec_ref = refs[16:]
-    here_first = scalars[0] == 0
-    same = scalars[1] == 1
-    total = None
+def combine_kernel(scalars, *refs):
+    hidden, blocks = refs[:8], refs[8:12]
+    res_ref, dec_res_ref, out_ref, dec_ref, rows, weights, hidden_sems, weight_sems = refs[12:]
+    wide = hidden[0].shape[1]
+
+    def hidden_copy(i, j):
+        part = scalars[0] if j == 0 else 1 - scalars[0]
+        at = pl.ds(pl.multiple_of((2 * i + part) * wide, wide), wide)
+        source = hidden[4 * (i % 2) + 2 * (i // 2) + j]
+        return pltpu.make_async_copy(source, rows.at[:, at], hidden_sems.at[i, j])
+
+    def weight_copy(i, slot, part, plane):
+        source = blocks[2 * (plane // 2) + i % 2].at[i // 2, plane % 2, part]
+        at = pl.ds((2 * i + part) * wide, wide)
+        return pltpu.make_async_copy(source, weights.at[slot, :, at], weight_sems.at[i, slot, part])
+
+    every = [(i, slot, part) for slot in range(2) for i in range(4) for part in range(2)]
     for i in range(4):
-        core, moved = i % 2, i // 2
-        def piece(j):
-            return jnp.where(same, hidden[core * 4 + j + 2 * moved][...], hidden[core * 4 + j + 2 * (1 - moved)][...])
-
-        near, far = piece(0), piece(1)
-        rows = jnp.concatenate([jnp.where(here_first, near, far), jnp.where(here_first, far, near)], axis=1)
-        weight = jnp.concatenate([weights[2 * i][...], weights[2 * i + 1][...]], axis=1)
-        term = jnp.dot(rows, weight, preferred_element_type=jnp.float32)
-        total = term if total is None else total + term
-    out_ref[...] = (res_ref[...].astype(jnp.float32) + total[:prompt]).astype(jnp.bfloat16)
-    dec_ref[...] = (dec_res_ref[...].astype(jnp.float32) + total[prompt : prompt + dec]).astype(jnp.bfloat16)
-
-
-def combine(scalars, hidden, weights, res, dec_res):
-    operands = [*hidden, *weights, res, dec_res]
+        for j in range(2):
+            hidden_copy(i, j).start()
+    for chosen, planes in enumerate(((0, 1), (1, 0), (2, 3), (3, 2))):
+
+        @pl.when(scalars[1] == chosen)
+        def _(planes=planes):
+            for i, slot, part in every:
+                weight_copy(i, slot, part, planes[slot]).start()
+
+    for i in range(4):
+        for j in range(2):
+            hidden_copy(i, j).wait()
+    total = []
+    for slot in range(2):
+        for i, at, part in every:
+            if at == slot:
+                weight_copy(i, slot, part, 0).wait()
+        total.append(
+            lax.dot_general(rows[...], weights[slot], (((1,), (1,)), ((), ())), preferred_element_type=jnp.float32)
+        )
+    total = jnp.concatenate(total, axis=1)
+    groups, block = out_ref.shape[:2]
+    for r in range(groups):
+        out_ref[r] = (res_ref[r].astype(jnp.float32) + total[r * block : (r + 1) * block]).astype(jnp.bfloat16)
+    for step in range(dec_ref.shape[0]):
+        at = groups * block + step * groups
+        dec_ref[step] = (dec_res_ref[step].astype(jnp.float32) + total[at : at + groups]).astype(jnp.bfloat16)
+
+
+def combine(scalars, hidden, blocks, res, dec_res):
+    anywhere = pl.BlockSpec(memory_space=pl.ANY)
     return pl.pallas_call(
-        lambda *refs: combine_kernel((res.shape[0], dec_res.shape[0]), *refs),
+        combine_kernel,
         grid_spec=pltpu.PrefetchScalarGridSpec(
             num_scalar_prefetch=1,
             grid=(1,),
-            in_specs=[whole(a.shape) for a in operands],
+            in_specs=[anywhere] * (len(hidden) + len(blocks))
+            + [whole(res.shape), whole(dec_res.shape)],
             out_specs=[whole(res.shape), whole(dec_res.shape)],
+            scratch_shapes=[
+                pltpu.VMEM((hidden[0].shape[0], 8 * hidden[0].shape[1]), jnp.bfloat16),
+                pltpu.VMEM((2, blocks[0].shape[3], 8 * blocks[0].shape[4]), jnp.bfloat16),
+                pltpu.SemaphoreType.DMA((4, 2)),
+                pltpu.SemaphoreType.DMA((4, 2, 2)),
+            ],
         ),
         out_shape=[
             jax.ShapeDtypeStruct(res.shape, jnp.bfloat16),
@@ -398,16 +482,7 @@
         ],
         compiler_params=params(),
         name="combine",
-    )(scalars, *operands)
-
-
-def spread(value, is_end):
-    pair = move(value, to_pair)
-    third_mid = move(value, mid_swap)
-    fourth_mid = move(pair, mid_swap)
-    third_end = move(third_mid, mid_to_end)
-    fourth_end = move(fourth_mid, mid_to_end)
-    return (value,), (pair,), (third_mid, third_end), (fourth_mid, fourth_end)
+    )(scalars, *hidden, *blocks, res, dec_res)
 
 
 def local_grid(
@@ -417,70 +492,99 @@
     steps = dec_spikes.shape[0]
     all_heads, head = head_gain.shape
     heads = all_heads // 2
-    wide = heads * head
     planes = lax.axis_size("rep")
     c, t, z = (lax.axis_index(name) for name in AXES)
-    parity = t % 2
-    y = t // 2
+    parity = t & 1
+    y = t >> 1
     is_end = (z == 0) | (z == planes - 1)
     end = is_end.astype(jnp.int32)
     third = jnp.where(is_end, z ^ 2, z ^ 3)
     fourth = jnp.where(is_end, z ^ 3, z ^ 2)
     scalars = jnp.stack([c, end, parity, z, z ^ 1, third, fourth]).astype(jnp.int32)
 
-    kept = lax.dynamic_slice_in_dim(qkv_weight, c * wide, wide, 2)
-    given = lax.dynamic_slice_in_dim(qkv_weight, (1 - c) * wide, wide, 2)
-    other = move(given, to_ctx)
-    mine_parts = spread(kept, is_end)
-    other_parts = spread(other, is_end)
+    def meet(c, t, r):
+        return (1 - c, t, r) if c == t // 2 else (c, t ^ 2, r)
+
+    def corner(c, t, r):
+        return None if c == t // 2 else (1 - c, t ^ 2, r)
+
+    def near_pass(c, t, r):
+        return None if t % 2 == r // 2 else (c, t ^ 1, r)
+
+    def far_pass(c, t, r):
+        return (c, t ^ 1, r) if t % 2 == r // 2 else None
+
+    kept, given = split(scalars, qkv_weight, out_weight.T)
+    pair_kept = move(kept, to_pair, "pair_kept")
+    mid1_kept = move(kept, mid_swap, "mid1_kept")
+    other = move(given, to_ctx, "pre_w")
 
     counts = spikes.reshape(groups * block, width)
-    dec_counts = dec_spikes.reshape(steps * groups, width)
-    dec_padded = jnp.pad(dec_counts, ((0, DEC_PAD - steps * groups), (0, 0)))
-    own_x = embed(counts, thresholds, in_scale, planes, block // 2)
-    dec_x = embed(dec_padded, thresholds, in_scale, planes, DEC_PAD)
-    first_x = move(lax.dynamic_slice_in_dim(own_x, parity * block, block, 1), to_ctx)
-    second_x = move(first_x, to_core)
-    xs = (own_x, first_x, second_x, dec_x)
-
-    def meet(c, t, r):
-        return (c, t, r) if c == t // 2 else (1 - c, t ^ 2, r)
-
-    out_block = move(out_weight, meet)
-    (o_own,), (o_pair,), o_third, o_fourth = spread(out_block, is_end)
-    o_third = jnp.where(is_end, o_third[1], o_third[0])
-    o_fourth = jnp.where(is_end, o_fourth[1], o_fourth[0])
-    z_even = z % 2 == 0
-    low = z < 2
-    near_half = (jnp.where(z_even, o_own, o_pair), jnp.where(z_even, o_pair, o_own))
-    far_half = (jnp.where(low, o_third, o_fourth), jnp.where(low, o_fourth, o_third))
-    near_mine = z // 2 == parity
-    used = [jnp.where(near_mine, a, b) for a, b in zip(near_half, far_half)]
-    passed = [jnp.where(near_mine, b, a) for a, b in zip(near_half, far_half)]
-    sibling = [move(p, to_core) for p in passed]
-    out_weights = used + sibling + [move(u, to_ctx) for u in used] + [move(s, to_ctx) for s in sibling]
-
-    summed = None
-    for step in range(3):
-        summed = project(scalars, step, xs, mine_parts[step], other_parts[step], summed)
-    gain = lax.dynamic_slice_in_dim(head_gain, c * heads, heads, 0)
-    near, far = attend(
-        scalars, xs, mine_parts[3], other_parts[3], summed, prior_state, gain, lengths, (groups, block, heads, head, steps)
-    )
-    mine = [near, move(far, to_ctx), move(near, to_y), move(far, to_diagonal)]
-    hidden = mine + [move(m, to_core) for m in mine]
+    own_x = embed(counts, thresholds, in_scale, planes, block // 4)
+    given_x = lax.dynamic_slice_in_dim(own_x, parity * block, block, 1)
+
+    first_x = move(after(given_x, other), to_ctx, "x_ctx")
+
+    stage = (pair_kept, mid1_kept, other, given_x)
+    mid2_kept = move(after(pair_kept, *stage), mid_swap, "mid2_kept")
+    end1_kept = move(after(mid1_kept, *stage), mid_to_end, "end1_kept")
+    pair_other = move(after(other, *stage), to_pair, "pair_other")
+    mid1_other = move(after(other, *stage), mid_swap, "mid1_other")
+    dec_x = embed_steps(after(dec_spikes, *stage), thresholds, in_scale, planes)
 
     columns = width // lax.axis_size("tp")
 
     def gate(rows):
-        part = lax.dynamic_slice_in_dim(rows, t * columns, columns, 1)
+        part = lax.dynamic_slice_in_dim(rows, t * columns, columns, 2)
         level = lax.dynamic_slice_in_dim(thresholds, t * columns, columns, 0)
         scale = lax.dynamic_slice_in_dim(in_scale, t * columns, columns, 0)
         return (jnp.where(part >= level, part, 0).astype(jnp.float32) * scale).astype(jnp.bfloat16)
 
-    flags = jnp.stack([c, (c == y).astype(jnp.int32)]).astype(jnp.int32)
-    out, dec_out = combine(flags, hidden, out_weights, gate(counts), gate(dec_counts))
-    return out.reshape(groups, block, columns), dec_out.reshape(steps, groups, columns)
+    res, dec_res = gate(after(spikes, *stage)), gate(after(dec_spikes, *stage))
+    near_blocks = jnp.stack([after(kept, *stage)[3:], pair_kept[3:]])
+
+    stage = (mid2_kept, end1_kept, pair_other, mid1_other, first_x, near_blocks, dec_x, res, dec_res)
+    end2_kept = move(after(mid2_kept, *stage), mid_to_end, "end2_kept")
+    mid2_other = move(after(pair_other, *stage), mid_swap, "mid2_other")
+    end1_other = move(after(mid1_other, *stage), mid_to_end, "end1_other")
+    second_x = move(after(first_x, *stage), to_core, "x_core")
+    xs = (own_x, first_x, second_x, dec_x)
+    summed = project(scalars, 0, xs, (kept, pair_kept), (other, pair_other), None)
+
+    def carry(blocks, name):
+        return blocks, move(blocks, meet, name + "_meet"), move(blocks, corner, name + "_corner")
+
+    def place_out(blocks, met, far, passing, name):
+        own = jnp.where(c == y, jnp.stack([blocks, met]), jnp.stack([met, far]))
+        return own, move(own, passing, name + "_core")
+
+    third_kept = jnp.where(is_end, end1_kept, mid1_kept)
+    near = carry(after(near_blocks, second_x, third_kept), "near")
+
+    stage = (mid2_other, end1_other, summed)
+    end2_other = move(after(mid2_other, *stage), mid_to_end, "end2_other")
+    near = place_out(near[0], near[1], after(near[2], summed), near_pass, "near")
+    third_other = jnp.where(is_end, after(end1_other, *stage), mid1_other)
+    summed = project(scalars, 2, xs, (third_kept,), (third_other,), summed)
+    fourth_kept = jnp.where(is_end, after(end2_kept, *stage), mid2_kept)
+    far = carry(after(jnp.stack([third_kept[3:], fourth_kept[3:]]), near[0]), "far")
+    gain = lax.dynamic_slice_in_dim(head_gain, c * heads, heads, 0)
+
+    dims = (groups, block, heads, head, steps)
+    own_rows, far_rows = attend(
+        scalars, xs, (fourth_kept,), (mid2_other, end2_other), summed, prior_state, gain, lengths, dims
+    )
+    h_ctx = move(far_rows, to_ctx, "h_ctx")
+    h_y = move(own_rows, to_y, "h_y")
+    h_diag = move(far_rows, to_diagonal, "h_diag")
+    mine = [own_rows, h_ctx, h_y, h_diag]
+    far = place_out(far[0], far[1], after(far[2], h_ctx, h_y, h_diag), far_pass, "far")
+    hidden = mine + [move(m, to_core, "h_core") for m in mine]
+
+    near_first = z & 1
+    far_first = 2 + (z >> 1)
+    flags = jnp.stack([c, jnp.where((z >> 1) == parity, near_first, far_first)]).astype(jnp.int32)
+    return combine(flags, hidden, near + far, res, dec_res)
 
 
 def solution(mesh):

time: 252 us -> 193 us (0.77); the launches traced: 251 us -> 189 us
  starting transfers between devices: 76.3 us -> 43.9 us
  waiting for transfers between devices: 106 us -> 74.5 us
  local copies, waits for them, and re-layouts: 15.5 us -> 7.55 us
  other arithmetic: 8.38 us -> 16.1 us
    ppermute x32 -> x26, starting transfers between devices: 76.3 us -> 43.9 us  [move(): return lax.ppermute(value, AXES, pairs)]
    ppermute x32 -> x26, waiting for transfers between devices: 106 us -> 74.5 us  [move(): return lax.ppermute(value, AXES, pairs)]
    select_n x2 -> x5, other arithmetic: 4.43 us -> 9.22 us  [the longest x2 5.67 us: place_out(): own = jnp.where(c == y, jnp.stack([blocks, met]), jnp.stack([met, far]))]
    broadcast_in_dim x2 -> x0, local copies, waits for them, and re-layouts: 2.65 us -> none  [the longest x1 1.33 us: embed(): thresholds[None]]
    dynamic_slice x2 -> x1, local copies, waits for them, and re-layouts: 5.14 us -> 2.91 us  [local_grid(): given_x = lax.dynamic_slice_in_dim(own_x, parity * block, block, 1)]
    pallas_call x4 -> x5, Pallas kernels: 28.4 us -> 29.8 us  [the longest x2 16 us: project(): pl.pallas_call(lambda *refs: project_kernel(steps, bool(earlier), *refs),...]
    pallas_call x2 -> x1, Pallas kernels: 7.68 us -> 7.75 us  [embed(): pl.pallas_call(lambda *refs: embed_kernel(parts, *refs), grid=(rows // ti...]
  transfers between devices with their start and end apart: 32 -> 26, of which waited for: 11 -> 8; matrix products, arithmetic and copies ran while one was open for 6% -> 12% of each run, Pallas kernels for 13% -> 18%
where the time goes in v2:
time: 193 us; the launch traced here: 189 us
  waiting for transfers between devices  74.5 us (39%)
  Pallas kernels  46 us (24%)
  starting transfers between devices  43.9 us (23%)
  other arithmetic  16.1 us (8%)
  local copies, waits for them, and re-layouts  7.55 us (4%)
    ppermute x26, waiting for transfers between devices, move(): return lax.ppermute(value, AXES, pairs)  74.5 us
    ppermute x26, starting transfers between devices, move(): return lax.ppermute(value, AXES, pairs)  43.9 us
    pallas_call x2, Pallas kernels, project(): pl.pallas_call(lambda *refs: project_kernel(steps, bool(earlier), *refs),...  16 us
    pallas_call x1, Pallas kernels, combine(): pl.pallas_call(combine_kernel, grid_spec=pltpu.PrefetchScalarGridSpec(num...  8.61 us
    pallas_call x1, Pallas kernels, attend(): pl.pallas_call(lambda *refs: attend_kernel(dims, *refs), grid_spec=pltpu....  8.44 us
    pallas_call x1, Pallas kernels, embed(): pl.pallas_call(lambda *refs: embed_kernel(parts, *refs), grid=(rows // ti...  7.75 us
    select_n x2, other arithmetic, place_out(): own = jnp.where(c == y, jnp.stack([blocks, met]), jnp.stack([met, far]))  5.67 us
    convert_element_type x2, other arithmetic, gate(): (jnp.where(part >= level, part, 0).astype(jnp.float32) * scale).astype(jn...  4.06 us
  transfers between devices with their start and end apart: 26, of which 8 were waited for; matrix products, arithmetic and copies ran while one was open for 12% of the time, Pallas kernels for 18%

profile of v2, /device:TPU:0, one launch (start us, length us, event | category | flops | bytes accessed | tf_op | source)
XLA Modules:
  0.0 189.0 jit_solution(12810644340671243847)
XLA Ops:
  1.3 3.5 %split.1 = (bf16[5,448,256]{2,1,0:T(8,128)(2,1)}, bf16[3,448,256]{2,1,0:T(8,128)(2,1)}) custom-call(s32[7]{0:T(128)} %stack.94.scalars.refs_0_, bf16[3,448,512]{2,1,0:T(8,128)(2,1)} %given_in.1, bf16[3,448,512]{2,1,0:T(8,128)(2,1)} %given_in.1, bf16[448,512]{1,0:T(8,128)(2,1)} %bitcast.26), custom_call_target="tpu_custom_call" | custom-call | tf_op jit(solution)/shard_map/split/pallas_call | solution.py:191
  4.8 2.9 %collective-permute-start = (bf16[3,448,256]{2,1,0:T(8,128)(2,1)}, bf16[3,448,256]{2,1,0:T(8,128)(2,1)}, u32[]{:S(2)}, u32[]{:S(2)}) collective-permute-start(bf16[3,448,256]{2,1,0:T(8,128)(2,1)} %get-tuple-element.24), channel_id=1, source_target_pairs={{0,16},{1,17},{2,18},{3,19},{4,20},{5,21},{6,22},{7,23},{8,24},{9,... | collective-permute-start | bytes 2064392 | tf_op jit(solution)/shard_map/pre_w/ppermute | solution.py:134
  7.8 1.6 collective-permute-start.2
  9.3 1.7 collective-permute-start.3
  11.0 7.8 %embed.1.refs_1_ = bf16[4,512,896]{2,1,0:T(8,128)(2,1)} custom-call(s32[512,3584]{1,0:T(8,128)} %bitcast.24, s32[3584]{0:T(1024)} %refs_1_.3, f32[3584]{0:T(1024)} %refs_2_.3), custom_call_target="tpu_custom_call" | custom-call | tf_op jit(solution)/shard_map/embed/pallas_call | solution.py:242
  18.8 2.9 %constant_dynamic-slice_fusion.1 = bf16[4,256,896]{2,1,0:T(8,128)(2,1)} fusion(bf16[4,512,896]{2,1,0:T(8,128)(2,1)} %embed.1.refs_1_, s32[]{:T(128)S(6)} %select_n.67), kind=kLoop, calls=%fused_computation.20 | loop fusion | bytes 3670020 | tf_op jit(solution)/shard_map/dynamic_slice | solution.py:524
  21.7 1.8 collective-permute-done.refs_7_
  23.5 1.7 collective-permute-start.1
  25.3 9.4 %collective-permute-done.2.refs_6_ = bf16[5,448,256]{2,1,0:T(8,128)(2,1)S(1)} collective-permute-done((bf16[5,448,256]{2,1,0:T(8,128)(2,1)}, bf16[5,448,256]{2,1,0:T(8,128)(2,1)S(1)}, u32[]{:S(2)}, u32[]{:S(2)}) %collective-permute-start.2) | collective-permute-done | bytes 1146912 | tf_op jit(solution)/shard_map/pair_kept/ppermute | solution.py:134
  36.0 1.8 collective-permute-start.4
  39.3 7.6 %collective-permute-start.6 = (bf16[3,448,256]{2,1,0:T(8,128)(2,1)}, bf16[3,448,256]{2,1,0:T(8,128)(2,1)}, u32[]{:S(2)}, u32[]{:S(2)}) collective-permute-start(bf16[3,448,256]{2,1,0:T(8,128)(2,1)} %collective-permute-done.refs_7_), channel_id=1, source_target_pairs={{0,1},{1,0},{2,3},{3,2},{4,5},{5,4},{6,7},{7,6},{8,9},{9,8},{10,11... | collective-permute-start | bytes 2064392 | tf_op jit(solution)/shard_map/pair_other/ppermute | solution.py:134
  46.9 1.5 collective-permute-start.7
  49.5 1.7 embed_steps.1.refs_4_
  53.6 2.7 %fusion.2.refs_12_ = bf16[2,256,896]{2,1,0:T(8,128)(2,1)} fusion(s32[2,256,3584]{2,1,0:T(8,128)} %param.9, s32[]{:T(128)S(6)} %select_n.68, f32[896]{0:T(1024)S(1)} %dynamic_slice.23, s32[896]{0:T(1024)S(1)} %dynamic_slice.22), kind=kLoop, calls=%fused_computation.3 | loop fusion | flops 2293760 | bytes 2759684 | tf_op jit(solution)/shard_map/convert_element_type | solution.py:541
  56.3 23.5 %collective-permute-done.6.refs_8_ = bf16[3,448,256]{2,1,0:T(8,128)(2,1)} collective-permute-done((bf16[3,448,256]{2,1,0:T(8,128)(2,1)}, bf16[3,448,256]{2,1,0:T(8,128)(2,1)}, u32[]{:S(2)}, u32[]{:S(2)}) %collective-permute-start.6) | collective-permute-done | bytes 688160 | tf_op jit(solution)/shard_map/pair_other/ppermute | solution.py:134
  82.5 1.5 collective-permute-start.10
  85.4 1.6 collective-permute-start.21
  87.1 3.3 %collective-permute-start.20 = (bf16[2,2,448,256]{3,2,1,0:T(8,128)(2,1)}, bf16[2,2,448,256]{3,2,1,0:T(8,128)(2,1)}, u32[]{:S(2)}, u32[]{:S(2)}) collective-permute-start(bf16[2,2,448,256]{3,2,1,0:T(8,128)(2,1)} %pad_maximum_fusion), channel_id=1, source_target_pairs={{0,16},{1,17},{2,18},{3,19},{4,20},{5,21},{6,22},{7,23},{8,0},{9,1... | collective-permute-start | bytes 2752520 | tf_op jit(solution)/shard_map/near_meet/ppermute | solution.py:134
  90.4 8.7 %project.2.refs_7_ = f32[1040,768]{1,0:T(8,128)} custom-call(s32[7]{0:T(128)} %stack.94.scalars.refs_0_, bf16[4,512,896]{2,1,0:T(8,128)(2,1)} %embed.1.refs_1_, bf16[4,256,896]{2,1,0:T(8,128)(2,1)} %copy-done.1, bf16[4,256,896]{2,1,0:T(8,128)(2,1)} %collective-permute-done.8.refs_3_, bf16[4,16,896]{2,1,0:T(8,128)(2,1)} %embed_steps.1.refs_4_, ...), custom_call_target="tpu_custom_call" | custom-call | tf_op jit(solution)/shard_map/project/pallas_call | solution.py:301
  99.1 27.5 %collective-permute-done.11 = bf16[3,448,256]{2,1,0:T(8,128)(2,1)} collective-permute-done((bf16[3,448,256]{2,1,0:T(8,128)(2,1)}, bf16[3,448,256]{2,1,0:T(8,128)(2,1)}, u32[]{:S(2)}, u32[]{:S(2)}) %collective-permute-start.11) | collective-permute-done | bytes 688160 | tf_op jit(solution)/shard_map/end1_other/ppermute | solution.py:134
  129.2 2.3 %maximum_select_fusion.refs_8_ = bf16[2,2,2,448,256]{4,3,2,1,0:T(8,128)(2,1)S(1)} fusion(bf16[1,2,2,448,256]{4,3,2,1,0:T(8,128)(2,1)} %bitcast.13, bf16[1,2,2,448,256]{4,3,2,1,0:T(8,128)(2,1)} %bitcast.12, bf16[1,2,2,448,256]{4,3,2,1,0:T(8,128)(2,1)} %bitcast.14, pred[]{:T(512)S(6)} %eq.16), kind=kLoop, calls=%fused_computation.4 | loop fusion | flops 2752512 | bytes 4587521 | tf_op jit(solution)/shard_map/jit(_where)/select_n | solution.py:558
  132.3 4.4 %collective-permute-start.23 = (bf16[2,2,448,256]{3,2,1,0:T(8,128)(2,1)}, bf16[2,2,448,256]{3,2,1,0:T(8,128)(2,1)}, u32[]{:S(2)}, u32[]{:S(2)}) collective-permute-start(bf16[2,2,448,256]{3,2,1,0:T(8,128)(2,1)} %pad_maximum_fusion.1), channel_id=1, source_target_pairs={{0,16},{1,17},{2,18},{3,19},{4,20},{5,21},{6,22},{7,23},{8,0},{9,1... | collective-permute-start | bytes 2752520 | tf_op jit(solution)/shard_map/far_meet/ppermute | solution.py:134
  137.3 2.0 %broadcast_select_fusion.2.refs_6_ = bf16[3,448,256]{2,1,0:T(8,128)(2,1)} fusion(bf16[3,448,256]{2,1,0:T(8,128)(2,1)} %collective-permute-done.11, bf16[3,448,256]{2,1,0:T(8,128)(2,1)} %collective-permute-done.7, pred[]{:T(512)S(6)} %or.3), kind=kLoop, calls=%fused_computation.10 | loop fusion | flops 344064 | bytes 2064385 | tf_op jit(solution)/shard_map/jit(_where)/select_n | solution.py:567
  139.3 7.3 %project.3.refs_8_ = f32[1040,768]{1,0:T(8,128)} custom-call(s32[7]{0:T(128)} %stack.94.scalars.refs_0_, bf16[4,512,896]{2,1,0:T(8,128)(2,1)} %embed.1.refs_1_, bf16[4,256,896]{2,1,0:T(8,128)(2,1)} %copy-done.1, bf16[4,256,896]{2,1,0:T(8,128)(2,1)} %collective-permute-done.8.refs_3_, bf16[4,16,896]{2,1,0:T(8,128)(2,1)} %embed_steps.1.refs_4_, ...), custom_call_target="tpu_custom_call" | custom-call | tf_op jit(solution)/shard_map/project/pallas_call | solution.py:301
  146.6 8.4 %attend.1 = (bf16[528,256]{1,0:T(8,128)(2,1)}, bf16[528,256]{1,0:T(8,128)(2,1)}) custom-call(s32[7]{0:T(128)} %stack.94.scalars.refs_0_, bf16[4,512,896]{2,1,0:T(8,128)(2,1)} %embed.1.refs_1_, bf16[4,256,896]{2,1,0:T(8,128)(2,1)} %copy-done.1, bf16[4,256,896]{2,1,0:T(8,128)(2,1)} %collective-permute-done.8.refs_3_, bf16[4,16,896]{2,1,0:T(8,128)(2,1)} %embed_steps.1.refs_4_, ...), custom_call_target="tpu_custom_call" | custom-call | flops 2862612480 | bytes 3194880 | tf_op jit(solution)/shard_map/attend/pallas_call | solution.py:397
  156.5 2.0 %collective-permute-start.15 = (bf16[528,256]{1,0:T(8,128)(2,1)}, bf16[528,256]{1,0:T(8,128)(2,1)}, u32[]{:S(2)}, u32[]{:S(2)}) collective-permute-start(bf16[528,256]{1,0:T(8,128)(2,1)} %get-tuple-element.41), channel_id=1, source_target_pairs={{0,24},{1,25},{2,26},{3,27},{4,28},{5,29},{6,30},{7,31},{8,16},{9,... | collective-permute-start | bytes 811016 | tf_op jit(solution)/shard_map/h_diag/ppermute | solution.py:134
  158.5 6.1 %collective-permute-done.13.refs_1_ = bf16[528,256]{1,0:T(8,128)(2,1)S(1)} collective-permute-done((bf16[528,256]{1,0:T(8,128)(2,1)}, bf16[528,256]{1,0:T(8,128)(2,1)S(1)}, u32[]{:S(2)}, u32[]{:S(2)}) %collective-permute-start.13) | collective-permute-done | bytes 270368 | tf_op jit(solution)/shard_map/h_ctx/ppermute | solution.py:134
  166.0 3.0 %collective-permute-done.15.refs_3_ = bf16[528,256]{1,0:T(8,128)(2,1)} collective-permute-done((bf16[528,256]{1,0:T(8,128)(2,1)}, bf16[528,256]{1,0:T(8,128)(2,1)}, u32[]{:S(2)}, u32[]{:S(2)}) %collective-permute-start.15) | collective-permute-done | bytes 270368 | tf_op jit(solution)/shard_map/h_diag/ppermute | solution.py:134
  169.0 3.3 %maximum_select_fusion.1.refs_10_ = bf16[2,2,2,448,256]{4,3,2,1,0:T(8,128)(2,1)} fusion(bf16[1,2,2,448,256]{4,3,2,1,0:T(8,128)(2,1)} %bitcast.18, bf16[1,2,2,448,256]{4,3,2,1,0:T(8,128)(2,1)} %bitcast.17, bf16[1,2,2,448,256]{4,3,2,1,0:T(8,128)(2,1)S(1)} %bitcast.25, pred[]{:T(512)S(6)} %eq.16), kind=kLoop, calls=%fused_computation.5 | loop fusion | flops 2752512 | bytes 4587521 | tf_op jit(solution)/shard_map/jit(_where)/select_n | solution.py:558
  172.4 2.5 %collective-permute-start.25 = (bf16[2,2,2,448,256]{4,3,2,1,0:T(8,128)(2,1)}, bf16[2,2,2,448,256]{4,3,2,1,0:T(8,128)(2,1)}, u32[]{:S(2)}, u32[]{:S(2)}) collective-permute-start(bf16[2,2,2,448,256]{4,3,2,1,0:T(8,128)(2,1)} %maximum_select_fusion.1.refs_10_), channel_id=1, source_target_pairs={{0,4},{1,5},{6,2},{7,3},{8,12},{9,13},{14,10},{15,11},{16,20},{17,... | collective-permute-start | bytes 5505032 | tf_op jit(solution)/shard_map/far_core/ppermute | solution.py:134
  175.5 2.3 %collective-permute-done.16.refs_4_ = bf16[528,256]{1,0:T(8,128)(2,1)S(1)} collective-permute-done((bf16[528,256]{1,0:T(8,128)(2,1)S(1)}, bf16[528,256]{1,0:T(8,128)(2,1)S(1)}, u32[]{:S(2)}, u32[]{:S(2)}) %collective-permute-start.16) | collective-permute-done | bytes 270368 | tf_op jit(solution)/shard_map/h_core/ppermute | solution.py:134
  180.3 8.6 %combine.1 = (bf16[2,256,896]{2,1,0:T(8,128)(2,1)}, bf16[4,2,896]{2,1,0:T(2,128)(2,1)}) custom-call(s32[2]{0:T(128)} %pad_add_fusion.scalars, bf16[528,256]{1,0:T(8,128)(2,1)} %get-tuple-element.40.refs_0_, bf16[528,256]{1,0:T(8,128)(2,1)} %copy-done.7, bf16[528,256]{1,0:T(8,128)(2,1)} %collective-permute-done.14.refs_2_, ...), custom_call_target="tpu_custom_call" | custom-call | tf_op jit(solution)/shard_map/combine/pallas_call | solution.py:464
  (70 shorter events, 20.8 us)
Async XLA Ops:
  0.6 136.1 %copy-start = (f32[4,128]{1,0:T(4,128)S(1)}, f32[4,128]{1,0:T(4,128)}, u32[]{:S(2)}) copy-start(f32[4,128]{1,0:T(4,128)} %param.15) | copy-start | bytes 6148
  4.8 18.7 %collective-permute-start = (bf16[3,448,256]{2,1,0:T(8,128)(2,1)}, bf16[3,448,256]{2,1,0:T(8,128)(2,1)}, u32[]{:S(2)}, u32[]{:S(2)}) collective-permute-start(bf16[3,448,256]{2,1,0:T(8,128)(2,1)} %get-tuple-element.24), channel_id=1, source_target_pairs={{0,16},{1,17},{2,18},{3,19},{4,20},{5,21},{6,22},{7,23},{8,24},{9,... | collective-permute-start | bytes 2064392 | tf_op jit(solution)/shard_map/pre_w/ppermute | solution.py:134
  7.8 26.9 %collective-permute-start.2 = (bf16[5,448,256]{2,1,0:T(8,128)(2,1)}, bf16[5,448,256]{2,1,0:T(8,128)(2,1)S(1)}, u32[]{:S(2)}, u32[]{:S(2)}) collective-permute-start(bf16[5,448,256]{2,1,0:T(8,128)(2,1)} %get-tuple-element.30.refs_5_), channel_id=1, source_target_pairs={{0,1},{1,0},{2,3},{3,2},{4,5},{5,4},{6,7},{7,6},{8,9},{9,8},{10,11... | collective-permute-start | bytes 3440648 | tf_op jit(solution)/shard_map/pair_kept/ppermute | solution.py:134
  9.3 25.4 %collective-permute-start.3 = (bf16[5,448,256]{2,1,0:T(8,128)(2,1)}, bf16[5,448,256]{2,1,0:T(8,128)(2,1)}, u32[]{:S(2)}, u32[]{:S(2)}) collective-permute-start(bf16[5,448,256]{2,1,0:T(8,128)(2,1)} %get-tuple-element.30.refs_5_), channel_id=1, source_target_pairs={{1,2},{2,1},{5,6},{6,5},{9,10},{10,9},{13,14},{14,13},{17,18},{18,... | collective-permute-start | bytes 3440648 | tf_op jit(solution)/shard_map/mid1_kept/ppermute | solution.py:134
  23.5 56.3 %collective-permute-start.1 = (bf16[4,256,896]{2,1,0:T(8,128)(2,1)}, bf16[4,256,896]{2,1,0:T(8,128)(2,1)S(1)}, u32[]{:S(2)}, u32[]{:S(2)}) collective-permute-start(bf16[4,256,896]{2,1,0:T(8,128)(2,1)} %constant_dynamic-slice_fusion.1), channel_id=1, source_target_pairs={{0,16},{1,17},{2,18},{3,19},{4,20},{5,21},{6,22},{7,23},{8,24},{9,... | collective-permute-start | bytes 5505032 | tf_op jit(solution)/shard_map/x_ctx/ppermute | solution.py:134
  34.7 17.5 %copy-start.5 = (bf16[5,448,256]{2,1,0:T(8,128)(2,1)}, bf16[5,448,256]{2,1,0:T(8,128)(2,1)S(1)}, u32[]{:S(2)}) copy-start(bf16[5,448,256]{2,1,0:T(8,128)(2,1)S(1)} %collective-permute-done.2.refs_6_) | copy-start | bytes 3440644
  34.7 45.1 %collective-permute-start.5 = (bf16[5,448,256]{2,1,0:T(8,128)(2,1)}, bf16[5,448,256]{2,1,0:T(8,128)(2,1)}, u32[]{:S(2)}, u32[]{:S(2)}) collective-permute-start(bf16[5,448,256]{2,1,0:T(8,128)(2,1)} %collective-permute-done.3), channel_id=1, source_target_pairs={{1,0},{2,3},{5,4},{6,7},{9,8},{10,11},{13,12},{14,15},{17,16},{18,... | collective-permute-start | bytes 3440648 | tf_op jit(solution)/shard_map/end1_kept/ppermute | solution.py:134
  36.0 43.8 %collective-permute-start.4 = (bf16[5,448,256]{2,1,0:T(8,128)(2,1)S(1)}, bf16[5,448,256]{2,1,0:T(8,128)(2,1)}, u32[]{:S(2)}, u32[]{:S(2)}) collective-permute-start(bf16[5,448,256]{2,1,0:T(8,128)(2,1)S(1)} %collective-permute-done.2.refs_6_), channel_id=1, source_target_pairs={{1,2},{2,1},{5,6},{6,5},{9,10},{10,9},{13,14},{14,13},{17,18},{18,... | collective-permute-start | bytes 3440648 | tf_op jit(solution)/shard_map/mid2_kept/ppermute | solution.py:134
  39.3 40.5 %collective-permute-start.6 = (bf16[3,448,256]{2,1,0:T(8,128)(2,1)}, bf16[3,448,256]{2,1,0:T(8,128)(2,1)}, u32[]{:S(2)}, u32[]{:S(2)}) collective-permute-start(bf16[3,448,256]{2,1,0:T(8,128)(2,1)} %collective-permute-done.refs_7_), channel_id=1, source_target_pairs={{0,1},{1,0},{2,3},{3,2},{4,5},{5,4},{6,7},{7,6},{8,9},{9,8},{10,11... | collective-permute-start | bytes 2064392 | tf_op jit(solution)/shard_map/pair_other/ppermute | solution.py:134
  46.9 32.9 %collective-permute-start.7 = (bf16[3,448,256]{2,1,0:T(8,128)(2,1)}, bf16[3,448,256]{2,1,0:T(8,128)(2,1)}, u32[]{:S(2)}, u32[]{:S(2)}) collective-permute-start(bf16[3,448,256]{2,1,0:T(8,128)(2,1)} %collective-permute-done.refs_7_), channel_id=1, source_target_pairs={{1,2},{2,1},{5,6},{6,5},{9,10},{10,9},{13,14},{14,13},{17,18},{18,... | collective-permute-start | bytes 2064392 | tf_op jit(solution)/shard_map/mid1_other/ppermute | solution.py:134
  79.8 10.6 %copy-start.1 = (bf16[4,256,896]{2,1,0:T(8,128)(2,1)}, bf16[4,256,896]{2,1,0:T(8,128)(2,1)S(1)}, u32[]{:S(2)}) copy-start(bf16[4,256,896]{2,1,0:T(8,128)(2,1)S(1)} %collective-permute-done.1.refs_2_) | copy-start | bytes 5505028
  79.8 5.6 %collective-permute-start.8 = (bf16[4,256,896]{2,1,0:T(8,128)(2,1)S(1)}, bf16[4,256,896]{2,1,0:T(8,128)(2,1)}, u32[]{:S(2)}, u32[]{:S(2)}) collective-permute-start(bf16[4,256,896]{2,1,0:T(8,128)(2,1)S(1)} %collective-permute-done.1.refs_2_), channel_id=1, source_target_pairs={{0,4},{1,5},{2,6},{3,7},{4,0},{5,1},{6,2},{7,3},{8,12},{9,13},{10,... | collective-permute-start | bytes 5505032 | tf_op jit(solution)/shard_map/x_core/ppermute | solution.py:134
  79.9 46.7 %collective-permute-start.9 = (bf16[5,448,256]{2,1,0:T(8,128)(2,1)}, bf16[5,448,256]{2,1,0:T(8,128)(2,1)S(1)}, u32[]{:S(2)}, u32[]{:S(2)}) collective-permute-start(bf16[5,448,256]{2,1,0:T(8,128)(2,1)} %collective-permute-done.4), channel_id=1, source_target_pairs={{1,0},{2,3},{5,4},{6,7},{9,8},{10,11},{13,12},{14,15},{17,16},{18,... | collective-permute-start | bytes 3440648 | tf_op jit(solution)/shard_map/end2_kept/ppermute | solution.py:134
  81.2 45.4 %collective-permute-start.11 = (bf16[3,448,256]{2,1,0:T(8,128)(2,1)}, bf16[3,448,256]{2,1,0:T(8,128)(2,1)}, u32[]{:S(2)}, u32[]{:S(2)}) collective-permute-start(bf16[3,448,256]{2,1,0:T(8,128)(2,1)} %collective-permute-done.7), channel_id=1, source_target_pairs={{1,0},{2,3},{5,4},{6,7},{9,8},{10,11},{13,12},{14,15},{17,16},{18,... | collective-permute-start | bytes 2064392 | tf_op jit(solution)/shard_map/end1_other/ppermute | solution.py:134
  82.5 44.1 %collective-permute-start.10 = (bf16[3,448,256]{2,1,0:T(8,128)(2,1)}, bf16[3,448,256]{2,1,0:T(8,128)(2,1)}, u32[]{:S(2)}, u32[]{:S(2)}) collective-permute-start(bf16[3,448,256]{2,1,0:T(8,128)(2,1)} %collective-permute-done.6.refs_8_), channel_id=1, source_target_pairs={{1,2},{2,1},{5,6},{6,5},{9,10},{10,9},{13,14},{14,13},{17,18},{18,... | collective-permute-start | bytes 2064392 | tf_op jit(solution)/shard_map/mid2_other/ppermute | solution.py:134
  85.4 43.8 %collective-permute-start.21 = (bf16[2,2,448,256]{3,2,1,0:T(8,128)(2,1)}, bf16[2,2,448,256]{3,2,1,0:T(8,128)(2,1)}, u32[]{:S(2)}, u32[]{:S(2)}) collective-permute-start(bf16[2,2,448,256]{3,2,1,0:T(8,128)(2,1)} %pad_maximum_fusion), channel_id=1, source_target_pairs={{8,16},{9,17},{10,18},{11,19},{12,20},{13,21},{14,22},{15,23},{16,... | collective-permute-start | bytes 2752520 | tf_op jit(solution)/shard_map/near_corner/ppermute | solution.py:134
  87.1 42.2 %collective-permute-start.20 = (bf16[2,2,448,256]{3,2,1,0:T(8,128)(2,1)}, bf16[2,2,448,256]{3,2,1,0:T(8,128)(2,1)}, u32[]{:S(2)}, u32[]{:S(2)}) collective-permute-start(bf16[2,2,448,256]{3,2,1,0:T(8,128)(2,1)} %pad_maximum_fusion), channel_id=1, source_target_pairs={{0,16},{1,17},{2,18},{3,19},{4,20},{5,21},{6,22},{7,23},{8,0},{9,1... | collective-permute-start | bytes 2752520 | tf_op jit(solution)/shard_map/near_meet/ppermute | solution.py:134
  126.6 20.0 %collective-permute-start.12 = (bf16[3,448,256]{2,1,0:T(8,128)(2,1)}, bf16[3,448,256]{2,1,0:T(8,128)(2,1)}, u32[]{:S(2)}, u32[]{:S(2)}) collective-permute-start(bf16[3,448,256]{2,1,0:T(8,128)(2,1)} %collective-permute-done.10.refs_6_), channel_id=1, source_target_pairs={{1,0},{2,3},{5,4},{6,7},{9,8},{10,11},{13,12},{14,15},{17,16},{18,... | collective-permute-start | bytes 2064392 | tf_op jit(solution)/shard_map/end2_other/ppermute | solution.py:134
  131.6 33.1 %copy-start.2 = (bf16[2,2,2,448,256]{4,3,2,1,0:T(8,128)(2,1)}, bf16[2,2,2,448,256]{4,3,2,1,0:T(8,128)(2,1)S(1)}, u32[]{:S(2)}) copy-start(bf16[2,2,2,448,256]{4,3,2,1,0:T(8,128)(2,1)S(1)} %maximum_select_fusion.refs_8_) | copy-start | bytes 5505028
  131.6 37.4 %collective-permute-start.24 = (bf16[2,2,448,256]{3,2,1,0:T(8,128)(2,1)}, bf16[2,2,448,256]{3,2,1,0:T(8,128)(2,1)S(1)}, u32[]{:S(2)}, u32[]{:S(2)}) collective-permute-start(bf16[2,2,448,256]{3,2,1,0:T(8,128)(2,1)} %pad_maximum_fusion.1), channel_id=1, source_target_pairs={{8,16},{9,17},{10,18},{11,19},{12,20},{13,21},{14,22},{15,23},{16,... | collective-permute-start | bytes 2752520 | tf_op jit(solution)/shard_map/far_corner/ppermute | solution.py:134
  132.3 36.7 %collective-permute-start.23 = (bf16[2,2,448,256]{3,2,1,0:T(8,128)(2,1)}, bf16[2,2,448,256]{3,2,1,0:T(8,128)(2,1)}, u32[]{:S(2)}, u32[]{:S(2)}) collective-permute-start(bf16[2,2,448,256]{3,2,1,0:T(8,128)(2,1)} %pad_maximum_fusion.1), channel_id=1, source_target_pairs={{0,16},{1,17},{2,18},{3,19},{4,20},{5,21},{6,22},{7,23},{8,0},{9,1... | collective-permute-start | bytes 2752520 | tf_op jit(solution)/shard_map/far_meet/ppermute | solution.py:134
  155.0 9.6 %collective-permute-start.13 = (bf16[528,256]{1,0:T(8,128)(2,1)}, bf16[528,256]{1,0:T(8,128)(2,1)S(1)}, u32[]{:S(2)}, u32[]{:S(2)}) collective-permute-start(bf16[528,256]{1,0:T(8,128)(2,1)} %get-tuple-element.41), channel_id=1, source_target_pairs={{0,16},{1,17},{2,18},{3,19},{4,20},{5,21},{6,22},{7,23},{8,24},{9,... | collective-permute-start | bytes 811016 | tf_op jit(solution)/shard_map/h_ctx/ppermute | solution.py:134
  155.0 10.9 %collective-permute-start.14 = (bf16[528,256]{1,0:T(8,128)(2,1)}, bf16[528,256]{1,0:T(8,128)(2,1)}, u32[]{:S(2)}, u32[]{:S(2)}) collective-permute-start(bf16[528,256]{1,0:T(8,128)(2,1)} %get-tuple-element.40.refs_0_), channel_id=1, source_target_pairs={{0,8},{1,9},{2,10},{3,11},{4,12},{5,13},{6,14},{7,15},{8,0},{9,1},... | collective-permute-start | bytes 811016 | tf_op jit(solution)/shard_map/h_y/ppermute | solution.py:134
  156.5 12.5 %collective-permute-start.15 = (bf16[528,256]{1,0:T(8,128)(2,1)}, bf16[528,256]{1,0:T(8,128)(2,1)}, u32[]{:S(2)}, u32[]{:S(2)}) collective-permute-start(bf16[528,256]{1,0:T(8,128)(2,1)} %get-tuple-element.41), channel_id=1, source_target_pairs={{0,24},{1,25},{2,26},{3,27},{4,28},{5,29},{6,30},{7,31},{8,16},{9,... | collective-permute-start | bytes 811016 | tf_op jit(solution)/shard_map/h_diag/ppermute | solution.py:134
  164.7 10.3 %copy-start.7 = (bf16[528,256]{1,0:T(8,128)(2,1)}, bf16[528,256]{1,0:T(8,128)(2,1)S(1)}, u32[]{:S(2)}) copy-start(bf16[528,256]{1,0:T(8,128)(2,1)S(1)} %collective-permute-done.13.refs_1_) | copy-start | bytes 811012
  164.7 14.9 %collective-permute-start.22 = (bf16[2,2,2,448,256]{4,3,2,1,0:T(8,128)(2,1)S(1)}, bf16[2,2,2,448,256]{4,3,2,1,0:T(8,128)(2,1)}, u32[]{:S(2)}, u32[]{:S(2)}) collective-permute-start(bf16[2,2,2,448,256]{4,3,2,1,0:T(8,128)(2,1)S(1)} %maximum_select_fusion.refs_8_), channel_id=1, source_target_pairs={{2,6},{3,7},{4,0},{5,1},{10,14},{11,15},{12,8},{13,9},{18,22},{19,... | collective-permute-start | bytes 5505032 | tf_op jit(solution)/shard_map/near_core/ppermute | solution.py:134
  169.0 5.9 %copy-start.6 = (bf16[528,256]{1,0:T(8,128)(2,1)S(1)}, bf16[528,256]{1,0:T(8,128)(2,1)}, u32[]{:S(2)}) copy-start(bf16[528,256]{1,0:T(8,128)(2,1)} %get-tuple-element.40.refs_0_) | copy-start | bytes 811012
  172.4 7.2 %collective-permute-start.25 = (bf16[2,2,2,448,256]{4,3,2,1,0:T(8,128)(2,1)}, bf16[2,2,2,448,256]{4,3,2,1,0:T(8,128)(2,1)}, u32[]{:S(2)}, u32[]{:S(2)}) collective-permute-start(bf16[2,2,2,448,256]{4,3,2,1,0:T(8,128)(2,1)} %maximum_select_fusion.1.refs_10_), channel_id=1, source_target_pairs={{0,4},{1,5},{6,2},{7,3},{8,12},{9,13},{14,10},{15,11},{16,20},{17,... | collective-permute-start | bytes 5505032 | tf_op jit(solution)/shard_map/far_core/ppermute | solution.py:134
  174.9 2.9 %collective-permute-start.16 = (bf16[528,256]{1,0:T(8,128)(2,1)S(1)}, bf16[528,256]{1,0:T(8,128)(2,1)S(1)}, u32[]{:S(2)}, u32[]{:S(2)}) collective-permute-start(bf16[528,256]{1,0:T(8,128)(2,1)S(1)} %copy-done.6), channel_id=1, source_target_pairs={{0,4},{1,5},{2,6},{3,7},{4,0},{5,1},{6,2},{7,3},{8,12},{9,13},{10,... | collective-permute-start | bytes 811016 | tf_op jit(solution)/shard_map/h_core/ppermute | solution.py:134
  174.9 3.9 %collective-permute-start.17 = (bf16[528,256]{1,0:T(8,128)(2,1)S(1)}, bf16[528,256]{1,0:T(8,128)(2,1)S(1)}, u32[]{:S(2)}, u32[]{:S(2)}) collective-permute-start(bf16[528,256]{1,0:T(8,128)(2,1)S(1)} %collective-permute-done.13.refs_1_), channel_id=1, source_target_pairs={{0,4},{1,5},{2,6},{3,7},{4,0},{5,1},{6,2},{7,3},{8,12},{9,13},{10,... | collective-permute-start | bytes 811016 | tf_op jit(solution)/shard_map/h_core/ppermute | solution.py:134
  175.4 3.4 %collective-permute-start.18 = (bf16[528,256]{1,0:T(8,128)(2,1)}, bf16[528,256]{1,0:T(8,128)(2,1)S(1)}, u32[]{:S(2)}, u32[]{:S(2)}) collective-permute-start(bf16[528,256]{1,0:T(8,128)(2,1)} %collective-permute-done.14.refs_2_), channel_id=1, source_target_pairs={{0,4},{1,5},{2,6},{3,7},{4,0},{5,1},{6,2},{7,3},{8,12},{9,13},{10,... | collective-permute-start | bytes 811016 | tf_op jit(solution)/shard_map/h_core/ppermute | solution.py:134
  177.8 1.8 collective-permute-start.19
  (6 other events, 12.5 us)

commit v3 on v2

--- a/solution.py
+++ b/solution.py
@@ -111,7 +111,7 @@
 
 
 AXES = ("ctx", "tp", "rep")
-VMEM_LIMIT = 60 * 1024 * 1024
+VMEM_LIMIT = 24 * 1024 * 1024
 DEC_PAD = 16
 
 
@@ -412,9 +412,44 @@
     )(scalars, *xs, *mine, *other, summed, prior, gain, lengths)
 
 
+def arrange_kernel(scalars, *refs):
+    groups, out_ref, sems = (refs[:3], refs[3:6]), refs[6], refs[7]
+
+    def copy(half, source):
+        return pltpu.make_async_copy(source, out_ref.at[half], sems.at[half])
+
+    for near in range(2):
+        for same in range(2):
+
+            @pl.when((scalars[1] == near) & (scalars[2] == same))
+            def _(near=near, same=same):
+                for half in range(2):
+                    copy(half, groups[near][half + 1 - same]).start()
+
+    for half in range(2):
+        copy(half, groups[0][0]).wait()
+
+
+def arrange(scalars, *blocks):
+    shape = (2, *blocks[0].shape)
+    return pl.pallas_call(
+        arrange_kernel,
+        grid_spec=pltpu.PrefetchScalarGridSpec(
+            num_scalar_prefetch=1,
+            grid=(1,),
+            in_specs=[pl.BlockSpec(memory_space=pl.ANY)] * 6,
+            out_specs=whole(shape),
+            scratch_shapes=[pltpu.SemaphoreType.DMA((2,))],
+        ),
+        out_shape=jax.ShapeDtypeStruct(shape, jnp.bfloat16),
+        compiler_params=params(),
+        name="arrange",
+    )(scalars, *blocks)
+
+
 def combine_kernel(scalars, *refs):
-    hidden, blocks = refs[:8], refs[8:12]
-    res_ref, dec_res_ref, out_ref, dec_ref, rows, weights, hidden_sems, weight_sems = refs[12:]
+    hidden, groups, passed = refs[:8], (refs[8:11], refs[11:14]), refs[14]
+    res_ref, dec_res_ref, out_ref, dec_ref, rows, weights, hidden_sems, weight_sems = refs[15:]
     wide = hidden[0].shape[1]
 
     def hidden_copy(i, j):
@@ -423,8 +458,7 @@
         source = hidden[4 * (i % 2) + 2 * (i // 2) + j]
         return pltpu.make_async_copy(source, rows.at[:, at], hidden_sems.at[i, j])
 
-    def weight_copy(i, slot, part, plane):
-        source = blocks[2 * (plane // 2) + i % 2].at[i // 2, plane % 2, part]
+    def weight_copy(i, slot, part, source):
         at = pl.ds((2 * i + part) * wide, wide)
         return pltpu.make_async_copy(source, weights.at[slot, :, at], weight_sems.at[i, slot, part])
 
@@ -432,12 +466,15 @@
     for i in range(4):
         for j in range(2):
             hidden_copy(i, j).start()
-    for chosen, planes in enumerate(((0, 1), (1, 0), (2, 3), (3, 2))):
-
-        @pl.when(scalars[1] == chosen)
-        def _(planes=planes):
-            for i, slot, part in every:
-                weight_copy(i, slot, part, planes[slot]).start()
+    for near in range(2):
+        for same in range(2):
+
+            @pl.when((scalars[1] == near) & (scalars[2] == same))
+            def _(near=near, same=same):
+                for i, slot, part in every:
+                    source = passed.at[i // 2] if i % 2 else groups[1 - near][i // 2 + 1 - same]
+                    plane = jnp.bitwise_xor(scalars[3], slot)
+                    weight_copy(i, slot, part, source.at[plane, part]).start()
 
     for i in range(4):
         for j in range(2):
@@ -446,7 +483,7 @@
     for slot in range(2):
         for i, at, part in every:
             if at == slot:
-                weight_copy(i, slot, part, 0).wait()
+                weight_copy(i, slot, part, passed.at[0, 0, 0]).wait()
         total.append(
             lax.dot_general(rows[...], weights[slot], (((1,), (1,)), ((), ())), preferred_element_type=jnp.float32)
         )
@@ -471,7 +508,7 @@
             out_specs=[whole(res.shape), whole(dec_res.shape)],
             scratch_shapes=[
                 pltpu.VMEM((hidden[0].shape[0], 8 * hidden[0].shape[1]), jnp.bfloat16),
-                pltpu.VMEM((2, blocks[0].shape[3], 8 * blocks[0].shape[4]), jnp.bfloat16),
+                pltpu.VMEM((2, blocks[0].shape[2], 8 * blocks[0].shape[3]), jnp.bfloat16),
                 pltpu.SemaphoreType.DMA((4, 2)),
                 pltpu.SemaphoreType.DMA((4, 2, 2)),
             ],
@@ -508,12 +545,6 @@
     def corner(c, t, r):
         return None if c == t // 2 else (1 - c, t ^ 2, r)
 
-    def near_pass(c, t, r):
-        return None if t % 2 == r // 2 else (c, t ^ 1, r)
-
-    def far_pass(c, t, r):
-        return (c, t ^ 1, r) if t % 2 == r // 2 else None
-
     kept, given = split(scalars, qkv_weight, out_weight.T)
     pair_kept = move(kept, to_pair, "pair_kept")
     mid1_kept = move(kept, mid_swap, "mid1_kept")
@@ -532,18 +563,9 @@
     mid1_other = move(after(other, *stage), mid_swap, "mid1_other")
     dec_x = embed_steps(after(dec_spikes, *stage), thresholds, in_scale, planes)
 
-    columns = width // lax.axis_size("tp")
-
-    def gate(rows):
-        part = lax.dynamic_slice_in_dim(rows, t * columns, columns, 2)
-        level = lax.dynamic_slice_in_dim(thresholds, t * columns, columns, 0)
-        scale = lax.dynamic_slice_in_dim(in_scale, t * columns, columns, 0)
-        return (jnp.where(part >= level, part, 0).astype(jnp.float32) * scale).astype(jnp.bfloat16)
-
-    res, dec_res = gate(after(spikes, *stage)), gate(after(dec_spikes, *stage))
     near_blocks = jnp.stack([after(kept, *stage)[3:], pair_kept[3:]])
 
-    stage = (mid2_kept, end1_kept, pair_other, mid1_other, first_x, near_blocks, dec_x, res, dec_res)
+    stage = (mid2_kept, end1_kept, pair_other, mid1_other, first_x, near_blocks, dec_x)
     end2_kept = move(after(mid2_kept, *stage), mid_to_end, "end2_kept")
     mid2_other = move(after(pair_other, *stage), mid_swap, "mid2_other")
     end1_other = move(after(mid1_other, *stage), mid_to_end, "end1_other")
@@ -554,20 +576,24 @@
     def carry(blocks, name):
         return blocks, move(blocks, meet, name + "_meet"), move(blocks, corner, name + "_corner")
 
-    def place_out(blocks, met, far, passing, name):
-        own = jnp.where(c == y, jnp.stack([blocks, met]), jnp.stack([met, far]))
-        return own, move(own, passing, name + "_core")
-
     third_kept = jnp.where(is_end, end1_kept, mid1_kept)
     near = carry(after(near_blocks, second_x, third_kept), "near")
 
-    stage = (mid2_other, end1_other, summed)
+    columns = width // lax.axis_size("tp")
+
+    def gate(rows):
+        part = lax.dynamic_slice_in_dim(rows, t * columns, columns, 2)
+        level = lax.dynamic_slice_in_dim(thresholds, t * columns, columns, 0)
+        scale = lax.dynamic_slice_in_dim(in_scale, t * columns, columns, 0)
+        return (jnp.where(part >= level, part, 0).astype(jnp.float32) * scale).astype(jnp.bfloat16)
+
+    res, dec_res = gate(after(spikes, second_x)), gate(after(dec_spikes, second_x))
+    stage = (mid2_other, end1_other, summed, res, dec_res)
     end2_other = move(after(mid2_other, *stage), mid_to_end, "end2_other")
-    near = place_out(near[0], near[1], after(near[2], summed), near_pass, "near")
     third_other = jnp.where(is_end, after(end1_other, *stage), mid1_other)
     summed = project(scalars, 2, xs, (third_kept,), (third_other,), summed)
     fourth_kept = jnp.where(is_end, after(end2_kept, *stage), mid2_kept)
-    far = carry(after(jnp.stack([third_kept[3:], fourth_kept[3:]]), near[0]), "far")
+    far = carry(after(jnp.stack([third_kept[3:], fourth_kept[3:]]), near[1], near[2]), "far")
     gain = lax.dynamic_slice_in_dim(head_gain, c * heads, heads, 0)
 
     dims = (groups, block, heads, head, steps)
@@ -578,13 +604,13 @@
     h_y = move(own_rows, to_y, "h_y")
     h_diag = move(far_rows, to_diagonal, "h_diag")
     mine = [own_rows, h_ctx, h_y, h_diag]
-    far = place_out(far[0], far[1], after(far[2], h_ctx, h_y, h_diag), far_pass, "far")
-    hidden = mine + [move(m, to_core, "h_core") for m in mine]
-
-    near_first = z & 1
-    far_first = 2 + (z >> 1)
-    flags = jnp.stack([c, jnp.where((z >> 1) == parity, near_first, far_first)]).astype(jnp.int32)
-    return combine(flags, hidden, near + far, res, dec_res)
+    near_used = (z >> 1) == parity
+    flags = jnp.stack([c, near_used, c == y, jnp.where(near_used, z & 1, z >> 1)]).astype(jnp.int32)
+    passed = arrange(flags, *near, far[0], far[1], after(far[2], own_rows))
+    blocks = (*near, *far, move(passed, to_core, "out_core"))
+    hidden = mine + [move(m, to_core, "h_core") for m in (after(own_rows, h_ctx), h_ctx, h_y, h_diag)]
+
+    return combine(flags, hidden, blocks, res, dec_res)
 
 
 def solution(mesh):

time: 193 us -> 186 us (0.964)
  Pallas kernels: 46 us -> 25.9 us
  waiting for transfers between devices: 74.5 us -> 92.8 us
  local copies, waits for them, and re-layouts: 7.55 us -> 17.8 us
  starting transfers between devices: 43.9 us -> 36.9 us
  other arithmetic: 16.1 us -> 9.44 us
    ppermute x26 -> x25, waiting for transfers between devices: 74.5 us -> 92.8 us  [move(): return lax.ppermute(value, AXES, pairs)]
    unnamed x24 -> x56, local copies, waits for them, and re-layouts: 0.72 us -> 16.2 us
    ppermute x26 -> x25, starting transfers between devices: 43.9 us -> 36.9 us  [move(): return lax.ppermute(value, AXES, pairs)]
    pallas_call x2, Pallas kernels: 16 us -> 9.72 us  [project(): pl.pallas_call(lambda *refs: project_kernel(steps, bool(earlier), *refs),...]
    pallas_call x1, Pallas kernels: 7.75 us -> 1.86 us  [embed(): pl.pallas_call(lambda *refs: embed_kernel(parts, *refs), grid=(rows // ti...]
    select_n x2 -> x0, other arithmetic: 5.67 us -> none  [place_out(): own = jnp.where(c == y, jnp.stack([blocks, met]), jnp.stack([met, far]))]
    pallas_call x1, Pallas kernels: 8.61 us -> 5.4 us  [combine(): pl.pallas_call(combine_kernel, grid_spec=pltpu.PrefetchScalarGridSpec(num...]
    pallas_call x1, Pallas kernels: 3.49 us -> 0.66 us  [split(): pl.pallas_call(split_kernel, grid_spec=pltpu.PrefetchScalarGridSpec(num_s...]
  transfers between devices with their start and end apart: 26 -> 25, of which waited for: 8 -> 9; matrix products, arithmetic and copies ran while one was open for 12% -> 6% of each run, Pallas kernels for 18% -> 10%
where the time goes in v3:
time: 186 us; the launch traced here: 184 us
  waiting for transfers between devices  92.8 us (50%)
  starting transfers between devices  36.9 us (20%)
  Pallas kernels  25.9 us (14%)
  local copies, waits for them, and re-layouts  17.8 us (10%)
  other arithmetic  9.44 us (5%)
    ppermute x25, waiting for transfers between devices, move(): return lax.ppermute(value, AXES, pairs)  92.8 us
    ppermute x25, starting transfers between devices, move(): return lax.ppermute(value, AXES, pairs)  36.9 us
    unnamed x56, local copies, waits for them, and re-layouts  16.2 us
    pallas_call x2, Pallas kernels, project(): pl.pallas_call(lambda *refs: project_kernel(steps, bool(earlier), *refs),...  9.72 us
    pallas_call x1, Pallas kernels, attend(): pl.pallas_call(lambda *refs: attend_kernel(dims, *refs), grid_spec=pltpu....  5.9 us
    pallas_call x1, Pallas kernels, combine(): pl.pallas_call(combine_kernel, grid_spec=pltpu.PrefetchScalarGridSpec(num...  5.4 us
    convert_element_type x2, other arithmetic, gate(): (jnp.where(part >= level, part, 0).astype(jnp.float32) * scale).astype(jn...  3.95 us
  transfers between devices with their start and end apart: 25, of which 9 were waited for; matrix products, arithmetic and copies ran while one was open for 6% of the time, Pallas kernels for 10%

profile of v3, /device:TPU:0, one launch (start us, length us, event | category | flops | bytes accessed | tf_op | source)
XLA Modules:
  0.0 183.9 jit_solution(4673273654216540125)
XLA Ops:
  0.8 1.3 copy-done.11
  3.8 3.0 %collective-permute-start = (bf16[3,448,256]{2,1,0:T(8,128)(2,1)S(1)}, bf16[3,448,256]{2,1,0:T(8,128)(2,1)}, u32[]{:S(2)}, u32[]{:S(2)}) collective-permute-start(bf16[3,448,256]{2,1,0:T(8,128)(2,1)S(1)} %get-tuple-element.25), channel_id=1, source_target_pairs={{0,16},{1,17},{2,18},{3,19},{4,20},{5,21},{6,22},{7,23},{8,24},{9,... | collective-permute-start | bytes 2064392 | tf_op jit(solution)/shard_map/pre_w/ppermute | solution.py:134
  6.8 1.6 collective-permute-start.2
  8.4 1.7 collective-permute-start.3
  10.1 3.1 %copy-done.6 = s32[2,256,3584]{2,1,0:T(8,128)S(1)} copy-done((s32[2,256,3584]{2,1,0:T(8,128)S(1)}, s32[2,256,3584]{2,1,0:T(8,128)}, u32[]{:S(2)}) %copy-start.6) | copy-done | bytes 7340056
  13.2 1.9 %embed.1.refs_1_ = bf16[4,512,896]{2,1,0:T(8,128)(2,1)S(1)} custom-call(s32[512,3584]{1,0:T(8,128)S(1)} %bitcast.20, s32[3584]{0:T(1024)S(1)} %copy-done.25, f32[3584]{0:T(1024)S(1)} %copy-done.24), custom_call_target="tpu_custom_call" | custom-call | tf_op jit(solution)/shard_map/embed/pallas_call | solution.py:242
  15.3 1.6 copy-done.1
  16.9 5.5 %collective-permute-done.refs_7_ = bf16[3,448,256]{2,1,0:T(8,128)(2,1)} collective-permute-done((bf16[3,448,256]{2,1,0:T(8,128)(2,1)S(1)}, bf16[3,448,256]{2,1,0:T(8,128)(2,1)}, u32[]{:S(2)}, u32[]{:S(2)}) %collective-permute-start) | collective-permute-done | bytes 688160 | tf_op jit(solution)/shard_map/pre_w/ppermute | solution.py:134
  22.4 1.7 collective-permute-start.1
  24.1 9.6 %collective-permute-done.2.refs_6_ = bf16[5,448,256]{2,1,0:T(8,128)(2,1)} collective-permute-done((bf16[5,448,256]{2,1,0:T(8,128)(2,1)S(1)}, bf16[5,448,256]{2,1,0:T(8,128)(2,1)}, u32[]{:S(2)}, u32[]{:S(2)}) %collective-permute-start.2) | collective-permute-done | bytes 1146912 | tf_op jit(solution)/shard_map/pair_kept/ppermute | solution.py:134
  33.6 1.7 collective-permute-start.4
  36.6 7.6 %collective-permute-start.6 = (bf16[3,448,256]{2,1,0:T(8,128)(2,1)}, bf16[3,448,256]{2,1,0:T(8,128)(2,1)S(1)}, u32[]{:S(2)}, u32[]{:S(2)}) collective-permute-start(bf16[3,448,256]{2,1,0:T(8,128)(2,1)} %collective-permute-done.refs_7_), channel_id=1, source_target_pairs={{0,1},{1,0},{2,3},{3,2},{4,5},{5,4},{6,7},{7,6},{8,9},{9,8},{10,11... | collective-permute-start | bytes 2064392 | tf_op jit(solution)/shard_map/pair_other/ppermute | solution.py:134
  44.2 1.5 collective-permute-start.7
  47.1 34.6 %collective-permute-done.6.refs_8_ = bf16[3,448,256]{2,1,0:T(8,128)(2,1)S(1)} collective-permute-done((bf16[3,448,256]{2,1,0:T(8,128)(2,1)}, bf16[3,448,256]{2,1,0:T(8,128)(2,1)S(1)}, u32[]{:S(2)}, u32[]{:S(2)}) %collective-permute-start.6) | collective-permute-done | bytes 688160 | tf_op jit(solution)/shard_map/pair_other/ppermute | solution.py:134
  83.9 1.5 broadcast_select_fusion.refs_5_
  85.5 1.5 collective-permute-start.10
  92.0 6.1 %project.2.refs_7_ = f32[1040,768]{1,0:T(8,128)S(1)} custom-call(s32[7]{0:T(128)S(1)} %stack.78.scalars.refs_0_, bf16[4,512,896]{2,1,0:T(8,128)(2,1)S(1)} %copy-done.2, bf16[4,256,896]{2,1,0:T(8,128)(2,1)S(1)} %collective-permute-done.1.refs_2_, bf16[4,256,896]{2,1,0:T(8,128)(2,1)} %collective-permute-done.8.refs_3_, ...), custom_call_target="tpu_custom_call" | custom-call | tf_op jit(solution)/shard_map/project/pallas_call | solution.py:301
  98.1 3.9 %fusion.2.refs_15_ = bf16[2,256,896]{2,1,0:T(8,128)(2,1)} fusion(s32[2,256,3584]{2,1,0:T(8,128)} %param.9, s32[]{:T(128)S(6)} %select_n.57, f32[896]{0:T(1024)S(1)} %dynamic_slice.23, s32[896]{0:T(1024)S(1)} %dynamic_slice.22), kind=kLoop, calls=%fused_computation.3 | loop fusion | flops 2293760 | bytes 2759684 | tf_op jit(solution)/shard_map/convert_element_type | solution.py:588
  102.1 24.9 %collective-permute-done.11 = bf16[3,448,256]{2,1,0:T(8,128)(2,1)S(1)} collective-permute-done((bf16[3,448,256]{2,1,0:T(8,128)(2,1)}, bf16[3,448,256]{2,1,0:T(8,128)(2,1)S(1)}, u32[]{:S(2)}, u32[]{:S(2)}) %collective-permute-start.11) | collective-permute-done | bytes 688160 | tf_op jit(solution)/shard_map/end1_other/ppermute | solution.py:134
  128.3 1.4 broadcast_select_fusion.1.refs_5_
  132.7 1.6 collective-permute-start.23
  134.4 3.3 %collective-permute-start.22 = (bf16[2,2,448,256]{3,2,1,0:T(8,128)(2,1)}, bf16[2,2,448,256]{3,2,1,0:T(8,128)(2,1)}, u32[]{:S(2)}, u32[]{:S(2)}) collective-permute-start(bf16[2,2,448,256]{3,2,1,0:T(8,128)(2,1)} %pad_maximum_fusion.1.refs_3_.refs_11_), channel_id=1, source_target_pairs={{0,16},{1,17},{2,18},{3,19},{4,20},{5,21},{6,22},{7,23},{8,0},{9,1... | collective-permute-start | bytes 2752520 | tf_op jit(solution)/shard_map/far_meet/ppermute | solution.py:134
  139.2 2.0 %copy-done.3 = bf16[4,512,896]{2,1,0:T(8,128)(2,1)S(1)} copy-done((bf16[4,512,896]{2,1,0:T(8,128)(2,1)S(1)}, bf16[4,512,896]{2,1,0:T(8,128)(2,1)}, u32[]{:S(2)}) %copy-start.3) | copy-done | bytes 3670040
  141.2 1.9 %copy-done.5 = f32[1040,768]{1,0:T(8,128)S(1)} copy-done((f32[1040,768]{1,0:T(8,128)S(1)}, f32[1040,768]{1,0:T(8,128)}, u32[]{:S(2)}) %copy-start.5) | copy-done | bytes 3194904
  143.1 3.6 %project.3.refs_8_ = f32[1040,768]{1,0:T(8,128)S(1)} custom-call(s32[7]{0:T(128)S(1)} %stack.78.scalars.refs_0_, bf16[4,512,896]{2,1,0:T(8,128)(2,1)S(1)} %copy-done.3, bf16[4,256,896]{2,1,0:T(8,128)(2,1)S(1)} %collective-permute-done.1.refs_2_, bf16[4,256,896]{2,1,0:T(8,128)(2,1)} %collective-permute-done.8.refs_3_, ...), custom_call_target="tpu_custom_call" | custom-call | tf_op jit(solution)/shard_map/project/pallas_call | solution.py:301
  146.7 5.9 %attend.1 = (bf16[528,256]{1,0:T(8,128)(2,1)S(1)}, bf16[528,256]{1,0:T(8,128)(2,1)S(1)}) custom-call(s32[7]{0:T(128)S(1)} %stack.78.scalars.refs_0_, bf16[4,512,896]{2,1,0:T(8,128)(2,1)S(1)} %copy-done.3, bf16[4,256,896]{2,1,0:T(8,128)(2,1)S(1)} %collective-permute-done.1.refs_2_, bf16[4,256,896]{2,1,0:T(8,128)(2,1)} %collective-permute-done.8.refs_3_, ...), custom_call_target="tpu_custom_call" | custom-call | flops 2862612480 | bytes 3194880 | tf_op jit(solution)/shard_map/attend/pallas_call | solution.py:397
  152.7 4.5 %collective-permute-done.22.refs_4_.refs_12_ = bf16[2,2,448,256]{3,2,1,0:T(8,128)(2,1)} collective-permute-done((bf16[2,2,448,256]{3,2,1,0:T(8,128)(2,1)}, bf16[2,2,448,256]{3,2,1,0:T(8,128)(2,1)}, u32[]{:S(2)}, u32[]{:S(2)}) %collective-permute-start.22) | collective-permute-done | bytes 917536 | tf_op jit(solution)/shard_map/far_meet/ppermute | solution.py:134
  157.2 2.2 %arrange.1 = bf16[2,2,2,448,256]{4,3,2,1,0:T(8,128)(2,1)S(1)} custom-call(s32[4]{0:T(128)S(1)} %pad_add_fusion.scalars, bf16[2,2,448,256]{3,2,1,0:T(8,128)(2,1)S(1)} %pad_maximum_fusion.refs_0_.refs_8_, bf16[2,2,448,256]{3,2,1,0:T(8,128)(2,1)S(1)} %copy-done.14, bf16[2,2,448,256]{3,2,1,0:T(8,128)(2,1)S(1)} %copy-done.16, ...), custom_call_target="tpu_custom_call" | custom-call | tf_op jit(solution)/shard_map/arrange/pallas_call | solution.py:435
  159.5 2.5 %collective-permute-start.13 = (bf16[528,256]{1,0:T(8,128)(2,1)S(1)}, bf16[528,256]{1,0:T(8,128)(2,1)S(1)}, u32[]{:S(2)}, u32[]{:S(2)}) collective-permute-start(bf16[528,256]{1,0:T(8,128)(2,1)S(1)} %get-tuple-element.43), channel_id=1, source_target_pairs={{0,16},{1,17},{2,18},{3,19},{4,20},{5,21},{6,22},{7,23},{8,24},{9,... | collective-permute-start | bytes 811016 | tf_op jit(solution)/shard_map/h_ctx/ppermute | solution.py:134
  163.6 5.8 %collective-permute-done.13.refs_1_ = bf16[528,256]{1,0:T(8,128)(2,1)S(1)} collective-permute-done((bf16[528,256]{1,0:T(8,128)(2,1)S(1)}, bf16[528,256]{1,0:T(8,128)(2,1)S(1)}, u32[]{:S(2)}, u32[]{:S(2)}) %collective-permute-start.13) | collective-permute-done | bytes 270368 | tf_op jit(solution)/shard_map/h_ctx/ppermute | solution.py:134
  169.9 6.5 %collective-permute-done.14.refs_2_ = bf16[528,256]{1,0:T(8,128)(2,1)S(1)} collective-permute-done((bf16[528,256]{1,0:T(8,128)(2,1)S(1)}, bf16[528,256]{1,0:T(8,128)(2,1)S(1)}, u32[]{:S(2)}, u32[]{:S(2)}) %collective-permute-start.14) | collective-permute-done | bytes 270368 | tf_op jit(solution)/shard_map/h_y/ppermute | solution.py:134
  178.4 5.4 %combine.1 = (bf16[2,256,896]{2,1,0:T(8,128)(2,1)}, bf16[4,2,896]{2,1,0:T(2,128)(2,1)}) custom-call(s32[4]{0:T(128)S(1)} %pad_add_fusion.scalars, bf16[528,256]{1,0:T(8,128)(2,1)S(1)} %get-tuple-element.44.refs_0_, bf16[528,256]{1,0:T(8,128)(2,1)S(1)} %collective-permute-done.13.refs_1_, bf16[528,256]{1,0:T(8,128)(2,1)S(1)} %collective-permute-done.14.refs_2_, ...), custom_call_target="tpu_custom_call" | custom-call | tf_op jit(solution)/shard_map/combine/pallas_call | solution.py:501
  (99 shorter events, 21.6 us)
Async XLA Ops:
  0.6 137.1 %copy-start = (f32[4,128]{1,0:T(4,128)S(1)}, f32[4,128]{1,0:T(4,128)}, u32[]{:S(2)}) copy-start(f32[4,128]{1,0:T(4,128)} %param.15) | copy-start | bytes 6148
  3.8 42.1 %copy-start.17 = (bf16[5,448,256]{2,1,0:T(8,128)(2,1)}, bf16[5,448,256]{2,1,0:T(8,128)(2,1)S(1)}, u32[]{:S(2)}) copy-start(bf16[5,448,256]{2,1,0:T(8,128)(2,1)S(1)} %get-tuple-element.31.refs_5_) | copy-start | bytes 3440644
  3.8 18.5 %collective-permute-start = (bf16[3,448,256]{2,1,0:T(8,128)(2,1)S(1)}, bf16[3,448,256]{2,1,0:T(8,128)(2,1)}, u32[]{:S(2)}, u32[]{:S(2)}) collective-permute-start(bf16[3,448,256]{2,1,0:T(8,128)(2,1)S(1)} %get-tuple-element.25), channel_id=1, source_target_pairs={{0,16},{1,17},{2,18},{3,19},{4,20},{5,21},{6,22},{7,23},{8,24},{9,... | collective-permute-start | bytes 2064392 | tf_op jit(solution)/shard_map/pre_w/ppermute | solution.py:134
  6.8 26.8 %collective-permute-start.2 = (bf16[5,448,256]{2,1,0:T(8,128)(2,1)S(1)}, bf16[5,448,256]{2,1,0:T(8,128)(2,1)}, u32[]{:S(2)}, u32[]{:S(2)}) collective-permute-start(bf16[5,448,256]{2,1,0:T(8,128)(2,1)S(1)} %get-tuple-element.31.refs_5_), channel_id=1, source_target_pairs={{0,1},{1,0},{2,3},{3,2},{4,5},{5,4},{6,7},{7,6},{8,9},{9,8},{10,11... | collective-permute-start | bytes 3440648 | tf_op jit(solution)/shard_map/pair_kept/ppermute | solution.py:134
  8.4 25.3 %collective-permute-start.3 = (bf16[5,448,256]{2,1,0:T(8,128)(2,1)S(1)}, bf16[5,448,256]{2,1,0:T(8,128)(2,1)}, u32[]{:S(2)}, u32[]{:S(2)}) collective-permute-start(bf16[5,448,256]{2,1,0:T(8,128)(2,1)S(1)} %get-tuple-element.31.refs_5_), channel_id=1, source_target_pairs={{1,2},{2,1},{5,6},{6,5},{9,10},{10,9},{13,14},{14,13},{17,18},{18,... | collective-permute-start | bytes 3440648 | tf_op jit(solution)/shard_map/mid1_kept/ppermute | solution.py:134
  15.1 30.6 %copy-start.23 = (s32[4,2,3584]{2,1,0:T(2,128)S(1)}, s32[4,2,3584]{2,1,0:T(2,128)}, u32[]{:S(2)}) copy-start(s32[4,2,3584]{2,1,0:T(2,128)} %refs_0_) | copy-start | bytes 344068
  22.4 59.3 %collective-permute-start.1 = (bf16[4,256,896]{2,1,0:T(8,128)(2,1)S(1)}, bf16[4,256,896]{2,1,0:T(8,128)(2,1)S(1)}, u32[]{:S(2)}, u32[]{:S(2)}) collective-permute-start(bf16[4,256,896]{2,1,0:T(8,128)(2,1)S(1)} %constant_dynamic-slice_fusion.1), channel_id=1, source_target_pairs={{0,16},{1,17},{2,18},{3,19},{4,20},{5,21},{6,22},{7,23},{8,24},{9,... | collective-permute-start | bytes 5505032 | tf_op jit(solution)/shard_map/x_ctx/ppermute | solution.py:134
  33.6 48.0 %collective-permute-start.4 = (bf16[5,448,256]{2,1,0:T(8,128)(2,1)}, bf16[5,448,256]{2,1,0:T(8,128)(2,1)}, u32[]{:S(2)}, u32[]{:S(2)}) collective-permute-start(bf16[5,448,256]{2,1,0:T(8,128)(2,1)} %collective-permute-done.2.refs_6_), channel_id=1, source_target_pairs={{1,2},{2,1},{5,6},{6,5},{9,10},{10,9},{13,14},{14,13},{17,18},{18,... | collective-permute-start | bytes 3440648 | tf_op jit(solution)/shard_map/mid2_kept/ppermute | solution.py:134
  35.3 46.3 %collective-permute-start.5 = (bf16[5,448,256]{2,1,0:T(8,128)(2,1)}, bf16[5,448,256]{2,1,0:T(8,128)(2,1)}, u32[]{:S(2)}, u32[]{:S(2)}) collective-permute-start(bf16[5,448,256]{2,1,0:T(8,128)(2,1)} %collective-permute-done.3), channel_id=1, source_target_pairs={{1,0},{2,3},{5,4},{6,7},{9,8},{10,11},{13,12},{14,15},{17,16},{18,... | collective-permute-start | bytes 3440648 | tf_op jit(solution)/shard_map/end1_kept/ppermute | solution.py:134
  36.6 45.0 %collective-permute-start.6 = (bf16[3,448,256]{2,1,0:T(8,128)(2,1)}, bf16[3,448,256]{2,1,0:T(8,128)(2,1)S(1)}, u32[]{:S(2)}, u32[]{:S(2)}) collective-permute-start(bf16[3,448,256]{2,1,0:T(8,128)(2,1)} %collective-permute-done.refs_7_), channel_id=1, source_target_pairs={{0,1},{1,0},{2,3},{3,2},{4,5},{5,4},{6,7},{7,6},{8,9},{9,8},{10,11... | collective-permute-start | bytes 2064392 | tf_op jit(solution)/shard_map/pair_other/ppermute | solution.py:134
  44.2 37.4 %collective-permute-start.7 = (bf16[3,448,256]{2,1,0:T(8,128)(2,1)}, bf16[3,448,256]{2,1,0:T(8,128)(2,1)}, u32[]{:S(2)}, u32[]{:S(2)}) collective-permute-start(bf16[3,448,256]{2,1,0:T(8,128)(2,1)} %collective-permute-done.refs_7_), channel_id=1, source_target_pairs={{1,2},{2,1},{5,6},{6,5},{9,10},{10,9},{13,14},{14,13},{17,18},{18,... | collective-permute-start | bytes 2064392 | tf_op jit(solution)/shard_map/mid1_other/ppermute | solution.py:134
  82.5 7.0 %collective-permute-start.8 = (bf16[4,256,896]{2,1,0:T(8,128)(2,1)S(1)}, bf16[4,256,896]{2,1,0:T(8,128)(2,1)}, u32[]{:S(2)}, u32[]{:S(2)}) collective-permute-start(bf16[4,256,896]{2,1,0:T(8,128)(2,1)S(1)} %collective-permute-done.1.refs_2_), channel_id=1, source_target_pairs={{0,4},{1,5},{2,6},{3,7},{4,0},{5,1},{6,2},{7,3},{8,12},{9,13},{10,... | collective-permute-start | bytes 5505032 | tf_op jit(solution)/shard_map/x_core/ppermute | solution.py:134
  82.5 44.5 %collective-permute-start.9 = (bf16[5,448,256]{2,1,0:T(8,128)(2,1)}, bf16[5,448,256]{2,1,0:T(8,128)(2,1)}, u32[]{:S(2)}, u32[]{:S(2)}) collective-permute-start(bf16[5,448,256]{2,1,0:T(8,128)(2,1)} %collective-permute-done.4), channel_id=1, source_target_pairs={{1,0},{2,3},{5,4},{6,7},{9,8},{10,11},{13,12},{14,15},{17,16},{18,... | collective-permute-start | bytes 3440648 | tf_op jit(solution)/shard_map/end2_kept/ppermute | solution.py:134
  85.5 16.6 %collective-permute-start.10 = (bf16[3,448,256]{2,1,0:T(8,128)(2,1)S(1)}, bf16[3,448,256]{2,1,0:T(8,128)(2,1)}, u32[]{:S(2)}, u32[]{:S(2)}) collective-permute-start(bf16[3,448,256]{2,1,0:T(8,128)(2,1)S(1)} %copy-done.20), channel_id=1, source_target_pairs={{1,2},{2,1},{5,6},{6,5},{9,10},{10,9},{13,14},{14,13},{17,18},{18,... | collective-permute-start | bytes 2064392 | tf_op jit(solution)/shard_map/mid2_other/ppermute | solution.py:134
  87.0 40.0 %collective-permute-start.11 = (bf16[3,448,256]{2,1,0:T(8,128)(2,1)}, bf16[3,448,256]{2,1,0:T(8,128)(2,1)S(1)}, u32[]{:S(2)}, u32[]{:S(2)}) collective-permute-start(bf16[3,448,256]{2,1,0:T(8,128)(2,1)} %collective-permute-done.7), channel_id=1, source_target_pairs={{1,0},{2,3},{5,4},{6,7},{9,8},{10,11},{13,12},{14,15},{17,16},{18,... | collective-permute-start | bytes 2064392 | tf_op jit(solution)/shard_map/end1_other/ppermute | solution.py:134
  89.4 41.4 %collective-permute-start.20 = (bf16[2,2,448,256]{3,2,1,0:T(8,128)(2,1)S(1)}, bf16[2,2,448,256]{3,2,1,0:T(8,128)(2,1)S(1)}, u32[]{:S(2)}, u32[]{:S(2)}) collective-permute-start(bf16[2,2,448,256]{3,2,1,0:T(8,128)(2,1)S(1)} %pad_maximum_fusion.refs_0_.refs_8_), channel_id=1, source_target_pairs={{0,16},{1,17},{2,18},{3,19},{4,20},{5,21},{6,22},{7,23},{8,0},{9,1... | collective-permute-start | bytes 2752520 | tf_op jit(solution)/shard_map/near_meet/ppermute | solution.py:134
  90.0 41.8 %collective-permute-start.21 = (bf16[2,2,448,256]{3,2,1,0:T(8,128)(2,1)S(1)}, bf16[2,2,448,256]{3,2,1,0:T(8,128)(2,1)S(1)}, u32[]{:S(2)}, u32[]{:S(2)}) collective-permute-start(bf16[2,2,448,256]{3,2,1,0:T(8,128)(2,1)S(1)} %pad_maximum_fusion.refs_0_.refs_8_), channel_id=1, source_target_pairs={{8,16},{9,17},{10,18},{11,19},{12,20},{13,21},{14,22},{15,23},{16,... | collective-permute-start | bytes 2752520 | tf_op jit(solution)/shard_map/near_corner/ppermute | solution.py:134
  98.1 31.6 %copy-start.4 = (f32[1040,768]{1,0:T(8,128)}, f32[1040,768]{1,0:T(8,128)S(1)}, u32[]{:S(2)}) copy-start(f32[1040,768]{1,0:T(8,128)S(1)} %project.2.refs_7_) | copy-start | bytes 9584644
  127.0 19.7 %collective-permute-start.12 = (bf16[3,448,256]{2,1,0:T(8,128)(2,1)}, bf16[3,448,256]{2,1,0:T(8,128)(2,1)}, u32[]{:S(2)}, u32[]{:S(2)}) collective-permute-start(bf16[3,448,256]{2,1,0:T(8,128)(2,1)} %collective-permute-done.10.refs_6_), channel_id=1, source_target_pairs={{1,0},{2,3},{5,4},{6,7},{9,8},{10,11},{13,12},{14,15},{17,16},{18,... | collective-permute-start | bytes 2064392 | tf_op jit(solution)/shard_map/end2_other/ppermute | solution.py:134
  132.7 19.9 %collective-permute-start.23 = (bf16[2,2,448,256]{3,2,1,0:T(8,128)(2,1)}, bf16[2,2,448,256]{3,2,1,0:T(8,128)(2,1)}, u32[]{:S(2)}, u32[]{:S(2)}) collective-permute-start(bf16[2,2,448,256]{3,2,1,0:T(8,128)(2,1)} %pad_maximum_fusion.1.refs_3_.refs_11_), channel_id=1, source_target_pairs={{8,16},{9,17},{10,18},{11,19},{12,20},{13,21},{14,22},{15,23},{16,... | collective-permute-start | bytes 2752520 | tf_op jit(solution)/shard_map/far_corner/ppermute | solution.py:134
  134.4 22.9 %collective-permute-start.22 = (bf16[2,2,448,256]{3,2,1,0:T(8,128)(2,1)}, bf16[2,2,448,256]{3,2,1,0:T(8,128)(2,1)}, u32[]{:S(2)}, u32[]{:S(2)}) collective-permute-start(bf16[2,2,448,256]{3,2,1,0:T(8,128)(2,1)} %pad_maximum_fusion.1.refs_3_.refs_11_), channel_id=1, source_target_pairs={{0,16},{1,17},{2,18},{3,19},{4,20},{5,21},{6,22},{7,23},{8,0},{9,1... | collective-permute-start | bytes 2752520 | tf_op jit(solution)/shard_map/far_meet/ppermute | solution.py:134
  146.7 10.5 %copy-start.14 = (bf16[2,2,448,256]{3,2,1,0:T(8,128)(2,1)S(1)}, bf16[2,2,448,256]{3,2,1,0:T(8,128)(2,1)}, u32[]{:S(2)}) copy-start(bf16[2,2,448,256]{3,2,1,0:T(8,128)(2,1)} %copy-done.13) | copy-start | bytes 2752516
  146.7 10.5 %copy-start.16 = (bf16[2,2,448,256]{3,2,1,0:T(8,128)(2,1)S(1)}, bf16[2,2,448,256]{3,2,1,0:T(8,128)(2,1)}, u32[]{:S(2)}) copy-start(bf16[2,2,448,256]{3,2,1,0:T(8,128)(2,1)} %copy-done.15) | copy-start | bytes 2752516
  152.7 25.7 %copy-start.12 = (bf16[2,256,896]{2,1,0:T(8,128)(2,1)S(1)}, bf16[2,256,896]{2,1,0:T(8,128)(2,1)}, u32[]{:S(2)}) copy-start(bf16[2,256,896]{2,1,0:T(8,128)(2,1)} %fusion.2.refs_15_) | copy-start | bytes 2752516
  159.4 18.9 %collective-permute-start.24 = (bf16[2,2,2,448,256]{4,3,2,1,0:T(8,128)(2,1)S(1)}, bf16[2,2,2,448,256]{4,3,2,1,0:T(8,128)(2,1)S(1)}, u32[]{:S(2)}, u32[]{:S(2)}) collective-permute-start(bf16[2,2,2,448,256]{4,3,2,1,0:T(8,128)(2,1)S(1)} %arrange.1), channel_id=1, source_target_pairs={{0,4},{1,5},{2,6},{3,7},{4,0},{5,1},{6,2},{7,3},{8,12},{9,13},{10,... | collective-permute-start | bytes 5505032 | tf_op jit(solution)/shard_map/out_core/ppermute | solution.py:134
  159.5 9.9 %collective-permute-start.13 = (bf16[528,256]{1,0:T(8,128)(2,1)S(1)}, bf16[528,256]{1,0:T(8,128)(2,1)S(1)}, u32[]{:S(2)}, u32[]{:S(2)}) collective-permute-start(bf16[528,256]{1,0:T(8,128)(2,1)S(1)} %get-tuple-element.43), channel_id=1, source_target_pairs={{0,16},{1,17},{2,18},{3,19},{4,20},{5,21},{6,22},{7,23},{8,24},{9,... | collective-permute-start | bytes 811016 | tf_op jit(solution)/shard_map/h_ctx/ppermute | solution.py:134
  162.1 14.3 %collective-permute-start.14 = (bf16[528,256]{1,0:T(8,128)(2,1)S(1)}, bf16[528,256]{1,0:T(8,128)(2,1)S(1)}, u32[]{:S(2)}, u32[]{:S(2)}) collective-permute-start(bf16[528,256]{1,0:T(8,128)(2,1)S(1)} %get-tuple-element.44.refs_0_), channel_id=1, source_target_pairs={{0,8},{1,9},{2,10},{3,11},{4,12},{5,13},{6,14},{7,15},{8,0},{9,1},... | collective-permute-start | bytes 811016 | tf_op jit(solution)/shard_map/h_y/ppermute | solution.py:134
  162.4 14.1 %collective-permute-start.15 = (bf16[528,256]{1,0:T(8,128)(2,1)S(1)}, bf16[528,256]{1,0:T(8,128)(2,1)S(1)}, u32[]{:S(2)}, u32[]{:S(2)}) collective-permute-start(bf16[528,256]{1,0:T(8,128)(2,1)S(1)} %get-tuple-element.43), channel_id=1, source_target_pairs={{0,24},{1,25},{2,26},{3,27},{4,28},{5,29},{6,30},{7,31},{8,16},{9,... | collective-permute-start | bytes 811016 | tf_op jit(solution)/shard_map/h_diag/ppermute | solution.py:134
  169.4 7.5 %collective-permute-start.16 = (bf16[528,256]{1,0:T(8,128)(2,1)S(1)}, bf16[528,256]{1,0:T(8,128)(2,1)S(1)}, u32[]{:S(2)}, u32[]{:S(2)}) collective-permute-start(bf16[528,256]{1,0:T(8,128)(2,1)S(1)} %get-tuple-element.44.refs_0_), channel_id=1, source_target_pairs={{0,4},{1,5},{2,6},{3,7},{4,0},{5,1},{6,2},{7,3},{8,12},{9,13},{10,... | collective-permute-start | bytes 811016 | tf_op jit(solution)/shard_map/h_core/ppermute | solution.py:134
  169.4 7.5 %collective-permute-start.17 = (bf16[528,256]{1,0:T(8,128)(2,1)S(1)}, bf16[528,256]{1,0:T(8,128)(2,1)S(1)}, u32[]{:S(2)}, u32[]{:S(2)}) collective-permute-start(bf16[528,256]{1,0:T(8,128)(2,1)S(1)} %collective-permute-done.13.refs_1_), channel_id=1, source_target_pairs={{0,4},{1,5},{2,6},{3,7},{4,0},{5,1},{6,2},{7,3},{8,12},{9,13},{10,... | collective-permute-start | bytes 811016 | tf_op jit(solution)/shard_map/h_core/ppermute | solution.py:134
  176.4 1.5 collective-permute-start.18
  176.4 1.9 %collective-permute-start.19 = (bf16[528,256]{1,0:T(8,128)(2,1)S(1)}, bf16[528,256]{1,0:T(8,128)(2,1)S(1)}, u32[]{:S(2)}, u32[]{:S(2)}) collective-permute-start(bf16[528,256]{1,0:T(8,128)(2,1)S(1)} %collective-permute-done.15.refs_3_), channel_id=1, source_target_pairs={{0,4},{1,5},{2,6},{3,7},{4,0},{5,1},{6,2},{7,3},{8,12},{9,13},{10,... | collective-permute-start | bytes 811016 | tf_op jit(solution)/shard_map/h_core/ppermute | solution.py:134
  (21 other events, 65.5 us)

commit v4 on v3

--- a/solution.py
+++ b/solution.py
@@ -138,6 +138,10 @@
     return lax.optimization_barrier((value, *earlier))[0]
 
 
+def after_all(values, *earlier):
+    return lax.optimization_barrier((*values, *earlier))[: len(values)]
+
+
 def to_ctx(c, t, r):
     return (1 - c, t, r)
 
@@ -314,9 +318,21 @@
     )(scalars, *xs, *mine, *other, *earlier)
 
 
-def attend_kernel(
-    dims, scalars, own_x, first_x, second_x, dec_x, mine, other0, other1, sum_ref, prior_ref, gain_ref, lengths, near_ref, far_ref, qkv
-):
+def attend_kernel(dims, scalars, *refs):
+    own_x, first_x, second_x, dec_x, mine, other0, other1, sum_ref, prior_ref, gain_ref, lengths = refs[:11]
+    sets, near_ref, far_ref, passed_ref, qkv, sems = (refs[11:14], refs[14:17]), *refs[17:]
+
+    def copy(half, source):
+        return pltpu.make_async_copy(source, passed_ref.at[half], sems.at[half])
+
+    for near in range(2):
+        for same in range(2):
+
+            @pl.when((scalars[7] == near) & (scalars[8] == same))
+            def _(near=near, same=same):
+                for half in range(2):
+                    copy(half, sets[near][half + 1 - same]).start()
+
     groups, block, heads, head, steps = dims
     for index in range(3):
         weight = weights_of(scalars, (mine,), (other0, other1), index)
@@ -380,9 +396,11 @@
         done = finish(read, gain)
         near_ref[groups * block :, h * head : (h + 1) * head] = done
         far_ref[groups * block :, h * head : (h + 1) * head] = done
-
-
-def attend(scalars, xs, mine, other, summed, prior, gain, lengths, dims):
+    for half in range(2):
+        copy(half, sets[0][0]).wait()
+
+
+def attend(scalars, xs, mine, other, summed, prior, gain, lengths, blocks, dims):
     groups, block, heads, head, _ = dims
     rows, columns = summed.shape
     shape = (groups * block + DEC_PAD, heads * head)
@@ -393,6 +411,8 @@
         whole(gain.shape),
         pl.BlockSpec(memory_space=pltpu.SMEM),
     ]
+    in_specs += [pl.BlockSpec(memory_space=pl.ANY)] * len(blocks)
+    passed = (2, *blocks[0].shape)
     out = jax.ShapeDtypeStruct(shape, jnp.bfloat16)
     return pl.pallas_call(
         lambda *refs: attend_kernel(dims, *refs),
@@ -400,72 +420,27 @@
             num_scalar_prefetch=1,
             grid=(1,),
             in_specs=in_specs,
-            out_specs=[whole(shape), whole(shape)],
-            scratch_shapes=[pltpu.VMEM((rows, columns), jnp.bfloat16)],
+            out_specs=[whole(shape), whole(shape), whole(passed)],
+            scratch_shapes=[pltpu.VMEM((rows, columns), jnp.bfloat16), pltpu.SemaphoreType.DMA((2,))],
         ),
-        out_shape=[out, out],
+        out_shape=[out, out, jax.ShapeDtypeStruct(passed, jnp.bfloat16)],
         compiler_params=params(),
         cost_estimate=pl.CostEstimate(
             flops=2 * rows * columns * xs[0].shape[2] * 2, bytes_accessed=4 * rows * columns, transcendentals=0
         ),
         name="attend",
-    )(scalars, *xs, *mine, *other, summed, prior, gain, lengths)
-
-
-def arrange_kernel(scalars, *refs):
-    groups, out_ref, sems = (refs[:3], refs[3:6]), refs[6], refs[7]
-
-    def copy(half, source):
-        return pltpu.make_async_copy(source, out_ref.at[half], sems.at[half])
-
-    for near in range(2):
-        for same in range(2):
-
-            @pl.when((scalars[1] == near) & (scalars[2] == same))
-            def _(near=near, same=same):
-                for half in range(2):
-                    copy(half, groups[near][half + 1 - same]).start()
-
-    for half in range(2):
-        copy(half, groups[0][0]).wait()
-
-
-def arrange(scalars, *blocks):
-    shape = (2, *blocks[0].shape)
-    return pl.pallas_call(
-        arrange_kernel,
-        grid_spec=pltpu.PrefetchScalarGridSpec(
-            num_scalar_prefetch=1,
-            grid=(1,),
-            in_specs=[pl.BlockSpec(memory_space=pl.ANY)] * 6,
-            out_specs=whole(shape),
-            scratch_shapes=[pltpu.SemaphoreType.DMA((2,))],
-        ),
-        out_shape=jax.ShapeDtypeStruct(shape, jnp.bfloat16),
-        compiler_params=params(),
-        name="arrange",
-    )(scalars, *blocks)
-
-
-def combine_kernel(scalars, *refs):
-    hidden, groups, passed = refs[:8], (refs[8:11], refs[11:14]), refs[14]
-    res_ref, dec_res_ref, out_ref, dec_ref, rows, weights, hidden_sems, weight_sems = refs[15:]
-    wide = hidden[0].shape[1]
-
-    def hidden_copy(i, j):
-        part = scalars[0] if j == 0 else 1 - scalars[0]
-        at = pl.ds(pl.multiple_of((2 * i + part) * wide, wide), wide)
-        source = hidden[4 * (i % 2) + 2 * (i // 2) + j]
-        return pltpu.make_async_copy(source, rows.at[:, at], hidden_sems.at[i, j])
-
-    def weight_copy(i, slot, part, source):
-        at = pl.ds((2 * i + part) * wide, wide)
-        return pltpu.make_async_copy(source, weights.at[slot, :, at], weight_sems.at[i, slot, part])
-
-    every = [(i, slot, part) for slot in range(2) for i in range(4) for part in range(2)]
-    for i in range(4):
-        for j in range(2):
-            hidden_copy(i, j).start()
+    )(scalars, *xs, *mine, *other, summed, prior, gain, lengths, *blocks)
+
+
+def lay_kernel(scalars, *refs):
+    groups, passed, out_ref, sems = (refs[:3], refs[3:6]), refs[6], refs[7], refs[8]
+    depth, wide = passed.shape[3:]
+
+    def copy(i, slot, part, source):
+        target = out_ref.at[pl.ds(slot * depth, depth), pl.ds((2 * i + part) * wide, wide)]
+        return pltpu.make_async_copy(source, target, sems.at[i, slot, part])
+
+    every = [(i, slot, part) for i in range(4) for slot in range(2) for part in range(2)]
     for near in range(2):
         for same in range(2):
 
@@ -474,20 +449,49 @@
                 for i, slot, part in every:
                     source = passed.at[i // 2] if i % 2 else groups[1 - near][i // 2 + 1 - same]
                     plane = jnp.bitwise_xor(scalars[3], slot)
-                    weight_copy(i, slot, part, source.at[plane, part]).start()
-
-    for i in range(4):
-        for j in range(2):
-            hidden_copy(i, j).wait()
-    total = []
-    for slot in range(2):
-        for i, at, part in every:
-            if at == slot:
-                weight_copy(i, slot, part, passed.at[0, 0, 0]).wait()
-        total.append(
-            lax.dot_general(rows[...], weights[slot], (((1,), (1,)), ((), ())), preferred_element_type=jnp.float32)
-        )
-    total = jnp.concatenate(total, axis=1)
+                    copy(i, slot, part, source.at[plane, part]).start()
+
+    for i, slot, part in every:
+        copy(i, slot, part, passed.at[0, 0, 0]).wait()
+
+
+def lay(scalars, *blocks):
+    depth, wide = blocks[0].shape[2:]
+    shape = (2 * depth, 8 * wide)
+    return pl.pallas_call(
+        lay_kernel,
+        grid_spec=pltpu.PrefetchScalarGridSpec(
+            num_scalar_prefetch=1,
+            grid=(1,),
+            in_specs=[pl.BlockSpec(memory_space=pl.ANY)] * len(blocks),
+            out_specs=whole(shape),
+            scratch_shapes=[pltpu.SemaphoreType.DMA((4, 2, 2))],
+        ),
+        out_shape=jax.ShapeDtypeStruct(shape, jnp.bfloat16),
+        compiler_params=params(),
+        name="lay",
+    )(scalars, *blocks)
+
+
+def combine_kernel(scalars, *refs):
+    hidden = refs[:8]
+    weights_ref, res_ref, dec_res_ref, out_ref, dec_ref, rows, sems = refs[8:]
+    wide = hidden[0].shape[1]
+
+    def copy(i, j):
+        part = scalars[0] if j == 0 else 1 - scalars[0]
+        at = pl.ds(pl.multiple_of((2 * i + part) * wide, wide), wide)
+        source = hidden[4 * (i % 2) + 2 * (i // 2) + j]
+        return pltpu.make_async_copy(source, rows.at[:, at], sems.at[i, j])
+
+    every = [(i, j) for i in range(4) for j in range(2)]
+    for i, j in every:
+        copy(i, j).start()
+    for i, j in every:
+        copy(i, j).wait()
+    total = lax.dot_general(
+        rows[...], weights_ref[...], (((1,), (1,)), ((), ())), preferred_element_type=jnp.float32
+    )
     groups, block = out_ref.shape[:2]
     for r in range(groups):
         out_ref[r] = (res_ref[r].astype(jnp.float32) + total[r * block : (r + 1) * block]).astype(jnp.bfloat16)
@@ -496,21 +500,18 @@
         dec_ref[step] = (dec_res_ref[step].astype(jnp.float32) + total[at : at + groups]).astype(jnp.bfloat16)
 
 
-def combine(scalars, hidden, blocks, res, dec_res):
-    anywhere = pl.BlockSpec(memory_space=pl.ANY)
+def combine(scalars, hidden, weights, res, dec_res):
     return pl.pallas_call(
         combine_kernel,
         grid_spec=pltpu.PrefetchScalarGridSpec(
             num_scalar_prefetch=1,
             grid=(1,),
-            in_specs=[anywhere] * (len(hidden) + len(blocks))
-            + [whole(res.shape), whole(dec_res.shape)],
+            in_specs=[pl.BlockSpec(memory_space=pl.ANY)] * len(hidden)
+            + [whole(weights.shape), whole(res.shape), whole(dec_res.shape)],
             out_specs=[whole(res.shape), whole(dec_res.shape)],
             scratch_shapes=[
-                pltpu.VMEM((hidden[0].shape[0], 8 * hidden[0].shape[1]), jnp.bfloat16),
-                pltpu.VMEM((2, blocks[0].shape[2], 8 * blocks[0].shape[3]), jnp.bfloat16),
+                pltpu.VMEM((hidden[0].shape[0], weights.shape[1]), jnp.bfloat16),
                 pltpu.SemaphoreType.DMA((4, 2)),
-                pltpu.SemaphoreType.DMA((4, 2, 2)),
             ],
         ),
         out_shape=[
@@ -519,7 +520,7 @@
         ],
         compiler_params=params(),
         name="combine",
-    )(scalars, *hidden, *blocks, res, dec_res)
+    )(scalars, *hidden, weights, res, dec_res)
 
 
 def local_grid(
@@ -537,7 +538,8 @@
     end = is_end.astype(jnp.int32)
     third = jnp.where(is_end, z ^ 2, z ^ 3)
     fourth = jnp.where(is_end, z ^ 3, z ^ 2)
-    scalars = jnp.stack([c, end, parity, z, z ^ 1, third, fourth]).astype(jnp.int32)
+    near_used = (z >> 1) == parity
+    scalars = jnp.stack([c, end, parity, z, z ^ 1, third, fourth, near_used, c == y]).astype(jnp.int32)
 
     def meet(c, t, r):
         return (1 - c, t, r) if c == t // 2 else (c, t ^ 2, r)
@@ -568,7 +570,7 @@
     stage = (mid2_kept, end1_kept, pair_other, mid1_other, first_x, near_blocks, dec_x)
     end2_kept = move(after(mid2_kept, *stage), mid_to_end, "end2_kept")
     mid2_other = move(after(pair_other, *stage), mid_swap, "mid2_other")
-    end1_other = move(after(mid1_other, *stage), mid_to_end, "end1_other")
+    end1_other = move(after(mid1_other, mid2_other), mid_to_end, "end1_other")
     second_x = move(after(first_x, *stage), to_core, "x_core")
     xs = (own_x, first_x, second_x, dec_x)
     summed = project(scalars, 0, xs, (kept, pair_kept), (other, pair_other), None)
@@ -588,29 +590,27 @@
         return (jnp.where(part >= level, part, 0).astype(jnp.float32) * scale).astype(jnp.bfloat16)
 
     res, dec_res = gate(after(spikes, second_x)), gate(after(dec_spikes, second_x))
+    fourth_kept = jnp.where(is_end, after(end2_kept, summed), mid2_kept)
+    far = carry(after(jnp.stack([third_kept[3:], fourth_kept[3:]]), near[1], near[2]), "far")
     stage = (mid2_other, end1_other, summed, res, dec_res)
     end2_other = move(after(mid2_other, *stage), mid_to_end, "end2_other")
     third_other = jnp.where(is_end, after(end1_other, *stage), mid1_other)
     summed = project(scalars, 2, xs, (third_kept,), (third_other,), summed)
-    fourth_kept = jnp.where(is_end, after(end2_kept, *stage), mid2_kept)
-    far = carry(after(jnp.stack([third_kept[3:], fourth_kept[3:]]), near[1], near[2]), "far")
     gain = lax.dynamic_slice_in_dim(head_gain, c * heads, heads, 0)
 
+    flags = jnp.stack([c, near_used, c == y, jnp.where(near_used, z & 1, z >> 1)]).astype(jnp.int32)
     dims = (groups, block, heads, head, steps)
-    own_rows, far_rows = attend(
-        scalars, xs, (fourth_kept,), (mid2_other, end2_other), summed, prior_state, gain, lengths, dims
+    own_rows, far_rows, passed = attend(
+        scalars, xs, (fourth_kept,), (mid2_other, end2_other), summed, prior_state, gain, lengths, near + far, dims
     )
     h_ctx = move(far_rows, to_ctx, "h_ctx")
     h_y = move(own_rows, to_y, "h_y")
     h_diag = move(far_rows, to_diagonal, "h_diag")
     mine = [own_rows, h_ctx, h_y, h_diag]
-    near_used = (z >> 1) == parity
-    flags = jnp.stack([c, near_used, c == y, jnp.where(near_used, z & 1, z >> 1)]).astype(jnp.int32)
-    passed = arrange(flags, *near, far[0], far[1], after(far[2], own_rows))
-    blocks = (*near, *far, move(passed, to_core, "out_core"))
-    hidden = mine + [move(m, to_core, "h_core") for m in (after(own_rows, h_ctx), h_ctx, h_y, h_diag)]
-
-    return combine(flags, hidden, blocks, res, dec_res)
+    weights = lay(flags, *near, *far, move(passed, to_core, "out_core"))
+    mine = [own_rows, h_ctx, h_y, h_diag]
+    hidden = mine + [move(m, to_core, "h_core") for m in after_all(mine, weights)]
+    return combine(flags, hidden, weights, res, dec_res)
 
 
 def solution(mesh):

time: 186 us -> 180 us (0.968)
  waiting for transfers between devices: 92.8 us -> 89.1 us
  Pallas kernels: 25.9 us -> 29.2 us
  starting transfers between devices: 36.9 us -> 33.6 us
    ppermute x25, waiting for transfers between devices: 92.8 us -> 89.1 us  [move(): return lax.ppermute(value, AXES, pairs)]
    ppermute x25, starting transfers between devices: 36.9 us -> 33.6 us  [move(): return lax.ppermute(value, AXES, pairs)]
    pallas_call x1, Pallas kernels: 5.9 us -> 8.84 us  [attend(): pl.pallas_call(lambda *refs: attend_kernel(dims, *refs), grid_spec=pltpu....]
    unnamed x56 -> x54, local copies, waits for them, and re-layouts: 16.2 us -> 15.9 us
  transfers between devices with their start and end apart: 25 -> 25, of which waited for: 9 -> 13; matrix products, arithmetic and copies ran while one was open for 6% -> 5% of each run, Pallas kernels for 10% -> 8%
where the time goes in v4:
time: 180 us; the launch traced here: 179 us
  waiting for transfers between devices  89.1 us (50%)
  starting transfers between devices  33.6 us (19%)
  Pallas kernels  29.2 us (16%)
  local copies, waits for them, and re-layouts  17.4 us (10%)
  other arithmetic  8.26 us (5%)
    ppermute x25, waiting for transfers between devices, move(): return lax.ppermute(value, AXES, pairs)  89.1 us
    ppermute x25, starting transfers between devices, move(): return lax.ppermute(value, AXES, pairs)  33.6 us
    unnamed x54, local copies, waits for them, and re-layouts  15.9 us
    pallas_call x2, Pallas kernels, project(): pl.pallas_call(lambda *refs: project_kernel(steps, bool(earlier), *refs),...  10.2 us
    pallas_call x1, Pallas kernels, attend(): pl.pallas_call(lambda *refs: attend_kernel(dims, *refs), grid_spec=pltpu....  8.84 us
    pallas_call x1, Pallas kernels, combine(): pl.pallas_call(combine_kernel, grid_spec=pltpu.PrefetchScalarGridSpec(num...  5.17 us
  transfers between devices with their start and end apart: 25, of which 13 were waited for; matrix products, arithmetic and copies ran while one was open for 5% of the time, Pallas kernels for 8%

profile of v4, /device:TPU:0, one launch (start us, length us, event | category | flops | bytes accessed | tf_op | source)
XLA Modules:
  0.0 178.9 jit_solution(3769882007372110704)
XLA Ops:
  0.8 1.3 copy-done.11
  3.8 3.0 %collective-permute-start = (bf16[3,448,256]{2,1,0:T(8,128)(2,1)S(1)}, bf16[3,448,256]{2,1,0:T(8,128)(2,1)}, u32[]{:S(2)}, u32[]{:S(2)}) collective-permute-start(bf16[3,448,256]{2,1,0:T(8,128)(2,1)S(1)} %get-tuple-element.28), channel_id=1, source_target_pairs={{0,16},{1,17},{2,18},{3,19},{4,20},{5,21},{6,22},{7,23},{8,24},{9,... | collective-permute-start | bytes 2064392 | tf_op jit(solution)/shard_map/pre_w/ppermute | solution.py:134
  6.8 1.6 collective-permute-start.2
  8.4 1.7 collective-permute-start.3
  10.1 3.1 %copy-done.6 = s32[2,256,3584]{2,1,0:T(8,128)S(1)} copy-done((s32[2,256,3584]{2,1,0:T(8,128)S(1)}, s32[2,256,3584]{2,1,0:T(8,128)}, u32[]{:S(2)}) %copy-start.6) | copy-done | bytes 7340056
  13.2 1.9 %embed.1.refs_1_ = bf16[4,512,896]{2,1,0:T(8,128)(2,1)S(1)} custom-call(s32[512,3584]{1,0:T(8,128)S(1)} %bitcast.20, s32[3584]{0:T(1024)S(1)} %copy-done.25, f32[3584]{0:T(1024)S(1)} %copy-done.24), custom_call_target="tpu_custom_call" | custom-call | tf_op jit(solution)/shard_map/embed/pallas_call | solution.py:246
  15.2 1.6 copy-done.1
  16.8 5.5 %collective-permute-done.refs_7_ = bf16[3,448,256]{2,1,0:T(8,128)(2,1)} collective-permute-done((bf16[3,448,256]{2,1,0:T(8,128)(2,1)S(1)}, bf16[3,448,256]{2,1,0:T(8,128)(2,1)}, u32[]{:S(2)}, u32[]{:S(2)}) %collective-permute-start) | collective-permute-done | bytes 688160 | tf_op jit(solution)/shard_map/pre_w/ppermute | solution.py:134
  22.4 1.7 collective-permute-start.1
  24.1 9.6 %collective-permute-done.2.refs_6_ = bf16[5,448,256]{2,1,0:T(8,128)(2,1)} collective-permute-done((bf16[5,448,256]{2,1,0:T(8,128)(2,1)S(1)}, bf16[5,448,256]{2,1,0:T(8,128)(2,1)}, u32[]{:S(2)}, u32[]{:S(2)}) %collective-permute-start.2) | collective-permute-done | bytes 1146912 | tf_op jit(solution)/shard_map/pair_kept/ppermute | solution.py:134
  33.7 1.7 collective-permute-start.4
  36.6 7.6 %collective-permute-start.6 = (bf16[3,448,256]{2,1,0:T(8,128)(2,1)}, bf16[3,448,256]{2,1,0:T(8,128)(2,1)}, u32[]{:S(2)}, u32[]{:S(2)}) collective-permute-start(bf16[3,448,256]{2,1,0:T(8,128)(2,1)} %collective-permute-done.refs_7_), channel_id=1, source_target_pairs={{0,1},{1,0},{2,3},{3,2},{4,5},{5,4},{6,7},{7,6},{8,9},{9,8},{10,11... | collective-permute-start | bytes 2064392 | tf_op jit(solution)/shard_map/pair_other/ppermute | solution.py:134
  44.2 1.5 collective-permute-start.7
  47.1 34.6 %collective-permute-done.6.refs_8_ = bf16[3,448,256]{2,1,0:T(8,128)(2,1)} collective-permute-done((bf16[3,448,256]{2,1,0:T(8,128)(2,1)}, bf16[3,448,256]{2,1,0:T(8,128)(2,1)}, u32[]{:S(2)}, u32[]{:S(2)}) %collective-permute-start.6) | collective-permute-done | bytes 688160 | tf_op jit(solution)/shard_map/pair_other/ppermute | solution.py:134
  83.1 1.5 collective-permute-start.10
  84.8 1.5 broadcast_select_fusion.refs_5_
  91.3 6.3 %project.2.refs_7_ = f32[1040,768]{1,0:T(8,128)S(1)} custom-call(s32[9]{0:T(128)S(1)} %stack.80.scalars.refs_0_, bf16[4,512,896]{2,1,0:T(8,128)(2,1)S(1)} %copy-done.2, bf16[4,256,896]{2,1,0:T(8,128)(2,1)S(1)} %collective-permute-done.1.refs_2_, bf16[4,256,896]{2,1,0:T(8,128)(2,1)} %collective-permute-done.8.refs_3_, ...), custom_call_target="tpu_custom_call" | custom-call | tf_op jit(solution)/shard_map/project/pallas_call | solution.py:305
  97.6 14.5 %collective-permute-done.9 = bf16[5,448,256]{2,1,0:T(8,128)(2,1)} collective-permute-done((bf16[5,448,256]{2,1,0:T(8,128)(2,1)}, bf16[5,448,256]{2,1,0:T(8,128)(2,1)}, u32[]{:S(2)}, u32[]{:S(2)}) %collective-permute-start.9) | collective-permute-done | bytes 1146912 | tf_op jit(solution)/shard_map/end2_kept/ppermute | solution.py:134
  112.1 1.4 broadcast_select_fusion.1.refs_5_
  115.3 1.6 collective-permute-start.16
  116.9 2.7 %fusion.2.refs_9_ = bf16[2,256,896]{2,1,0:T(8,128)(2,1)} fusion(s32[2,256,3584]{2,1,0:T(8,128)} %param.9, s32[]{:T(128)S(6)} %select_n.58, f32[896]{0:T(1024)S(1)} %dynamic_slice.23, s32[896]{0:T(1024)S(1)} %dynamic_slice.22), kind=kLoop, calls=%fused_computation.3 | loop fusion | flops 2293760 | bytes 2759684 | tf_op jit(solution)/shard_map/convert_element_type | solution.py:590
  119.6 6.8 %collective-permute-done.11 = bf16[3,448,256]{2,1,0:T(8,128)(2,1)} collective-permute-done((bf16[3,448,256]{2,1,0:T(8,128)(2,1)}, bf16[3,448,256]{2,1,0:T(8,128)(2,1)}, u32[]{:S(2)}, u32[]{:S(2)}) %collective-permute-start.11) | collective-permute-done | bytes 688160 | tf_op jit(solution)/shard_map/end1_other/ppermute | solution.py:134
  129.2 2.0 %copy-done.3 = bf16[4,512,896]{2,1,0:T(8,128)(2,1)S(1)} copy-done((bf16[4,512,896]{2,1,0:T(8,128)(2,1)S(1)}, bf16[4,512,896]{2,1,0:T(8,128)(2,1)}, u32[]{:S(2)}) %copy-start.3) | copy-done | bytes 3670040
  131.3 1.9 %copy-done.5 = f32[1040,768]{1,0:T(8,128)S(1)} copy-done((f32[1040,768]{1,0:T(8,128)S(1)}, f32[1040,768]{1,0:T(8,128)}, u32[]{:S(2)}) %copy-start.5) | copy-done | bytes 3194904
  133.2 3.9 %project.3.refs_8_ = f32[1040,768]{1,0:T(8,128)S(1)} custom-call(s32[9]{0:T(128)S(1)} %stack.80.scalars.refs_0_, bf16[4,512,896]{2,1,0:T(8,128)(2,1)S(1)} %copy-done.3, bf16[4,256,896]{2,1,0:T(8,128)(2,1)S(1)} %collective-permute-done.1.refs_2_, bf16[4,256,896]{2,1,0:T(8,128)(2,1)} %collective-permute-done.8.refs_3_, ...), custom_call_target="tpu_custom_call" | custom-call | tf_op jit(solution)/shard_map/project/pallas_call | solution.py:305
  137.0 8.6 %collective-permute-done.12.refs_7_ = bf16[3,448,256]{2,1,0:T(8,128)(2,1)} collective-permute-done((bf16[3,448,256]{2,1,0:T(8,128)(2,1)}, bf16[3,448,256]{2,1,0:T(8,128)(2,1)}, u32[]{:S(2)}, u32[]{:S(2)}) %collective-permute-start.12) | collective-permute-done | bytes 688160 | tf_op jit(solution)/shard_map/end2_other/ppermute | solution.py:134
  145.7 8.8 %attend.1 = (bf16[528,256]{1,0:T(8,128)(2,1)S(1)}, bf16[528,256]{1,0:T(8,128)(2,1)}, bf16[2,2,2,448,256]{4,3,2,1,0:T(8,128)(2,1)}) custom-call(s32[9]{0:T(128)S(1)} %stack.80.scalars.refs_0_, bf16[4,512,896]{2,1,0:T(8,128)(2,1)S(1)} %copy-done.3, bf16[4,256,896]{2,1,0:T(8,128)(2,1)S(1)} %collective-permute-done.1.refs_2_, ...), custom_call_target="tpu_custom_call" | custom-call | flops 2862612480 | bytes 3194880 | tf_op jit(solution)/shard_map/attend/pallas_call | solution.py:417
  155.3 1.5 collective-permute-start.18
  156.8 1.4 collective-permute-start.19
  161.1 2.4 %lay.1.refs_8_ = bf16[896,2048]{1,0:T(8,128)(2,1)S(1)} custom-call(s32[4]{0:T(128)S(1)} %pad_add_fusion.scalars, bf16[2,2,448,256]{3,2,1,0:T(8,128)(2,1)S(1)} %pad_maximum_fusion.refs_12_.refs_0_, bf16[2,2,448,256]{3,2,1,0:T(8,128)(2,1)S(1)} %copy-done.15, bf16[2,2,448,256]{3,2,1,0:T(8,128)(2,1)S(1)} %copy-done.18, ...), custom_call_target="tpu_custom_call" | custom-call | tf_op jit(solution)/shard_map/lay/pallas_call | solution.py:461
  164.2 6.4 %collective-permute-done.19.refs_3_ = bf16[528,256]{1,0:T(8,128)(2,1)} collective-permute-done((bf16[528,256]{1,0:T(8,128)(2,1)}, bf16[528,256]{1,0:T(8,128)(2,1)}, u32[]{:S(2)}, u32[]{:S(2)}) %collective-permute-start.19) | collective-permute-done | bytes 270368 | tf_op jit(solution)/shard_map/h_diag/ppermute | solution.py:134
  173.6 5.2 %combine.1 = (bf16[2,256,896]{2,1,0:T(8,128)(2,1)}, bf16[4,2,896]{2,1,0:T(2,128)(2,1)}) custom-call(s32[4]{0:T(128)S(1)} %pad_add_fusion.scalars, bf16[528,256]{1,0:T(8,128)(2,1)S(1)} %get-tuple-element.50.refs_0_, bf16[528,256]{1,0:T(8,128)(2,1)S(1)} %collective-permute-done.17.refs_1_, bf16[528,256]{1,0:T(8,128)(2,1)} %collective-permute-done.18.refs_2_, ...), custom_call_target="tpu_custom_call" | custom-call | tf_op jit(solution)/shard_map/combine/pallas_call | solution.py:504
  (97 shorter events, 22.6 us)
Async XLA Ops:
  0.6 127.1 %copy-start = (f32[4,128]{1,0:T(4,128)S(1)}, f32[4,128]{1,0:T(4,128)}, u32[]{:S(2)}) copy-start(f32[4,128]{1,0:T(4,128)} %param.15) | copy-start | bytes 6148
  3.8 42.1 %copy-start.19 = (bf16[5,448,256]{2,1,0:T(8,128)(2,1)}, bf16[5,448,256]{2,1,0:T(8,128)(2,1)S(1)}, u32[]{:S(2)}) copy-start(bf16[5,448,256]{2,1,0:T(8,128)(2,1)S(1)} %get-tuple-element.34.refs_5_) | copy-start | bytes 3440644
  3.8 18.5 %collective-permute-start = (bf16[3,448,256]{2,1,0:T(8,128)(2,1)S(1)}, bf16[3,448,256]{2,1,0:T(8,128)(2,1)}, u32[]{:S(2)}, u32[]{:S(2)}) collective-permute-start(bf16[3,448,256]{2,1,0:T(8,128)(2,1)S(1)} %get-tuple-element.28), channel_id=1, source_target_pairs={{0,16},{1,17},{2,18},{3,19},{4,20},{5,21},{6,22},{7,23},{8,24},{9,... | collective-permute-start | bytes 2064392 | tf_op jit(solution)/shard_map/pre_w/ppermute | solution.py:134
  6.8 26.8 %collective-permute-start.2 = (bf16[5,448,256]{2,1,0:T(8,128)(2,1)S(1)}, bf16[5,448,256]{2,1,0:T(8,128)(2,1)}, u32[]{:S(2)}, u32[]{:S(2)}) collective-permute-start(bf16[5,448,256]{2,1,0:T(8,128)(2,1)S(1)} %get-tuple-element.34.refs_5_), channel_id=1, source_target_pairs={{0,1},{1,0},{2,3},{3,2},{4,5},{5,4},{6,7},{7,6},{8,9},{9,8},{10,11... | collective-permute-start | bytes 3440648 | tf_op jit(solution)/shard_map/pair_kept/ppermute | solution.py:134
  8.4 25.3 %collective-permute-start.3 = (bf16[5,448,256]{2,1,0:T(8,128)(2,1)S(1)}, bf16[5,448,256]{2,1,0:T(8,128)(2,1)}, u32[]{:S(2)}, u32[]{:S(2)}) collective-permute-start(bf16[5,448,256]{2,1,0:T(8,128)(2,1)S(1)} %get-tuple-element.34.refs_5_), channel_id=1, source_target_pairs={{1,2},{2,1},{5,6},{6,5},{9,10},{10,9},{13,14},{14,13},{17,18},{18,... | collective-permute-start | bytes 3440648 | tf_op jit(solution)/shard_map/mid1_kept/ppermute | solution.py:134
  15.0 30.7 %copy-start.23 = (s32[4,2,3584]{2,1,0:T(2,128)S(1)}, s32[4,2,3584]{2,1,0:T(2,128)}, u32[]{:S(2)}) copy-start(s32[4,2,3584]{2,1,0:T(2,128)} %refs_0_) | copy-start | bytes 344068
  22.4 59.4 %collective-permute-start.1 = (bf16[4,256,896]{2,1,0:T(8,128)(2,1)S(1)}, bf16[4,256,896]{2,1,0:T(8,128)(2,1)S(1)}, u32[]{:S(2)}, u32[]{:S(2)}) collective-permute-start(bf16[4,256,896]{2,1,0:T(8,128)(2,1)S(1)} %constant_dynamic-slice_fusion.1), channel_id=1, source_target_pairs={{0,16},{1,17},{2,18},{3,19},{4,20},{5,21},{6,22},{7,23},{8,24},{9,... | collective-permute-start | bytes 5505032 | tf_op jit(solution)/shard_map/x_ctx/ppermute | solution.py:134
  33.7 48.1 %collective-permute-start.4 = (bf16[5,448,256]{2,1,0:T(8,128)(2,1)}, bf16[5,448,256]{2,1,0:T(8,128)(2,1)}, u32[]{:S(2)}, u32[]{:S(2)}) collective-permute-start(bf16[5,448,256]{2,1,0:T(8,128)(2,1)} %collective-permute-done.2.refs_6_), channel_id=1, source_target_pairs={{1,2},{2,1},{5,6},{6,5},{9,10},{10,9},{13,14},{14,13},{17,18},{18,... | collective-permute-start | bytes 3440648 | tf_op jit(solution)/shard_map/mid2_kept/ppermute | solution.py:134
  35.3 46.4 %collective-permute-start.5 = (bf16[5,448,256]{2,1,0:T(8,128)(2,1)}, bf16[5,448,256]{2,1,0:T(8,128)(2,1)}, u32[]{:S(2)}, u32[]{:S(2)}) collective-permute-start(bf16[5,448,256]{2,1,0:T(8,128)(2,1)} %collective-permute-done.3), channel_id=1, source_target_pairs={{1,0},{2,3},{5,4},{6,7},{9,8},{10,11},{13,12},{14,15},{17,16},{18,... | collective-permute-start | bytes 3440648 | tf_op jit(solution)/shard_map/end1_kept/ppermute | solution.py:134
  36.6 45.1 %collective-permute-start.6 = (bf16[3,448,256]{2,1,0:T(8,128)(2,1)}, bf16[3,448,256]{2,1,0:T(8,128)(2,1)}, u32[]{:S(2)}, u32[]{:S(2)}) collective-permute-start(bf16[3,448,256]{2,1,0:T(8,128)(2,1)} %collective-permute-done.refs_7_), channel_id=1, source_target_pairs={{0,1},{1,0},{2,3},{3,2},{4,5},{5,4},{6,7},{7,6},{8,9},{9,8},{10,11... | collective-permute-start | bytes 2064392 | tf_op jit(solution)/shard_map/pair_other/ppermute | solution.py:134
  44.2 37.5 %collective-permute-start.7 = (bf16[3,448,256]{2,1,0:T(8,128)(2,1)}, bf16[3,448,256]{2,1,0:T(8,128)(2,1)}, u32[]{:S(2)}, u32[]{:S(2)}) collective-permute-start(bf16[3,448,256]{2,1,0:T(8,128)(2,1)} %collective-permute-done.refs_7_), channel_id=1, source_target_pairs={{1,2},{2,1},{5,6},{6,5},{9,10},{10,9},{13,14},{14,13},{17,18},{18,... | collective-permute-start | bytes 2064392 | tf_op jit(solution)/shard_map/mid1_other/ppermute | solution.py:134
  81.8 4.6 %collective-permute-start.8 = (bf16[4,256,896]{2,1,0:T(8,128)(2,1)S(1)}, bf16[4,256,896]{2,1,0:T(8,128)(2,1)}, u32[]{:S(2)}, u32[]{:S(2)}) collective-permute-start(bf16[4,256,896]{2,1,0:T(8,128)(2,1)S(1)} %collective-permute-done.1.refs_2_), channel_id=1, source_target_pairs={{0,4},{1,5},{2,6},{3,7},{4,0},{5,1},{6,2},{7,3},{8,12},{9,13},{10,... | collective-permute-start | bytes 5505032 | tf_op jit(solution)/shard_map/x_core/ppermute | solution.py:134
  81.8 30.3 %collective-permute-start.9 = (bf16[5,448,256]{2,1,0:T(8,128)(2,1)}, bf16[5,448,256]{2,1,0:T(8,128)(2,1)}, u32[]{:S(2)}, u32[]{:S(2)}) collective-permute-start(bf16[5,448,256]{2,1,0:T(8,128)(2,1)} %collective-permute-done.4), channel_id=1, source_target_pairs={{1,0},{2,3},{5,4},{6,7},{9,8},{10,11},{13,12},{14,15},{17,16},{18,... | collective-permute-start | bytes 3440648 | tf_op jit(solution)/shard_map/end2_kept/ppermute | solution.py:134
  83.1 5.6 %collective-permute-start.10 = (bf16[3,448,256]{2,1,0:T(8,128)(2,1)}, bf16[3,448,256]{2,1,0:T(8,128)(2,1)}, u32[]{:S(2)}, u32[]{:S(2)}) collective-permute-start(bf16[3,448,256]{2,1,0:T(8,128)(2,1)} %collective-permute-done.6.refs_8_), channel_id=1, source_target_pairs={{1,2},{2,1},{5,6},{6,5},{9,10},{10,9},{13,14},{14,13},{17,18},{18,... | collective-permute-start | bytes 2064392 | tf_op jit(solution)/shard_map/mid2_other/ppermute | solution.py:134
  86.4 28.4 %collective-permute-start.13 = (bf16[2,2,448,256]{3,2,1,0:T(8,128)(2,1)S(1)}, bf16[2,2,448,256]{3,2,1,0:T(8,128)(2,1)S(1)}, u32[]{:S(2)}, u32[]{:S(2)}) collective-permute-start(bf16[2,2,448,256]{3,2,1,0:T(8,128)(2,1)S(1)} %pad_maximum_fusion.refs_12_.refs_0_), channel_id=1, source_target_pairs={{0,16},{1,17},{2,18},{3,19},{4,20},{5,21},{6,22},{7,23},{8,0},{9,1... | collective-permute-start | bytes 2752520 | tf_op jit(solution)/shard_map/near_meet/ppermute | solution.py:134
  86.9 27.8 %collective-permute-start.14 = (bf16[2,2,448,256]{3,2,1,0:T(8,128)(2,1)S(1)}, bf16[2,2,448,256]{3,2,1,0:T(8,128)(2,1)S(1)}, u32[]{:S(2)}, u32[]{:S(2)}) collective-permute-start(bf16[2,2,448,256]{3,2,1,0:T(8,128)(2,1)S(1)} %pad_maximum_fusion.refs_12_.refs_0_), channel_id=1, source_target_pairs={{8,16},{9,17},{10,18},{11,19},{12,20},{13,21},{14,22},{15,23},{16,... | collective-permute-start | bytes 2752520 | tf_op jit(solution)/shard_map/near_corner/ppermute | solution.py:134
  88.7 37.7 %collective-permute-start.11 = (bf16[3,448,256]{2,1,0:T(8,128)(2,1)}, bf16[3,448,256]{2,1,0:T(8,128)(2,1)}, u32[]{:S(2)}, u32[]{:S(2)}) collective-permute-start(bf16[3,448,256]{2,1,0:T(8,128)(2,1)} %collective-permute-done.7), channel_id=1, source_target_pairs={{1,0},{2,3},{5,4},{6,7},{9,8},{10,11},{13,12},{14,15},{17,16},{18,... | collective-permute-start | bytes 2064392 | tf_op jit(solution)/shard_map/end1_other/ppermute | solution.py:134
  97.6 16.0 %copy-start.4 = (f32[1040,768]{1,0:T(8,128)}, f32[1040,768]{1,0:T(8,128)S(1)}, u32[]{:S(2)}) copy-start(f32[1040,768]{1,0:T(8,128)S(1)} %project.2.refs_7_) | copy-start | bytes 9584644
  114.7 31.0 %collective-permute-start.15 = (bf16[2,2,448,256]{3,2,1,0:T(8,128)(2,1)}, bf16[2,2,448,256]{3,2,1,0:T(8,128)(2,1)}, u32[]{:S(2)}, u32[]{:S(2)}) collective-permute-start(bf16[2,2,448,256]{3,2,1,0:T(8,128)(2,1)} %pad_maximum_fusion.1.refs_15_.refs_3_), channel_id=1, source_target_pairs={{0,16},{1,17},{2,18},{3,19},{4,20},{5,21},{6,22},{7,23},{8,0},{9,1... | collective-permute-start | bytes 2752520 | tf_op jit(solution)/shard_map/far_meet/ppermute | solution.py:134
  115.3 30.4 %collective-permute-start.16 = (bf16[2,2,448,256]{3,2,1,0:T(8,128)(2,1)}, bf16[2,2,448,256]{3,2,1,0:T(8,128)(2,1)}, u32[]{:S(2)}, u32[]{:S(2)}) collective-permute-start(bf16[2,2,448,256]{3,2,1,0:T(8,128)(2,1)} %pad_maximum_fusion.1.refs_15_.refs_3_), channel_id=1, source_target_pairs={{8,16},{9,17},{10,18},{11,19},{12,20},{13,21},{14,22},{15,23},{16,... | collective-permute-start | bytes 2752520 | tf_op jit(solution)/shard_map/far_corner/ppermute | solution.py:134
  126.4 19.2 %collective-permute-start.12 = (bf16[3,448,256]{2,1,0:T(8,128)(2,1)}, bf16[3,448,256]{2,1,0:T(8,128)(2,1)}, u32[]{:S(2)}, u32[]{:S(2)}) collective-permute-start(bf16[3,448,256]{2,1,0:T(8,128)(2,1)} %collective-permute-done.10.refs_6_), channel_id=1, source_target_pairs={{1,0},{2,3},{5,4},{6,7},{9,8},{10,11},{13,12},{14,15},{17,16},{18,... | collective-permute-start | bytes 2064392 | tf_op jit(solution)/shard_map/end2_other/ppermute | solution.py:134
  133.2 12.6 %copy-start.21 = (f32[2,4,128,128]{3,2,1,0:T(8,128)S(1)}, f32[2,4,128,128]{3,2,1,0:T(8,128)}, u32[]{:S(2)}) copy-start(f32[2,4,128,128]{3,2,1,0:T(8,128)} %refs_9_.1) | copy-start | bytes 1572868
  133.2 12.6 %copy-start.26 = (s32[2]{0:T(128)S(1)}, s32[2]{0:T(128)}, u32[]{:S(2)}) copy-start(s32[2]{0:T(128)} %refs_11_.1) | copy-start | bytes 28
  154.6 4.2 %collective-permute-start.20 = (bf16[2,2,2,448,256]{4,3,2,1,0:T(8,128)(2,1)}, bf16[2,2,2,448,256]{4,3,2,1,0:T(8,128)(2,1)}, u32[]{:S(2)}, u32[]{:S(2)}) collective-permute-start(bf16[2,2,2,448,256]{4,3,2,1,0:T(8,128)(2,1)} %get-tuple-element.49), channel_id=1, source_target_pairs={{0,4},{1,5},{2,6},{3,7},{4,0},{5,1},{6,2},{7,3},{8,12},{9,13},{10,... | collective-permute-start | bytes 5505032 | tf_op jit(solution)/shard_map/out_core/ppermute | solution.py:134
  154.7 9.6 %collective-permute-start.17 = (bf16[528,256]{1,0:T(8,128)(2,1)}, bf16[528,256]{1,0:T(8,128)(2,1)S(1)}, u32[]{:S(2)}, u32[]{:S(2)}) collective-permute-start(bf16[528,256]{1,0:T(8,128)(2,1)} %get-tuple-element.48), channel_id=1, source_target_pairs={{0,16},{1,17},{2,18},{3,19},{4,20},{5,21},{6,22},{7,23},{8,24},{9,... | collective-permute-start | bytes 811016 | tf_op jit(solution)/shard_map/h_ctx/ppermute | solution.py:134
  155.3 9.0 %collective-permute-start.18 = (bf16[528,256]{1,0:T(8,128)(2,1)S(1)}, bf16[528,256]{1,0:T(8,128)(2,1)}, u32[]{:S(2)}, u32[]{:S(2)}) collective-permute-start(bf16[528,256]{1,0:T(8,128)(2,1)S(1)} %get-tuple-element.50.refs_0_), channel_id=1, source_target_pairs={{0,8},{1,9},{2,10},{3,11},{4,12},{5,13},{6,14},{7,15},{8,0},{9,1},... | collective-permute-start | bytes 811016 | tf_op jit(solution)/shard_map/h_y/ppermute | solution.py:134
  156.8 13.8 %collective-permute-start.19 = (bf16[528,256]{1,0:T(8,128)(2,1)}, bf16[528,256]{1,0:T(8,128)(2,1)}, u32[]{:S(2)}, u32[]{:S(2)}) collective-permute-start(bf16[528,256]{1,0:T(8,128)(2,1)} %get-tuple-element.48), channel_id=1, source_target_pairs={{0,24},{1,25},{2,26},{3,27},{4,28},{5,29},{6,30},{7,31},{8,16},{9,... | collective-permute-start | bytes 811016 | tf_op jit(solution)/shard_map/h_diag/ppermute | solution.py:134
  158.3 15.3 %copy-start.12 = (bf16[2,256,896]{2,1,0:T(8,128)(2,1)S(1)}, bf16[2,256,896]{2,1,0:T(8,128)(2,1)}, u32[]{:S(2)}) copy-start(bf16[2,256,896]{2,1,0:T(8,128)(2,1)} %fusion.2.refs_9_) | copy-start | bytes 2752516
  170.6 1.5 collective-permute-start.21
  170.6 2.0 %collective-permute-start.22 = (bf16[528,256]{1,0:T(8,128)(2,1)S(1)}, bf16[528,256]{1,0:T(8,128)(2,1)S(1)}, u32[]{:S(2)}, u32[]{:S(2)}) collective-permute-start(bf16[528,256]{1,0:T(8,128)(2,1)S(1)} %collective-permute-done.17.refs_1_), channel_id=1, source_target_pairs={{0,4},{1,5},{2,6},{3,7},{4,0},{5,1},{6,2},{7,3},{8,12},{9,13},{10,... | collective-permute-start | bytes 811016 | tf_op jit(solution)/shard_map/h_core/ppermute | solution.py:134
  171.1 2.0 %collective-permute-start.23 = (bf16[528,256]{1,0:T(8,128)(2,1)}, bf16[528,256]{1,0:T(8,128)(2,1)S(1)}, u32[]{:S(2)}, u32[]{:S(2)}) collective-permute-start(bf16[528,256]{1,0:T(8,128)(2,1)} %collective-permute-done.18.refs_2_), channel_id=1, source_target_pairs={{0,4},{1,5},{2,6},{3,7},{4,0},{5,1},{6,2},{7,3},{8,12},{9,13},{10,... | collective-permute-start | bytes 811016 | tf_op jit(solution)/shard_map/h_core/ppermute | solution.py:134
  171.1 2.4 %collective-permute-start.24 = (bf16[528,256]{1,0:T(8,128)(2,1)}, bf16[528,256]{1,0:T(8,128)(2,1)S(1)}, u32[]{:S(2)}, u32[]{:S(2)}) collective-permute-start(bf16[528,256]{1,0:T(8,128)(2,1)} %collective-permute-done.19.refs_3_), channel_id=1, source_target_pairs={{0,4},{1,5},{2,6},{3,7},{4,0},{5,1},{6,2},{7,3},{8,12},{9,13},{10,... | collective-permute-start | bytes 811016 | tf_op jit(solution)/shard_map/h_core/ppermute | solution.py:134
  (20 other events, 101.7 us)

commit v5 on v4

--- a/solution.py
+++ b/solution.py
@@ -320,10 +320,10 @@
 
 def attend_kernel(dims, scalars, *refs):
     own_x, first_x, second_x, dec_x, mine, other0, other1, sum_ref, prior_ref, gain_ref, lengths = refs[:11]
-    sets, near_ref, far_ref, passed_ref, qkv, sems = (refs[11:14], refs[14:17]), *refs[17:]
+    sets, near_ref, far_ref, passed_ref, qkv, held, sems = (refs[11:14], refs[14:17]), *refs[17:]
 
     def copy(half, source):
-        return pltpu.make_async_copy(source, passed_ref.at[half], sems.at[half])
+        return pltpu.make_async_copy(source, held.at[half], sems.at[half])
 
     for near in range(2):
         for same in range(2):
@@ -340,6 +340,10 @@
         for ref, at, rows in row_blocks((own_x, first_x, second_x, dec_x)):
             term = jnp.dot(ref[0], weight, preferred_element_type=jnp.float32)
             qkv[at : at + rows, columns] = (sum_ref[at : at + rows, columns] + term).astype(jnp.bfloat16)
+    for half in range(2):
+        copy(half, sets[0][0]).wait()
+    give = pltpu.make_async_copy(held, passed_ref, sems.at[2])
+    give.start()
     here = scalars[0]
     parity = scalars[2]
     wide = heads * head
@@ -396,8 +400,7 @@
         done = finish(read, gain)
         near_ref[groups * block :, h * head : (h + 1) * head] = done
         far_ref[groups * block :, h * head : (h + 1) * head] = done
-    for half in range(2):
-        copy(half, sets[0][0]).wait()
+    give.wait()
 
 
 def attend(scalars, xs, mine, other, summed, prior, gain, lengths, blocks, dims):
@@ -420,8 +423,12 @@
             num_scalar_prefetch=1,
             grid=(1,),
             in_specs=in_specs,
-            out_specs=[whole(shape), whole(shape), whole(passed)],
-            scratch_shapes=[pltpu.VMEM((rows, columns), jnp.bfloat16), pltpu.SemaphoreType.DMA((2,))],
+            out_specs=[whole(shape), whole(shape), pl.BlockSpec(memory_space=pl.ANY)],
+            scratch_shapes=[
+                pltpu.VMEM((rows, columns), jnp.bfloat16),
+                pltpu.VMEM(passed, jnp.bfloat16),
+                pltpu.SemaphoreType.DMA((3,)),
+            ],
         ),
         out_shape=[out, out, jax.ShapeDtypeStruct(passed, jnp.bfloat16)],
         compiler_params=params(),
@@ -558,11 +565,11 @@
 
     first_x = move(after(given_x, other), to_ctx, "x_ctx")
 
+    pair_other = move(after(other, given_x), to_pair, "pair_other")
+    mid1_other = move(after(other, given_x), mid_swap, "mid1_other")
     stage = (pair_kept, mid1_kept, other, given_x)
-    mid2_kept = move(after(pair_kept, *stage), mid_swap, "mid2_kept")
-    end1_kept = move(after(mid1_kept, *stage), mid_to_end, "end1_kept")
-    pair_other = move(after(other, *stage), to_pair, "pair_other")
-    mid1_other = move(after(other, *stage), mid_swap, "mid1_other")
+    mid2_kept = move(after(pair_kept, mid1_other, *stage), mid_swap, "mid2_kept")
+    end1_kept = move(after(mid1_kept, pair_other, *stage), mid_to_end, "end1_kept")
     dec_x = embed_steps(after(dec_spikes, *stage), thresholds, in_scale, planes)
 
     near_blocks = jnp.stack([after(kept, *stage)[3:], pair_kept[3:]])
@@ -593,7 +600,7 @@
     fourth_kept = jnp.where(is_end, after(end2_kept, summed), mid2_kept)
     far = carry(after(jnp.stack([third_kept[3:], fourth_kept[3:]]), near[1], near[2]), "far")
     stage = (mid2_other, end1_other, summed, res, dec_res)
-    end2_other = move(after(mid2_other, *stage), mid_to_end, "end2_other")
+    end2_other = move(after(mid2_other, fourth_kept), mid_to_end, "end2_other")
     third_other = jnp.where(is_end, after(end1_other, *stage), mid1_other)
     summed = project(scalars, 2, xs, (third_kept,), (third_other,), summed)
     gain = lax.dynamic_slice_in_dim(head_gain, c * heads, heads, 0)

time: 180 us -> 172 us (0.956)
  Pallas kernels: 29.2 us -> 24.7 us
  other arithmetic: 8.26 us -> 5.7 us
    unnamed x54 -> x56, local copies, waits for them, and re-layouts: 15.9 us -> 14.2 us
  transfers between devices with their start and end apart: 25 -> 25, of which waited for: 13 -> 14; matrix products, arithmetic and copies ran while one was open for 5% -> 4% of each run, Pallas kernels for 8% -> 7%
where the time goes in v5:
time: 172 us; the launch traced here: 171 us
  waiting for transfers between devices  89 us (52%)
  starting transfers between devices  34.9 us (20%)
  Pallas kernels  24.7 us (14%)
  local copies, waits for them, and re-layouts  15.7 us (9%)
  other arithmetic  5.7 us (3%)
    ppermute x25, waiting for transfers between devices, move(): return lax.ppermute(value, AXES, pairs)  89 us
    ppermute x25, starting transfers between devices, move(): return lax.ppermute(value, AXES, pairs)  34.9 us
    unnamed x56, local copies, waits for them, and re-layouts  14.2 us
    pallas_call x2, Pallas kernels, project(): pl.pallas_call(lambda *refs: project_kernel(steps, bool(earlier), *refs),...  8.55 us
    pallas_call x1, Pallas kernels, attend(): pl.pallas_call(lambda *refs: attend_kernel(dims, *refs), grid_spec=pltpu....  7.18 us
    pallas_call x1, Pallas kernels, combine(): pl.pallas_call(combine_kernel, grid_spec=pltpu.PrefetchScalarGridSpec(num...  5.09 us
  transfers between devices with their start and end apart: 25, of which 14 were waited for; matrix products, arithmetic and copies ran while one was open for 4% of the time, Pallas kernels for 7%

profile of v5, /device:TPU:0, one launch (start us, length us, event | category | flops | bytes accessed | tf_op | source)
XLA Modules:
  0.0 171.2 jit_solution(16500286023871763232)
XLA Ops:
  0.8 1.3 copy-done.12
  3.8 3.0 %collective-permute-start = (bf16[3,448,256]{2,1,0:T(8,128)(2,1)S(1)}, bf16[3,448,256]{2,1,0:T(8,128)(2,1)}, u32[]{:S(2)}, u32[]{:S(2)}) collective-permute-start(bf16[3,448,256]{2,1,0:T(8,128)(2,1)S(1)} %get-tuple-element.28), channel_id=1, source_target_pairs={{0,16},{1,17},{2,18},{3,19},{4,20},{5,21},{6,22},{7,23},{8,24},{9,... | collective-permute-start | bytes 2064392 | tf_op jit(solution)/shard_map/pre_w/ppermute | solution.py:134
  6.8 1.7 collective-permute-start.4
  8.5 3.5 %collective-permute-start.2 = (bf16[5,448,256]{2,1,0:T(8,128)(2,1)S(1)}, bf16[5,448,256]{2,1,0:T(8,128)(2,1)}, u32[]{:S(2)}, u32[]{:S(2)}) collective-permute-start(bf16[5,448,256]{2,1,0:T(8,128)(2,1)S(1)} %get-tuple-element.34.refs_5_), channel_id=1, source_target_pairs={{0,1},{1,0},{2,3},{3,2},{4,5},{5,4},{6,7},{7,6},{8,9},{9,8},{10,11... | collective-permute-start | bytes 3440648 | tf_op jit(solution)/shard_map/pair_kept/ppermute | solution.py:134
  12.0 3.1 %copy-done.7 = s32[2,256,3584]{2,1,0:T(8,128)S(1)} copy-done((s32[2,256,3584]{2,1,0:T(8,128)S(1)}, s32[2,256,3584]{2,1,0:T(8,128)}, u32[]{:S(2)}) %copy-start.7) | copy-done | bytes 7340056
  15.1 1.8 %embed.1.refs_1_ = bf16[4,512,896]{2,1,0:T(8,128)(2,1)S(1)} custom-call(s32[512,3584]{1,0:T(8,128)S(1)} %bitcast.20, s32[3584]{0:T(1024)S(1)} %copy-done.25, f32[3584]{0:T(1024)S(1)} %copy-done.26), custom_call_target="tpu_custom_call" | custom-call | tf_op jit(solution)/shard_map/embed/pallas_call | solution.py:246
  17.1 5.3 %collective-permute-done.refs_7_ = bf16[3,448,256]{2,1,0:T(8,128)(2,1)} collective-permute-done((bf16[3,448,256]{2,1,0:T(8,128)(2,1)S(1)}, bf16[3,448,256]{2,1,0:T(8,128)(2,1)}, u32[]{:S(2)}, u32[]{:S(2)}) %collective-permute-start) | collective-permute-done | bytes 688160 | tf_op jit(solution)/shard_map/pre_w/ppermute | solution.py:134
  22.4 1.8 %collective-permute-start.6 = (bf16[3,448,256]{2,1,0:T(8,128)(2,1)}, bf16[3,448,256]{2,1,0:T(8,128)(2,1)S(1)}, u32[]{:S(2)}, u32[]{:S(2)}) collective-permute-start(bf16[3,448,256]{2,1,0:T(8,128)(2,1)} %collective-permute-done.refs_7_), channel_id=1, source_target_pairs={{0,1},{1,0},{2,3},{3,2},{4,5},{5,4},{6,7},{7,6},{8,9},{9,8},{10,11... | collective-permute-start | bytes 2064392 | tf_op jit(solution)/shard_map/pair_other/ppermute | solution.py:134
  24.2 1.5 collective-permute-start.3
  25.7 1.5 collective-permute-start.1
  27.2 11.0 %collective-permute-done.2.refs_6_ = bf16[5,448,256]{2,1,0:T(8,128)(2,1)} collective-permute-done((bf16[5,448,256]{2,1,0:T(8,128)(2,1)S(1)}, bf16[5,448,256]{2,1,0:T(8,128)(2,1)}, u32[]{:S(2)}, u32[]{:S(2)}) %collective-permute-start.2) | collective-permute-done | bytes 1146912 | tf_op jit(solution)/shard_map/pair_kept/ppermute | solution.py:134
  38.2 13.2 %collective-permute-done.6.refs_8_ = bf16[3,448,256]{2,1,0:T(8,128)(2,1)S(1)} collective-permute-done((bf16[3,448,256]{2,1,0:T(8,128)(2,1)}, bf16[3,448,256]{2,1,0:T(8,128)(2,1)S(1)}, u32[]{:S(2)}, u32[]{:S(2)}) %collective-permute-start.6) | collective-permute-done | bytes 688160 | tf_op jit(solution)/shard_map/pair_other/ppermute | solution.py:134
  52.1 1.3 collective-permute-start.7
  54.8 25.8 %collective-permute-done.7 = bf16[5,448,256]{2,1,0:T(8,128)(2,1)S(1)} collective-permute-done((bf16[5,448,256]{2,1,0:T(8,128)(2,1)}, bf16[5,448,256]{2,1,0:T(8,128)(2,1)S(1)}, u32[]{:S(2)}, u32[]{:S(2)}) %collective-permute-start.7) | collective-permute-done | bytes 1146912 | tf_op jit(solution)/shard_map/end1_kept/ppermute | solution.py:134
  81.9 1.5 collective-permute-start.10
  85.1 4.2 %collective-permute-start.13 = (bf16[2,2,448,256]{3,2,1,0:T(8,128)(2,1)S(1)}, bf16[2,2,448,256]{3,2,1,0:T(8,128)(2,1)S(1)}, u32[]{:S(2)}, u32[]{:S(2)}) collective-permute-start(bf16[2,2,448,256]{3,2,1,0:T(8,128)(2,1)S(1)} %pad_maximum_fusion.refs_12_.refs_0_), channel_id=1, source_target_pairs={{0,16},{1,17},{2,18},{3,19},{4,20},{5,21},{6,22},{7,23},{8,0},{9,1... | collective-permute-start | bytes 2752520 | tf_op jit(solution)/shard_map/near_meet/ppermute | solution.py:134
  91.7 6.0 %project.2.refs_7_ = f32[1040,768]{1,0:T(8,128)S(1)} custom-call(s32[9]{0:T(128)S(1)} %stack.80.scalars.refs_0_, bf16[4,512,896]{2,1,0:T(8,128)(2,1)S(1)} %embed.1.refs_1_, bf16[4,256,896]{2,1,0:T(8,128)(2,1)S(1)} %collective-permute-done.1.refs_2_, bf16[4,256,896]{2,1,0:T(8,128)(2,1)S(1)} %collective-permute-done.8.refs_3_, ...), custom_call_target="tpu_custom_call" | custom-call | tf_op jit(solution)/shard_map/project/pallas_call | solution.py:305
  97.7 12.8 %collective-permute-done.9 = bf16[5,448,256]{2,1,0:T(8,128)(2,1)S(1)} collective-permute-done((bf16[5,448,256]{2,1,0:T(8,128)(2,1)S(1)}, bf16[5,448,256]{2,1,0:T(8,128)(2,1)S(1)}, u32[]{:S(2)}, u32[]{:S(2)}) %collective-permute-start.9) | collective-permute-done | bytes 1146912 | tf_op jit(solution)/shard_map/end2_kept/ppermute | solution.py:134
  113.8 1.6 collective-permute-start.16
  115.4 3.3 %collective-permute-start.15 = (bf16[2,2,448,256]{3,2,1,0:T(8,128)(2,1)}, bf16[2,2,448,256]{3,2,1,0:T(8,128)(2,1)}, u32[]{:S(2)}, u32[]{:S(2)}) collective-permute-start(bf16[2,2,448,256]{3,2,1,0:T(8,128)(2,1)} %pad_maximum_fusion.1.refs_15_.refs_3_), channel_id=1, source_target_pairs={{0,16},{1,17},{2,18},{3,19},{4,20},{5,21},{6,22},{7,23},{8,0},{9,1... | collective-permute-start | bytes 2752520 | tf_op jit(solution)/shard_map/far_meet/ppermute | solution.py:134
  120.3 2.9 %fusion.2.refs_9_ = bf16[2,256,896]{2,1,0:T(8,128)(2,1)} fusion(s32[2,256,3584]{2,1,0:T(8,128)} %param.9, s32[]{:T(128)S(6)} %select_n.60, f32[896]{0:T(1024)S(1)} %dynamic_slice.23, s32[896]{0:T(1024)S(1)} %dynamic_slice.22), kind=kLoop, calls=%fused_computation.3 | loop fusion | flops 2293760 | bytes 2759684 | tf_op jit(solution)/shard_map/convert_element_type | solution.py:597
  123.2 2.2 %collective-permute-done.12 = bf16[3,448,256]{2,1,0:T(8,128)(2,1)} collective-permute-done((bf16[3,448,256]{2,1,0:T(8,128)(2,1)}, bf16[3,448,256]{2,1,0:T(8,128)(2,1)}, u32[]{:S(2)}, u32[]{:S(2)}) %collective-permute-start.12) | collective-permute-done | bytes 688160 | tf_op jit(solution)/shard_map/end1_other/ppermute | solution.py:134
  126.6 1.5 copy-done.4
  128.1 1.9 %copy-done.6 = f32[1040,768]{1,0:T(8,128)S(1)} copy-done((f32[1040,768]{1,0:T(8,128)S(1)}, f32[1040,768]{1,0:T(8,128)}, u32[]{:S(2)}) %copy-start.6) | copy-done | bytes 3194904
  130.1 2.5 %project.3.refs_8_ = f32[1040,768]{1,0:T(8,128)S(1)} custom-call(s32[9]{0:T(128)S(1)} %stack.80.scalars.refs_0_, bf16[4,512,896]{2,1,0:T(8,128)(2,1)S(1)} %copy-done.2, bf16[4,256,896]{2,1,0:T(8,128)(2,1)S(1)} %collective-permute-done.1.refs_2_, bf16[4,256,896]{2,1,0:T(8,128)(2,1)S(1)} %copy-done.4, bf16[4,16,896]{2,1,0:T(8,128)(2,1)S(1)} %embed_steps.1.refs_4_, ...), custom_call_target="tpu_custom_call" | custom-call | tf_op jit(solution)/shard_map/project/pallas_call | solution.py:305
  132.6 7.1 %collective-permute-done.11.refs_7_ = bf16[3,448,256]{2,1,0:T(8,128)(2,1)S(1)} collective-permute-done((bf16[3,448,256]{2,1,0:T(8,128)(2,1)}, bf16[3,448,256]{2,1,0:T(8,128)(2,1)S(1)}, u32[]{:S(2)}, u32[]{:S(2)}) %collective-permute-start.11) | collective-permute-done | bytes 688160 | tf_op jit(solution)/shard_map/end2_other/ppermute | solution.py:134
  139.7 7.2 %attend.1 = (bf16[528,256]{1,0:T(8,128)(2,1)S(1)}, bf16[528,256]{1,0:T(8,128)(2,1)}, bf16[2,2,2,448,256]{4,3,2,1,0:T(8,128)(2,1)}) custom-call(s32[9]{0:T(128)S(1)} %stack.80.scalars.refs_0_, bf16[4,512,896]{2,1,0:T(8,128)(2,1)S(1)} %copy-done.2, bf16[4,256,896]{2,1,0:T(8,128)(2,1)S(1)} %collective-permute-done.1.refs_2_, ...), custom_call_target="tpu_custom_call" | custom-call | flops 2862612480 | bytes 3194880 | tf_op jit(solution)/shard_map/attend/pallas_call | solution.py:420
  147.0 1.6 collective-permute-start.19
  148.6 1.5 collective-permute-start.17
  154.6 2.9 %collective-permute-done.19.refs_3_ = bf16[528,256]{1,0:T(8,128)(2,1)S(1)} collective-permute-done((bf16[528,256]{1,0:T(8,128)(2,1)}, bf16[528,256]{1,0:T(8,128)(2,1)S(1)}, u32[]{:S(2)}, u32[]{:S(2)}) %collective-permute-start.19) | collective-permute-done | bytes 270368 | tf_op jit(solution)/shard_map/h_diag/ppermute | solution.py:134
  157.5 5.5 %collective-permute-done.17.refs_1_ = bf16[528,256]{1,0:T(8,128)(2,1)} collective-permute-done((bf16[528,256]{1,0:T(8,128)(2,1)}, bf16[528,256]{1,0:T(8,128)(2,1)}, u32[]{:S(2)}, u32[]{:S(2)}) %collective-permute-start.17) | collective-permute-done | bytes 270368 | tf_op jit(solution)/shard_map/h_ctx/ppermute | solution.py:134
  165.9 5.1 %combine.1 = (bf16[2,256,896]{2,1,0:T(8,128)(2,1)}, bf16[4,2,896]{2,1,0:T(2,128)(2,1)}) custom-call(s32[4]{0:T(128)S(1)} %pad_add_fusion.scalars, bf16[528,256]{1,0:T(8,128)(2,1)S(1)} %get-tuple-element.50.refs_0_, bf16[528,256]{1,0:T(8,128)(2,1)} %collective-permute-done.17.refs_1_, bf16[528,256]{1,0:T(8,128)(2,1)} %collective-permute-done.18.refs_2_, ...), custom_call_target="tpu_custom_call" | custom-call | tf_op jit(solution)/shard_map/combine/pallas_call | solution.py:511
  (99 shorter events, 22.7 us)
Async XLA Ops:
  0.6 118.3 %copy-start = (f32[4,128]{1,0:T(4,128)S(1)}, f32[4,128]{1,0:T(4,128)}, u32[]{:S(2)}) copy-start(f32[4,128]{1,0:T(4,128)} %param.15) | copy-start | bytes 6148
  3.8 49.8 %copy-start.20 = (bf16[5,448,256]{2,1,0:T(8,128)(2,1)}, bf16[5,448,256]{2,1,0:T(8,128)(2,1)S(1)}, u32[]{:S(2)}) copy-start(bf16[5,448,256]{2,1,0:T(8,128)(2,1)S(1)} %get-tuple-element.34.refs_5_) | copy-start | bytes 3440644
  3.8 18.5 %collective-permute-start = (bf16[3,448,256]{2,1,0:T(8,128)(2,1)S(1)}, bf16[3,448,256]{2,1,0:T(8,128)(2,1)}, u32[]{:S(2)}, u32[]{:S(2)}) collective-permute-start(bf16[3,448,256]{2,1,0:T(8,128)(2,1)S(1)} %get-tuple-element.28), channel_id=1, source_target_pairs={{0,16},{1,17},{2,18},{3,19},{4,20},{5,21},{6,22},{7,23},{8,24},{9,... | collective-permute-start | bytes 2064392 | tf_op jit(solution)/shard_map/pre_w/ppermute | solution.py:134
  6.8 20.4 %collective-permute-start.4 = (bf16[5,448,256]{2,1,0:T(8,128)(2,1)S(1)}, bf16[5,448,256]{2,1,0:T(8,128)(2,1)}, u32[]{:S(2)}, u32[]{:S(2)}) collective-permute-start(bf16[5,448,256]{2,1,0:T(8,128)(2,1)S(1)} %get-tuple-element.34.refs_5_), channel_id=1, source_target_pairs={{1,2},{2,1},{5,6},{6,5},{9,10},{10,9},{13,14},{14,13},{17,18},{18,... | collective-permute-start | bytes 3440648 | tf_op jit(solution)/shard_map/mid1_kept/ppermute | solution.py:134
  8.5 29.7 %collective-permute-start.2 = (bf16[5,448,256]{2,1,0:T(8,128)(2,1)S(1)}, bf16[5,448,256]{2,1,0:T(8,128)(2,1)}, u32[]{:S(2)}, u32[]{:S(2)}) collective-permute-start(bf16[5,448,256]{2,1,0:T(8,128)(2,1)S(1)} %get-tuple-element.34.refs_5_), channel_id=1, source_target_pairs={{0,1},{1,0},{2,3},{3,2},{4,5},{5,4},{6,7},{7,6},{8,9},{9,8},{10,11... | collective-permute-start | bytes 3440648 | tf_op jit(solution)/shard_map/pair_kept/ppermute | solution.py:134
  16.9 74.8 %copy-start.1 = (bf16[4,512,896]{2,1,0:T(8,128)(2,1)}, bf16[4,512,896]{2,1,0:T(8,128)(2,1)S(1)}, u32[]{:S(2)}) copy-start(bf16[4,512,896]{2,1,0:T(8,128)(2,1)S(1)} %embed.1.refs_1_) | copy-start | bytes 11010052
  16.9 36.5 %copy-start.24 = (s32[4,2,3584]{2,1,0:T(2,128)S(1)}, s32[4,2,3584]{2,1,0:T(2,128)}, u32[]{:S(2)}) copy-start(s32[4,2,3584]{2,1,0:T(2,128)} %refs_0_) | copy-start | bytes 344068
  22.4 29.0 %collective-permute-start.6 = (bf16[3,448,256]{2,1,0:T(8,128)(2,1)}, bf16[3,448,256]{2,1,0:T(8,128)(2,1)S(1)}, u32[]{:S(2)}, u32[]{:S(2)}) collective-permute-start(bf16[3,448,256]{2,1,0:T(8,128)(2,1)} %collective-permute-done.refs_7_), channel_id=1, source_target_pairs={{0,1},{1,0},{2,3},{3,2},{4,5},{5,4},{6,7},{7,6},{8,9},{9,8},{10,11... | collective-permute-start | bytes 2064392 | tf_op jit(solution)/shard_map/pair_other/ppermute | solution.py:134
  24.2 27.2 %collective-permute-start.3 = (bf16[3,448,256]{2,1,0:T(8,128)(2,1)}, bf16[3,448,256]{2,1,0:T(8,128)(2,1)}, u32[]{:S(2)}, u32[]{:S(2)}) collective-permute-start(bf16[3,448,256]{2,1,0:T(8,128)(2,1)} %collective-permute-done.refs_7_), channel_id=1, source_target_pairs={{1,2},{2,1},{5,6},{6,5},{9,10},{10,9},{13,14},{14,13},{17,18},{18,... | collective-permute-start | bytes 2064392 | tf_op jit(solution)/shard_map/mid1_other/ppermute | solution.py:134
  25.7 54.9 %collective-permute-start.1 = (bf16[4,256,896]{2,1,0:T(8,128)(2,1)S(1)}, bf16[4,256,896]{2,1,0:T(8,128)(2,1)S(1)}, u32[]{:S(2)}, u32[]{:S(2)}) collective-permute-start(bf16[4,256,896]{2,1,0:T(8,128)(2,1)S(1)} %constant_dynamic-slice_fusion.1), channel_id=1, source_target_pairs={{0,16},{1,17},{2,18},{3,19},{4,20},{5,21},{6,22},{7,23},{8,24},{9,... | collective-permute-start | bytes 5505032 | tf_op jit(solution)/shard_map/x_ctx/ppermute | solution.py:134
  51.4 3.4 %collective-permute-start.5 = (bf16[5,448,256]{2,1,0:T(8,128)(2,1)}, bf16[5,448,256]{2,1,0:T(8,128)(2,1)S(1)}, u32[]{:S(2)}, u32[]{:S(2)}) collective-permute-start(bf16[5,448,256]{2,1,0:T(8,128)(2,1)} %collective-permute-done.2.refs_6_), channel_id=1, source_target_pairs={{1,2},{2,1},{5,6},{6,5},{9,10},{10,9},{13,14},{14,13},{17,18},{18,... | collective-permute-start | bytes 3440648 | tf_op jit(solution)/shard_map/mid2_kept/ppermute | solution.py:134
  52.1 28.5 %collective-permute-start.7 = (bf16[5,448,256]{2,1,0:T(8,128)(2,1)}, bf16[5,448,256]{2,1,0:T(8,128)(2,1)S(1)}, u32[]{:S(2)}, u32[]{:S(2)}) collective-permute-start(bf16[5,448,256]{2,1,0:T(8,128)(2,1)} %collective-permute-done.4), channel_id=1, source_target_pairs={{1,0},{2,3},{5,4},{6,7},{9,8},{10,11},{13,12},{14,15},{17,16},{18,... | collective-permute-start | bytes 3440648 | tf_op jit(solution)/shard_map/end1_kept/ppermute | solution.py:134
  54.8 36.9 %copy-start.21 = (bf16[5,448,256]{2,1,0:T(8,128)(2,1)S(1)}, bf16[5,448,256]{2,1,0:T(8,128)(2,1)}, u32[]{:S(2)}) copy-start(bf16[5,448,256]{2,1,0:T(8,128)(2,1)} %copy-done.20) | copy-start | bytes 3440644
  80.6 3.8 %collective-permute-start.8 = (bf16[4,256,896]{2,1,0:T(8,128)(2,1)S(1)}, bf16[4,256,896]{2,1,0:T(8,128)(2,1)S(1)}, u32[]{:S(2)}, u32[]{:S(2)}) collective-permute-start(bf16[4,256,896]{2,1,0:T(8,128)(2,1)S(1)} %collective-permute-done.1.refs_2_), channel_id=1, source_target_pairs={{0,4},{1,5},{2,6},{3,7},{4,0},{5,1},{6,2},{7,3},{8,12},{9,13},{10,... | collective-permute-start | bytes 5505032 | tf_op jit(solution)/shard_map/x_core/ppermute | solution.py:134
  80.6 29.9 %collective-permute-start.9 = (bf16[5,448,256]{2,1,0:T(8,128)(2,1)S(1)}, bf16[5,448,256]{2,1,0:T(8,128)(2,1)S(1)}, u32[]{:S(2)}, u32[]{:S(2)}) collective-permute-start(bf16[5,448,256]{2,1,0:T(8,128)(2,1)S(1)} %collective-permute-done.5), channel_id=1, source_target_pairs={{1,0},{2,3},{5,4},{6,7},{9,8},{10,11},{13,12},{14,15},{17,16},{18,... | collective-permute-start | bytes 3440648 | tf_op jit(solution)/shard_map/end2_kept/ppermute | solution.py:134
  81.9 8.5 %collective-permute-start.10 = (bf16[3,448,256]{2,1,0:T(8,128)(2,1)S(1)}, bf16[3,448,256]{2,1,0:T(8,128)(2,1)}, u32[]{:S(2)}, u32[]{:S(2)}) collective-permute-start(bf16[3,448,256]{2,1,0:T(8,128)(2,1)S(1)} %collective-permute-done.6.refs_8_), channel_id=1, source_target_pairs={{1,2},{2,1},{5,6},{6,5},{9,10},{10,9},{13,14},{14,13},{17,18},{18,... | collective-permute-start | bytes 2064392 | tf_op jit(solution)/shard_map/mid2_other/ppermute | solution.py:134
  84.4 13.3 %copy-start.3 = (bf16[4,256,896]{2,1,0:T(8,128)(2,1)}, bf16[4,256,896]{2,1,0:T(8,128)(2,1)S(1)}, u32[]{:S(2)}) copy-start(bf16[4,256,896]{2,1,0:T(8,128)(2,1)S(1)} %collective-permute-done.8.refs_3_) | copy-start | bytes 5505028
  84.4 27.5 %collective-permute-start.14 = (bf16[2,2,448,256]{3,2,1,0:T(8,128)(2,1)S(1)}, bf16[2,2,448,256]{3,2,1,0:T(8,128)(2,1)S(1)}, u32[]{:S(2)}, u32[]{:S(2)}) collective-permute-start(bf16[2,2,448,256]{3,2,1,0:T(8,128)(2,1)S(1)} %pad_maximum_fusion.refs_12_.refs_0_), channel_id=1, source_target_pairs={{8,16},{9,17},{10,18},{11,19},{12,20},{13,21},{14,22},{15,23},{16,... | collective-permute-start | bytes 2752520 | tf_op jit(solution)/shard_map/near_corner/ppermute | solution.py:134
  85.1 27.8 %collective-permute-start.13 = (bf16[2,2,448,256]{3,2,1,0:T(8,128)(2,1)S(1)}, bf16[2,2,448,256]{3,2,1,0:T(8,128)(2,1)S(1)}, u32[]{:S(2)}, u32[]{:S(2)}) collective-permute-start(bf16[2,2,448,256]{3,2,1,0:T(8,128)(2,1)S(1)} %pad_maximum_fusion.refs_12_.refs_0_), channel_id=1, source_target_pairs={{0,16},{1,17},{2,18},{3,19},{4,20},{5,21},{6,22},{7,23},{8,0},{9,1... | collective-permute-start | bytes 2752520 | tf_op jit(solution)/shard_map/near_meet/ppermute | solution.py:134
  90.4 35.0 %collective-permute-start.12 = (bf16[3,448,256]{2,1,0:T(8,128)(2,1)}, bf16[3,448,256]{2,1,0:T(8,128)(2,1)}, u32[]{:S(2)}, u32[]{:S(2)}) collective-permute-start(bf16[3,448,256]{2,1,0:T(8,128)(2,1)} %collective-permute-done.3), channel_id=1, source_target_pairs={{1,0},{2,3},{5,4},{6,7},{9,8},{10,11},{13,12},{14,15},{17,16},{18,... | collective-permute-start | bytes 2064392 | tf_op jit(solution)/shard_map/end1_other/ppermute | solution.py:134
  113.8 25.9 %collective-permute-start.16 = (bf16[2,2,448,256]{3,2,1,0:T(8,128)(2,1)}, bf16[2,2,448,256]{3,2,1,0:T(8,128)(2,1)}, u32[]{:S(2)}, u32[]{:S(2)}) collective-permute-start(bf16[2,2,448,256]{3,2,1,0:T(8,128)(2,1)} %pad_maximum_fusion.1.refs_15_.refs_3_), channel_id=1, source_target_pairs={{8,16},{9,17},{10,18},{11,19},{12,20},{13,21},{14,22},{15,23},{16,... | collective-permute-start | bytes 2752520 | tf_op jit(solution)/shard_map/far_corner/ppermute | solution.py:134
  115.4 24.3 %collective-permute-start.15 = (bf16[2,2,448,256]{3,2,1,0:T(8,128)(2,1)}, bf16[2,2,448,256]{3,2,1,0:T(8,128)(2,1)}, u32[]{:S(2)}, u32[]{:S(2)}) collective-permute-start(bf16[2,2,448,256]{3,2,1,0:T(8,128)(2,1)} %pad_maximum_fusion.1.refs_15_.refs_3_), channel_id=1, source_target_pairs={{0,16},{1,17},{2,18},{3,19},{4,20},{5,21},{6,22},{7,23},{8,0},{9,1... | collective-permute-start | bytes 2752520 | tf_op jit(solution)/shard_map/far_meet/ppermute | solution.py:134
  118.9 20.8 %collective-permute-start.11 = (bf16[3,448,256]{2,1,0:T(8,128)(2,1)}, bf16[3,448,256]{2,1,0:T(8,128)(2,1)S(1)}, u32[]{:S(2)}, u32[]{:S(2)}) collective-permute-start(bf16[3,448,256]{2,1,0:T(8,128)(2,1)} %collective-permute-done.10.refs_6_), channel_id=1, source_target_pairs={{1,0},{2,3},{5,4},{6,7},{9,8},{10,11},{13,12},{14,15},{17,16},{18,... | collective-permute-start | bytes 2064392 | tf_op jit(solution)/shard_map/end2_other/ppermute | solution.py:134
  146.9 4.1 %collective-permute-start.20 = (bf16[2,2,2,448,256]{4,3,2,1,0:T(8,128)(2,1)}, bf16[2,2,2,448,256]{4,3,2,1,0:T(8,128)(2,1)S(1)}, u32[]{:S(2)}, u32[]{:S(2)}) collective-permute-start(bf16[2,2,2,448,256]{4,3,2,1,0:T(8,128)(2,1)} %get-tuple-element.49), channel_id=1, source_target_pairs={{0,4},{1,5},{2,6},{3,7},{4,0},{5,1},{6,2},{7,3},{8,12},{9,13},{10,... | collective-permute-start | bytes 5505032 | tf_op jit(solution)/shard_map/out_core/ppermute | solution.py:134
  147.0 10.5 %collective-permute-start.19 = (bf16[528,256]{1,0:T(8,128)(2,1)}, bf16[528,256]{1,0:T(8,128)(2,1)S(1)}, u32[]{:S(2)}, u32[]{:S(2)}) collective-permute-start(bf16[528,256]{1,0:T(8,128)(2,1)} %get-tuple-element.48), channel_id=1, source_target_pairs={{0,24},{1,25},{2,26},{3,27},{4,28},{5,29},{6,30},{7,31},{8,16},{9,... | collective-permute-start | bytes 811016 | tf_op jit(solution)/shard_map/h_diag/ppermute | solution.py:134
  148.6 14.4 %collective-permute-start.17 = (bf16[528,256]{1,0:T(8,128)(2,1)}, bf16[528,256]{1,0:T(8,128)(2,1)}, u32[]{:S(2)}, u32[]{:S(2)}) collective-permute-start(bf16[528,256]{1,0:T(8,128)(2,1)} %get-tuple-element.48), channel_id=1, source_target_pairs={{0,16},{1,17},{2,18},{3,19},{4,20},{5,21},{6,22},{7,23},{8,24},{9,... | collective-permute-start | bytes 811016 | tf_op jit(solution)/shard_map/h_ctx/ppermute | solution.py:134
  150.0 13.0 %collective-permute-start.18 = (bf16[528,256]{1,0:T(8,128)(2,1)S(1)}, bf16[528,256]{1,0:T(8,128)(2,1)}, u32[]{:S(2)}, u32[]{:S(2)}) collective-permute-start(bf16[528,256]{1,0:T(8,128)(2,1)S(1)} %get-tuple-element.50.refs_0_), channel_id=1, source_target_pairs={{0,8},{1,9},{2,10},{3,11},{4,12},{5,13},{6,14},{7,15},{8,0},{9,1},... | collective-permute-start | bytes 811016 | tf_op jit(solution)/shard_map/h_y/ppermute | solution.py:134
  150.6 15.3 %copy-start.13 = (bf16[2,256,896]{2,1,0:T(8,128)(2,1)S(1)}, bf16[2,256,896]{2,1,0:T(8,128)(2,1)}, u32[]{:S(2)}) copy-start(bf16[2,256,896]{2,1,0:T(8,128)(2,1)} %fusion.2.refs_9_) | copy-start | bytes 2752516
  163.0 1.9 %collective-permute-start.21 = (bf16[528,256]{1,0:T(8,128)(2,1)S(1)}, bf16[528,256]{1,0:T(8,128)(2,1)S(1)}, u32[]{:S(2)}, u32[]{:S(2)}) collective-permute-start(bf16[528,256]{1,0:T(8,128)(2,1)S(1)} %get-tuple-element.50.refs_0_), channel_id=1, source_target_pairs={{0,4},{1,5},{2,6},{3,7},{4,0},{5,1},{6,2},{7,3},{8,12},{9,13},{10,... | collective-permute-start | bytes 811016 | tf_op jit(solution)/shard_map/h_core/ppermute | solution.py:134
  163.0 2.2 %collective-permute-start.22 = (bf16[528,256]{1,0:T(8,128)(2,1)}, bf16[528,256]{1,0:T(8,128)(2,1)S(1)}, u32[]{:S(2)}, u32[]{:S(2)}) collective-permute-start(bf16[528,256]{1,0:T(8,128)(2,1)} %collective-permute-done.17.refs_1_), channel_id=1, source_target_pairs={{0,4},{1,5},{2,6},{3,7},{4,0},{5,1},{6,2},{7,3},{8,12},{9,13},{10,... | collective-permute-start | bytes 811016 | tf_op jit(solution)/shard_map/h_core/ppermute | solution.py:134
  163.5 2.4 %collective-permute-start.23 = (bf16[528,256]{1,0:T(8,128)(2,1)}, bf16[528,256]{1,0:T(8,128)(2,1)S(1)}, u32[]{:S(2)}, u32[]{:S(2)}) collective-permute-start(bf16[528,256]{1,0:T(8,128)(2,1)} %collective-permute-done.18.refs_2_), channel_id=1, source_target_pairs={{0,4},{1,5},{2,6},{3,7},{4,0},{5,1},{6,2},{7,3},{8,12},{9,13},{10,... | collective-permute-start | bytes 811016 | tf_op jit(solution)/shard_map/h_core/ppermute | solution.py:134
  163.5 2.4 %collective-permute-start.24 = (bf16[528,256]{1,0:T(8,128)(2,1)S(1)}, bf16[528,256]{1,0:T(8,128)(2,1)S(1)}, u32[]{:S(2)}, u32[]{:S(2)}) collective-permute-start(bf16[528,256]{1,0:T(8,128)(2,1)S(1)} %collective-permute-done.19.refs_3_), channel_id=1, source_target_pairs={{0,4},{1,5},{2,6},{3,7},{4,0},{5,1},{6,2},{7,3},{8,12},{9,13},{10,... | collective-permute-start | bytes 811016 | tf_op jit(solution)/shard_map/h_core/ppermute | solution.py:134
  (21 other events, 113.0 us)

commit v6 on v5

--- a/solution.py
+++ b/solution.py
@@ -444,7 +444,8 @@
     depth, wide = passed.shape[3:]
 
     def copy(i, slot, part, source):
-        target = out_ref.at[pl.ds(slot * depth, depth), pl.ds((2 * i + part) * wide, wide)]
+        at = 4 * (i % 2) + 2 * (i // 2) + part
+        target = out_ref.at[pl.ds(slot * depth, depth), pl.ds(at * wide, wide)]
         return pltpu.make_async_copy(source, target, sems.at[i, slot, part])
 
     every = [(i, slot, part) for i in range(4) for slot in range(2) for part in range(2)]
@@ -480,18 +481,17 @@
     )(scalars, *blocks)
 
 
-def combine_kernel(scalars, *refs):
-    hidden = refs[:8]
-    weights_ref, res_ref, dec_res_ref, out_ref, dec_ref, rows, sems = refs[8:]
+def combine_kernel(last, scalars, *refs):
+    hidden, weights_ref, refs = refs[:4], refs[4], refs[5:]
+    rows, sems = refs[-2:]
     wide = hidden[0].shape[1]
 
     def copy(i, j):
         part = scalars[0] if j == 0 else 1 - scalars[0]
         at = pl.ds(pl.multiple_of((2 * i + part) * wide, wide), wide)
-        source = hidden[4 * (i % 2) + 2 * (i // 2) + j]
-        return pltpu.make_async_copy(source, rows.at[:, at], sems.at[i, j])
-
-    every = [(i, j) for i in range(4) for j in range(2)]
+        return pltpu.make_async_copy(hidden[2 * i + j], rows.at[:, at], sems.at[i, j])
+
+    every = [(i, j) for i in range(2) for j in range(2)]
     for i, j in every:
         copy(i, j).start()
     for i, j in every:
@@ -499,6 +499,11 @@
     total = lax.dot_general(
         rows[...], weights_ref[...], (((1,), (1,)), ((), ())), preferred_element_type=jnp.float32
     )
+    if not last:
+        refs[0][...] = total
+        return
+    sum_ref, res_ref, dec_res_ref, out_ref, dec_ref = refs[:5]
+    total = sum_ref[...] + total
     groups, block = out_ref.shape[:2]
     for r in range(groups):
         out_ref[r] = (res_ref[r].astype(jnp.float32) + total[r * block : (r + 1) * block]).astype(jnp.bfloat16)
@@ -507,27 +512,27 @@
         dec_ref[step] = (dec_res_ref[step].astype(jnp.float32) + total[at : at + groups]).astype(jnp.bfloat16)
 
 
-def combine(scalars, hidden, weights, res, dec_res):
+def combine(scalars, hidden, weights, core, *rest):
+    rows, columns = hidden[0].shape[0], weights.shape[0]
+    half = weights.shape[1] // 2
+    out_shape = [jax.ShapeDtypeStruct((rows, columns), jnp.float32)]
+    if rest:
+        out_shape = [jax.ShapeDtypeStruct(res.shape, jnp.bfloat16) for res in rest[1:]]
     return pl.pallas_call(
-        combine_kernel,
+        lambda *refs: combine_kernel(bool(rest), *refs),
         grid_spec=pltpu.PrefetchScalarGridSpec(
             num_scalar_prefetch=1,
             grid=(1,),
             in_specs=[pl.BlockSpec(memory_space=pl.ANY)] * len(hidden)
-            + [whole(weights.shape), whole(res.shape), whole(dec_res.shape)],
-            out_specs=[whole(res.shape), whole(dec_res.shape)],
-            scratch_shapes=[
-                pltpu.VMEM((hidden[0].shape[0], weights.shape[1]), jnp.bfloat16),
-                pltpu.SemaphoreType.DMA((4, 2)),
-            ],
+            + [pl.BlockSpec((columns, half), lambda i, s: (0, core))]
+            + [whole(array.shape) for array in rest],
+            out_specs=[whole(out.shape) for out in out_shape],
+            scratch_shapes=[pltpu.VMEM((rows, half), jnp.bfloat16), pltpu.SemaphoreType.DMA((2, 2))],
         ),
-        out_shape=[
-            jax.ShapeDtypeStruct(res.shape, jnp.bfloat16),
-            jax.ShapeDtypeStruct(dec_res.shape, jnp.bfloat16),
-        ],
+        out_shape=out_shape,
         compiler_params=params(),
         name="combine",
-    )(scalars, *hidden, weights, res, dec_res)
+    )(scalars, *hidden, weights, *rest)
 
 
 def local_grid(
@@ -568,25 +573,25 @@
     pair_other = move(after(other, given_x), to_pair, "pair_other")
     mid1_other = move(after(other, given_x), mid_swap, "mid1_other")
     stage = (pair_kept, mid1_kept, other, given_x)
-    mid2_kept = move(after(pair_kept, mid1_other, *stage), mid_swap, "mid2_kept")
-    end1_kept = move(after(mid1_kept, pair_other, *stage), mid_to_end, "end1_kept")
+    mid2_kept = move(after(pair_kept, *stage), mid_swap, "mid2_kept")
+    end1_kept = move(after(mid1_kept, pair_other, mid1_other, *stage), mid_to_end, "end1_kept")
     dec_x = embed_steps(after(dec_spikes, *stage), thresholds, in_scale, planes)
 
     near_blocks = jnp.stack([after(kept, *stage)[3:], pair_kept[3:]])
 
     stage = (mid2_kept, end1_kept, pair_other, mid1_other, first_x, near_blocks, dec_x)
-    end2_kept = move(after(mid2_kept, *stage), mid_to_end, "end2_kept")
+    end2_kept = move(after(mid2_kept, near_blocks, dec_x), mid_to_end, "end2_kept")
     mid2_other = move(after(pair_other, *stage), mid_swap, "mid2_other")
     end1_other = move(after(mid1_other, mid2_other), mid_to_end, "end1_other")
-    second_x = move(after(first_x, *stage), to_core, "x_core")
+    third_kept = jnp.where(is_end, after(end1_kept, *stage), mid1_kept)
+    second_x = move(after(first_x, third_kept), to_core, "x_core")
     xs = (own_x, first_x, second_x, dec_x)
     summed = project(scalars, 0, xs, (kept, pair_kept), (other, pair_other), None)
 
     def carry(blocks, name):
         return blocks, move(blocks, meet, name + "_meet"), move(blocks, corner, name + "_corner")
 
-    third_kept = jnp.where(is_end, end1_kept, mid1_kept)
-    near = carry(after(near_blocks, second_x, third_kept), "near")
+    near = carry(after(near_blocks, third_kept), "near")
 
     columns = width // lax.axis_size("tp")
 
@@ -597,7 +602,7 @@
         return (jnp.where(part >= level, part, 0).astype(jnp.float32) * scale).astype(jnp.bfloat16)
 
     res, dec_res = gate(after(spikes, second_x)), gate(after(dec_spikes, second_x))
-    fourth_kept = jnp.where(is_end, after(end2_kept, summed), mid2_kept)
+    fourth_kept = jnp.where(is_end, end2_kept, mid2_kept)
     far = carry(after(jnp.stack([third_kept[3:], fourth_kept[3:]]), near[1], near[2]), "far")
     stage = (mid2_other, end1_other, summed, res, dec_res)
     end2_other = move(after(mid2_other, fourth_kept), mid_to_end, "end2_other")
@@ -616,8 +621,9 @@
     mine = [own_rows, h_ctx, h_y, h_diag]
     weights = lay(flags, *near, *far, move(passed, to_core, "out_core"))
     mine = [own_rows, h_ctx, h_y, h_diag]
-    hidden = mine + [move(m, to_core, "h_core") for m in after_all(mine, weights)]
-    return combine(flags, hidden, weights, res, dec_res)
+    sibling = [move(m, to_core, "h_core") for m in after_all(mine, weights)]
+    (partial,) = combine(flags, mine, weights, 0)
+    return tuple(combine(flags, sibling, weights, 1, partial, res, dec_res))
 
 
 def solution(mesh):

time: 172 us -> 166 us (0.965)
  waiting for transfers between devices: 89 us -> 81 us
  starting transfers between devices: 34.9 us -> 31.7 us
  local copies, waits for them, and re-layouts: 15.7 us -> 18.4 us
  Pallas kernels: 24.7 us -> 27.2 us
    ppermute x25, waiting for transfers between devices: 89 us -> 81 us  [move(): return lax.ppermute(value, AXES, pairs)]
    ppermute x25, starting transfers between devices: 34.9 us -> 31.7 us  [move(): return lax.ppermute(value, AXES, pairs)]
    unnamed x56 -> x52, local copies, waits for them, and re-layouts: 14.2 us -> 16.8 us
    pallas_call x1 -> x2, Pallas kernels: 5.09 us -> 6.25 us  [combine(): pl.pallas_call(lambda *refs: combine_kernel(bool(rest), *refs), grid_spec...]
  transfers between devices with their start and end apart: 25 -> 25, of which waited for: 14 -> 12; matrix products, arithmetic and copies ran while one was open for 4% -> 4% of each run, Pallas kernels for 7% -> 10%
where the time goes in v6:
time: 166 us; the launch traced here: 165 us
  waiting for transfers between devices  81 us (49%)
  starting transfers between devices  31.7 us (19%)
  Pallas kernels  27.2 us (16%)
  local copies, waits for them, and re-layouts  18.4 us (11%)
  other arithmetic  5.59 us (3%)
    ppermute x25, waiting for transfers between devices, move(): return lax.ppermute(value, AXES, pairs)  81 us
    ppermute x25, starting transfers between devices, move(): return lax.ppermute(value, AXES, pairs)  31.7 us
    unnamed x52, local copies, waits for them, and re-layouts  16.8 us
    pallas_call x2, Pallas kernels, project(): pl.pallas_call(lambda *refs: project_kernel(steps, bool(earlier), *refs),...  10 us
    pallas_call x1, Pallas kernels, attend(): pl.pallas_call(lambda *refs: attend_kernel(dims, *refs), grid_spec=pltpu....  7.14 us
    pallas_call x2, Pallas kernels, combine(): pl.pallas_call(lambda *refs: combine_kernel(bool(rest), *refs), grid_spec...  6.25 us
  transfers between devices with their start and end apart: 25, of which 12 were waited for; matrix products, arithmetic and copies ran while one was open for 4% of the time, Pallas kernels for 10%

profile of v6, /device:TPU:0, one launch (start us, length us, event | category | flops | bytes accessed | tf_op | source)
XLA Modules:
  0.0 165.3 jit_solution(8777442113762114691)
XLA Ops:
  0.8 1.3 copy-done.8
  3.8 3.0 %collective-permute-start = (bf16[3,448,256]{2,1,0:T(8,128)(2,1)S(1)}, bf16[3,448,256]{2,1,0:T(8,128)(2,1)}, u32[]{:S(2)}, u32[]{:S(2)}) collective-permute-start(bf16[3,448,256]{2,1,0:T(8,128)(2,1)S(1)} %get-tuple-element.28), channel_id=1, source_target_pairs={{0,16},{1,17},{2,18},{3,19},{4,20},{5,21},{6,22},{7,23},{8,24},{9,... | collective-permute-start | bytes 2064392 | tf_op jit(solution)/shard_map/pre_w/ppermute | solution.py:134
  6.8 1.7 %collective-permute-start.2 = (bf16[5,448,256]{2,1,0:T(8,128)(2,1)S(1)}, bf16[5,448,256]{2,1,0:T(8,128)(2,1)}, u32[]{:S(2)}, u32[]{:S(2)}) collective-permute-start(bf16[5,448,256]{2,1,0:T(8,128)(2,1)S(1)} %get-tuple-element.34.refs_5_), channel_id=1, source_target_pairs={{1,2},{2,1},{5,6},{6,5},{9,10},{10,9},{13,14},{14,13},{17,18},{18,... | collective-permute-start | bytes 3440648 | tf_op jit(solution)/shard_map/mid1_kept/ppermute | solution.py:134
  8.5 3.4 %collective-permute-start.5 = (bf16[5,448,256]{2,1,0:T(8,128)(2,1)S(1)}, bf16[5,448,256]{2,1,0:T(8,128)(2,1)}, u32[]{:S(2)}, u32[]{:S(2)}) collective-permute-start(bf16[5,448,256]{2,1,0:T(8,128)(2,1)S(1)} %get-tuple-element.34.refs_5_), channel_id=1, source_target_pairs={{0,1},{1,0},{2,3},{3,2},{4,5},{5,4},{6,7},{7,6},{8,9},{9,8},{10,11... | collective-permute-start | bytes 3440648 | tf_op jit(solution)/shard_map/pair_kept/ppermute | solution.py:134
  12.0 3.1 %copy-done.3 = s32[2,256,3584]{2,1,0:T(8,128)S(1)} copy-done((s32[2,256,3584]{2,1,0:T(8,128)S(1)}, s32[2,256,3584]{2,1,0:T(8,128)}, u32[]{:S(2)}) %copy-start.3) | copy-done | bytes 7340056
  15.1 1.8 %embed.1.refs_1_ = bf16[4,512,896]{2,1,0:T(8,128)(2,1)S(1)} custom-call(s32[512,3584]{1,0:T(8,128)S(1)} %bitcast.20, s32[3584]{0:T(1024)S(1)} %copy-done.24, f32[3584]{0:T(1024)S(1)} %copy-done.23), custom_call_target="tpu_custom_call" | custom-call | tf_op jit(solution)/shard_map/embed/pallas_call | solution.py:246
  17.1 1.6 copy-done.1
  18.7 3.7 %collective-permute-done.refs_7_ = bf16[3,448,256]{2,1,0:T(8,128)(2,1)} collective-permute-done((bf16[3,448,256]{2,1,0:T(8,128)(2,1)S(1)}, bf16[3,448,256]{2,1,0:T(8,128)(2,1)}, u32[]{:S(2)}, u32[]{:S(2)}) %collective-permute-start) | collective-permute-done | bytes 688160 | tf_op jit(solution)/shard_map/pre_w/ppermute | solution.py:134
  22.4 1.8 %collective-permute-start.3 = (bf16[3,448,256]{2,1,0:T(8,128)(2,1)}, bf16[3,448,256]{2,1,0:T(8,128)(2,1)S(1)}, u32[]{:S(2)}, u32[]{:S(2)}) collective-permute-start(bf16[3,448,256]{2,1,0:T(8,128)(2,1)} %collective-permute-done.refs_7_), channel_id=1, source_target_pairs={{0,1},{1,0},{2,3},{3,2},{4,5},{5,4},{6,7},{7,6},{8,9},{9,8},{10,11... | collective-permute-start | bytes 2064392 | tf_op jit(solution)/shard_map/pair_other/ppermute | solution.py:134
  24.2 1.5 collective-permute-start.4
  25.7 1.5 collective-permute-start.1
  27.2 11.0 %collective-permute-done.5.refs_6_ = bf16[5,448,256]{2,1,0:T(8,128)(2,1)} collective-permute-done((bf16[5,448,256]{2,1,0:T(8,128)(2,1)S(1)}, bf16[5,448,256]{2,1,0:T(8,128)(2,1)}, u32[]{:S(2)}, u32[]{:S(2)}) %collective-permute-start.5) | collective-permute-done | bytes 1146912 | tf_op jit(solution)/shard_map/pair_kept/ppermute | solution.py:134
  39.0 12.4 %collective-permute-done.3.refs_8_ = bf16[3,448,256]{2,1,0:T(8,128)(2,1)S(1)} collective-permute-done((bf16[3,448,256]{2,1,0:T(8,128)(2,1)}, bf16[3,448,256]{2,1,0:T(8,128)(2,1)S(1)}, u32[]{:S(2)}, u32[]{:S(2)}) %collective-permute-start.3) | collective-permute-done | bytes 688160 | tf_op jit(solution)/shard_map/pair_other/ppermute | solution.py:134
  54.0 1.3 collective-permute-start.9
  55.3 11.0 %collective-permute-done.1.refs_2_ = bf16[4,256,896]{2,1,0:T(8,128)(2,1)S(1)} collective-permute-done((bf16[4,256,896]{2,1,0:T(8,128)(2,1)S(1)}, bf16[4,256,896]{2,1,0:T(8,128)(2,1)S(1)}, u32[]{:S(2)}, u32[]{:S(2)}) %collective-permute-start.1) | collective-permute-done | bytes 1835040 | tf_op jit(solution)/shard_map/x_ctx/ppermute | solution.py:134
  66.3 15.1 %collective-permute-done.6 = bf16[5,448,256]{2,1,0:T(8,128)(2,1)S(1)} collective-permute-done((bf16[5,448,256]{2,1,0:T(8,128)(2,1)}, bf16[5,448,256]{2,1,0:T(8,128)(2,1)S(1)}, u32[]{:S(2)}, u32[]{:S(2)}) %collective-permute-start.6) | collective-permute-done | bytes 1146912 | tf_op jit(solution)/shard_map/end1_kept/ppermute | solution.py:134
  81.7 1.5 collective-permute-start.10
  86.9 17.0 %collective-permute-done.9 = bf16[5,448,256]{2,1,0:T(8,128)(2,1)S(1)} collective-permute-done((bf16[5,448,256]{2,1,0:T(8,128)(2,1)S(1)}, bf16[5,448,256]{2,1,0:T(8,128)(2,1)S(1)}, u32[]{:S(2)}, u32[]{:S(2)}) %collective-permute-start.9) | collective-permute-done | bytes 1146912 | tf_op jit(solution)/shard_map/end2_kept/ppermute | solution.py:134
  107.8 3.6 %collective-permute-start.15 = (bf16[2,2,448,256]{3,2,1,0:T(8,128)(2,1)}, bf16[2,2,448,256]{3,2,1,0:T(8,128)(2,1)}, u32[]{:S(2)}, u32[]{:S(2)}) collective-permute-start(bf16[2,2,448,256]{3,2,1,0:T(8,128)(2,1)} %pad_maximum_fusion.1.refs_15_.refs_3_), channel_id=1, source_target_pairs={{0,16},{1,17},{2,18},{3,19},{4,20},{5,21},{6,22},{7,23},{8,0},{9,1... | collective-permute-start | bytes 2752520 | tf_op jit(solution)/shard_map/far_meet/ppermute | solution.py:134
  111.5 1.6 collective-permute-start.16
  114.6 2.0 %copy-done.2 = bf16[4,512,896]{2,1,0:T(8,128)(2,1)S(1)} copy-done((bf16[4,512,896]{2,1,0:T(8,128)(2,1)S(1)}, bf16[4,512,896]{2,1,0:T(8,128)(2,1)}, u32[]{:S(2)}) %copy-start.2) | copy-done | bytes 3670040
  119.0 6.1 %project.2.refs_7_ = f32[1040,768]{1,0:T(8,128)S(1)} custom-call(s32[9]{0:T(128)S(1)} %stack.80.scalars.refs_0_, bf16[4,512,896]{2,1,0:T(8,128)(2,1)S(1)} %copy-done.2, bf16[4,256,896]{2,1,0:T(8,128)(2,1)S(1)} %collective-permute-done.1.refs_2_, bf16[4,256,896]{2,1,0:T(8,128)(2,1)} %collective-permute-done.8.refs_3_, ...), custom_call_target="tpu_custom_call" | custom-call | tf_op jit(solution)/shard_map/project/pallas_call | solution.py:305
  125.1 2.8 %fusion.2.refs_7_ = bf16[2,256,896]{2,1,0:T(8,128)(2,1)} fusion(s32[2,256,3584]{2,1,0:T(8,128)} %param.9, s32[]{:T(128)S(6)} %select_n.60, f32[896]{0:T(1024)S(1)} %dynamic_slice.23, s32[896]{0:T(1024)S(1)} %dynamic_slice.22), kind=kLoop, calls=%fused_computation.3 | loop fusion | flops 2293760 | bytes 2759684 | tf_op jit(solution)/shard_map/convert_element_type | solution.py:602
  129.2 3.9 %project.3.refs_8_ = f32[1040,768]{1,0:T(8,128)S(1)} custom-call(s32[9]{0:T(128)S(1)} %stack.80.scalars.refs_0_, bf16[4,512,896]{2,1,0:T(8,128)(2,1)S(1)} %copy-done.2, bf16[4,256,896]{2,1,0:T(8,128)(2,1)S(1)} %collective-permute-done.1.refs_2_, bf16[4,256,896]{2,1,0:T(8,128)(2,1)} %collective-permute-done.8.refs_3_, ...), custom_call_target="tpu_custom_call" | custom-call | tf_op jit(solution)/shard_map/project/pallas_call | solution.py:305
  134.0 7.1 %attend.1 = (bf16[528,256]{1,0:T(8,128)(2,1)S(1)}, bf16[528,256]{1,0:T(8,128)(2,1)}, bf16[2,2,2,448,256]{4,3,2,1,0:T(8,128)(2,1)}) custom-call(s32[9]{0:T(128)S(1)} %stack.80.scalars.refs_0_, bf16[4,512,896]{2,1,0:T(8,128)(2,1)S(1)} %copy-done.2, bf16[4,256,896]{2,1,0:T(8,128)(2,1)S(1)} %collective-permute-done.1.refs_2_, ...), custom_call_target="tpu_custom_call" | custom-call | flops 2862612480 | bytes 3194880 | tf_op jit(solution)/shard_map/attend/pallas_call | solution.py:420
  141.2 2.1 %collective-permute-start.17 = (bf16[528,256]{1,0:T(8,128)(2,1)}, bf16[528,256]{1,0:T(8,128)(2,1)S(1)}, u32[]{:S(2)}, u32[]{:S(2)}) collective-permute-start(bf16[528,256]{1,0:T(8,128)(2,1)} %get-tuple-element.48), channel_id=1, source_target_pairs={{0,16},{1,17},{2,18},{3,19},{4,20},{5,21},{6,22},{7,23},{8,24},{9,... | collective-permute-start | bytes 811016 | tf_op jit(solution)/shard_map/h_ctx/ppermute | solution.py:134
  143.4 1.5 collective-permute-start.19
  148.8 2.0 %collective-permute-done.17.refs_2_ = bf16[528,256]{1,0:T(8,128)(2,1)S(1)} collective-permute-done((bf16[528,256]{1,0:T(8,128)(2,1)}, bf16[528,256]{1,0:T(8,128)(2,1)S(1)}, u32[]{:S(2)}, u32[]{:S(2)}) %collective-permute-start.17) | collective-permute-done | bytes 270368 | tf_op jit(solution)/shard_map/h_ctx/ppermute | solution.py:134
  150.8 1.6 collective-permute-done.18.refs_3_
  152.4 5.3 %collective-permute-done.19.refs_4_ = bf16[528,256]{1,0:T(8,128)(2,1)} collective-permute-done((bf16[528,256]{1,0:T(8,128)(2,1)}, bf16[528,256]{1,0:T(8,128)(2,1)}, u32[]{:S(2)}, u32[]{:S(2)}) %collective-permute-start.19) | collective-permute-done | bytes 270368 | tf_op jit(solution)/shard_map/h_diag/ppermute | solution.py:134
  158.8 3.1 %combine.2.refs_6_ = f32[528,896]{1,0:T(8,128)S(1)} custom-call(s32[4]{0:T(128)S(1)} %pad_add_fusion.scalars.refs_0_, bf16[528,256]{1,0:T(8,128)(2,1)S(1)} %get-tuple-element.50.refs_1_, bf16[528,256]{1,0:T(8,128)(2,1)S(1)} %collective-permute-done.17.refs_2_, bf16[528,256]{1,0:T(8,128)(2,1)} %collective-permute-done.18.refs_3_, ...), custom_call_target="tpu_custom_call" | custom-call | tf_op jit(solution)/shard_map/combine/pallas_call | solution.py:521
  162.0 3.1 %combine.3 = (bf16[2,256,896]{2,1,0:T(8,128)(2,1)}, bf16[4,2,896]{2,1,0:T(2,128)(2,1)}) custom-call(s32[4]{0:T(128)S(1)} %pad_add_fusion.scalars.refs_0_, bf16[528,256]{1,0:T(8,128)(2,1)S(1)} %collective-permute-done.21.refs_1_, bf16[528,256]{1,0:T(8,128)(2,1)S(1)} %collective-permute-done.22.refs_2_, bf16[528,256]{1,0:T(8,128)(2,1)S(1)} %collective-permute-done.23.refs_3_, ...), custom_call_target="tpu_custom_call" | custom-call | tf_op jit(solution)/shard_map/combine/pallas_call | solution.py:521
  (96 shorter events, 24.0 us)
Async XLA Ops:
  0.6 112.6 %copy-start = (f32[4,128]{1,0:T(4,128)S(1)}, f32[4,128]{1,0:T(4,128)}, u32[]{:S(2)}) copy-start(f32[4,128]{1,0:T(4,128)} %param.15) | copy-start | bytes 6148
  0.6 11.3 %copy-start.24 = (s32[3584]{0:T(1024)S(1)}, s32[3584]{0:T(1024)}, u32[]{:S(2)}) copy-start(s32[3584]{0:T(1024)} %refs_1_.3) | copy-start | bytes 43012
  0.7 11.3 %copy-start.23 = (f32[3584]{0:T(1024)S(1)}, f32[3584]{0:T(1024)}, u32[]{:S(2)}) copy-start(f32[3584]{0:T(1024)} %refs_2_.3) | copy-start | bytes 43012
  3.8 49.0 %copy-start.16 = (bf16[5,448,256]{2,1,0:T(8,128)(2,1)}, bf16[5,448,256]{2,1,0:T(8,128)(2,1)S(1)}, u32[]{:S(2)}) copy-start(bf16[5,448,256]{2,1,0:T(8,128)(2,1)S(1)} %get-tuple-element.34.refs_5_) | copy-start | bytes 3440644
  3.8 18.5 %collective-permute-start = (bf16[3,448,256]{2,1,0:T(8,128)(2,1)S(1)}, bf16[3,448,256]{2,1,0:T(8,128)(2,1)}, u32[]{:S(2)}, u32[]{:S(2)}) collective-permute-start(bf16[3,448,256]{2,1,0:T(8,128)(2,1)S(1)} %get-tuple-element.28), channel_id=1, source_target_pairs={{0,16},{1,17},{2,18},{3,19},{4,20},{5,21},{6,22},{7,23},{8,24},{9,... | collective-permute-start | bytes 2064392 | tf_op jit(solution)/shard_map/pre_w/ppermute | solution.py:134
  6.8 20.4 %collective-permute-start.2 = (bf16[5,448,256]{2,1,0:T(8,128)(2,1)S(1)}, bf16[5,448,256]{2,1,0:T(8,128)(2,1)}, u32[]{:S(2)}, u32[]{:S(2)}) collective-permute-start(bf16[5,448,256]{2,1,0:T(8,128)(2,1)S(1)} %get-tuple-element.34.refs_5_), channel_id=1, source_target_pairs={{1,2},{2,1},{5,6},{6,5},{9,10},{10,9},{13,14},{14,13},{17,18},{18,... | collective-permute-start | bytes 3440648 | tf_op jit(solution)/shard_map/mid1_kept/ppermute | solution.py:134
  8.5 29.7 %collective-permute-start.5 = (bf16[5,448,256]{2,1,0:T(8,128)(2,1)S(1)}, bf16[5,448,256]{2,1,0:T(8,128)(2,1)}, u32[]{:S(2)}, u32[]{:S(2)}) collective-permute-start(bf16[5,448,256]{2,1,0:T(8,128)(2,1)S(1)} %get-tuple-element.34.refs_5_), channel_id=1, source_target_pairs={{0,1},{1,0},{2,3},{3,2},{4,5},{5,4},{6,7},{7,6},{8,9},{9,8},{10,11... | collective-permute-start | bytes 3440648 | tf_op jit(solution)/shard_map/pair_kept/ppermute | solution.py:134
  16.9 35.8 %copy-start.22 = (s32[4,2,3584]{2,1,0:T(2,128)S(1)}, s32[4,2,3584]{2,1,0:T(2,128)}, u32[]{:S(2)}) copy-start(s32[4,2,3584]{2,1,0:T(2,128)} %refs_0_) | copy-start | bytes 344068
  22.4 29.0 %collective-permute-start.3 = (bf16[3,448,256]{2,1,0:T(8,128)(2,1)}, bf16[3,448,256]{2,1,0:T(8,128)(2,1)S(1)}, u32[]{:S(2)}, u32[]{:S(2)}) collective-permute-start(bf16[3,448,256]{2,1,0:T(8,128)(2,1)} %collective-permute-done.refs_7_), channel_id=1, source_target_pairs={{0,1},{1,0},{2,3},{3,2},{4,5},{5,4},{6,7},{7,6},{8,9},{9,8},{10,11... | collective-permute-start | bytes 2064392 | tf_op jit(solution)/shard_map/pair_other/ppermute | solution.py:134
  24.2 27.2 %collective-permute-start.4 = (bf16[3,448,256]{2,1,0:T(8,128)(2,1)}, bf16[3,448,256]{2,1,0:T(8,128)(2,1)}, u32[]{:S(2)}, u32[]{:S(2)}) collective-permute-start(bf16[3,448,256]{2,1,0:T(8,128)(2,1)} %collective-permute-done.refs_7_), channel_id=1, source_target_pairs={{1,2},{2,1},{5,6},{6,5},{9,10},{10,9},{13,14},{14,13},{17,18},{18,... | collective-permute-start | bytes 2064392 | tf_op jit(solution)/shard_map/mid1_other/ppermute | solution.py:134
  25.7 40.6 %collective-permute-start.1 = (bf16[4,256,896]{2,1,0:T(8,128)(2,1)S(1)}, bf16[4,256,896]{2,1,0:T(8,128)(2,1)S(1)}, u32[]{:S(2)}, u32[]{:S(2)}) collective-permute-start(bf16[4,256,896]{2,1,0:T(8,128)(2,1)S(1)} %constant_dynamic-slice_fusion.1), channel_id=1, source_target_pairs={{0,16},{1,17},{2,18},{3,19},{4,20},{5,21},{6,22},{7,23},{8,24},{9,... | collective-permute-start | bytes 5505032 | tf_op jit(solution)/shard_map/x_ctx/ppermute | solution.py:134
  38.2 15.8 %collective-permute-start.7 = (bf16[5,448,256]{2,1,0:T(8,128)(2,1)}, bf16[5,448,256]{2,1,0:T(8,128)(2,1)S(1)}, u32[]{:S(2)}, u32[]{:S(2)}) collective-permute-start(bf16[5,448,256]{2,1,0:T(8,128)(2,1)} %collective-permute-done.5.refs_6_), channel_id=1, source_target_pairs={{1,2},{2,1},{5,6},{6,5},{9,10},{10,9},{13,14},{14,13},{17,18},{18,... | collective-permute-start | bytes 3440648 | tf_op jit(solution)/shard_map/mid2_kept/ppermute | solution.py:134
  51.4 30.3 %copy-start.18 = (bf16[3,448,256]{2,1,0:T(8,128)(2,1)}, bf16[3,448,256]{2,1,0:T(8,128)(2,1)S(1)}, u32[]{:S(2)}) copy-start(bf16[3,448,256]{2,1,0:T(8,128)(2,1)S(1)} %collective-permute-done.3.refs_8_) | copy-start | bytes 2064388
  51.4 30.1 %collective-permute-start.6 = (bf16[5,448,256]{2,1,0:T(8,128)(2,1)}, bf16[5,448,256]{2,1,0:T(8,128)(2,1)S(1)}, u32[]{:S(2)}, u32[]{:S(2)}) collective-permute-start(bf16[5,448,256]{2,1,0:T(8,128)(2,1)} %collective-permute-done.2), channel_id=1, source_target_pairs={{1,0},{2,3},{5,4},{6,7},{9,8},{10,11},{13,12},{14,15},{17,16},{18,... | collective-permute-start | bytes 3440648 | tf_op jit(solution)/shard_map/end1_kept/ppermute | solution.py:134
  54.0 49.9 %collective-permute-start.9 = (bf16[5,448,256]{2,1,0:T(8,128)(2,1)S(1)}, bf16[5,448,256]{2,1,0:T(8,128)(2,1)S(1)}, u32[]{:S(2)}, u32[]{:S(2)}) collective-permute-start(bf16[5,448,256]{2,1,0:T(8,128)(2,1)S(1)} %collective-permute-done.7), channel_id=1, source_target_pairs={{1,0},{2,3},{5,4},{6,7},{9,8},{10,11},{13,12},{14,15},{17,16},{18,... | collective-permute-start | bytes 3440648 | tf_op jit(solution)/shard_map/end2_kept/ppermute | solution.py:134
  81.6 32.9 %collective-permute-start.8 = (bf16[4,256,896]{2,1,0:T(8,128)(2,1)S(1)}, bf16[4,256,896]{2,1,0:T(8,128)(2,1)}, u32[]{:S(2)}, u32[]{:S(2)}) collective-permute-start(bf16[4,256,896]{2,1,0:T(8,128)(2,1)S(1)} %collective-permute-done.1.refs_2_), channel_id=1, source_target_pairs={{0,4},{1,5},{2,6},{3,7},{4,0},{5,1},{6,2},{7,3},{8,12},{9,13},{10,... | collective-permute-start | bytes 5505032 | tf_op jit(solution)/shard_map/x_core/ppermute | solution.py:134
  81.7 3.9 %collective-permute-start.10 = (bf16[3,448,256]{2,1,0:T(8,128)(2,1)S(1)}, bf16[3,448,256]{2,1,0:T(8,128)(2,1)}, u32[]{:S(2)}, u32[]{:S(2)}) collective-permute-start(bf16[3,448,256]{2,1,0:T(8,128)(2,1)S(1)} %collective-permute-done.3.refs_8_), channel_id=1, source_target_pairs={{1,2},{2,1},{5,6},{6,5},{9,10},{10,9},{13,14},{14,13},{17,18},{18,... | collective-permute-start | bytes 2064392 | tf_op jit(solution)/shard_map/mid2_other/ppermute | solution.py:134
  83.2 22.7 %collective-permute-start.13 = (bf16[2,2,448,256]{3,2,1,0:T(8,128)(2,1)S(1)}, bf16[2,2,448,256]{3,2,1,0:T(8,128)(2,1)S(1)}, u32[]{:S(2)}, u32[]{:S(2)}) collective-permute-start(bf16[2,2,448,256]{3,2,1,0:T(8,128)(2,1)S(1)} %pad_maximum_fusion.refs_12_.refs_0_), channel_id=1, source_target_pairs={{0,16},{1,17},{2,18},{3,19},{4,20},{5,21},{6,22},{7,23},{8,0},{9,1... | collective-permute-start | bytes 2752520 | tf_op jit(solution)/shard_map/near_meet/ppermute | solution.py:134
  83.8 23.1 %collective-permute-start.14 = (bf16[2,2,448,256]{3,2,1,0:T(8,128)(2,1)S(1)}, bf16[2,2,448,256]{3,2,1,0:T(8,128)(2,1)S(1)}, u32[]{:S(2)}, u32[]{:S(2)}) collective-permute-start(bf16[2,2,448,256]{3,2,1,0:T(8,128)(2,1)S(1)} %pad_maximum_fusion.refs_12_.refs_0_), channel_id=1, source_target_pairs={{8,16},{9,17},{10,18},{11,19},{12,20},{13,21},{14,22},{15,23},{16,... | collective-permute-start | bytes 2752520 | tf_op jit(solution)/shard_map/near_corner/ppermute | solution.py:134
  85.6 42.4 %collective-permute-start.12 = (bf16[3,448,256]{2,1,0:T(8,128)(2,1)}, bf16[3,448,256]{2,1,0:T(8,128)(2,1)}, u32[]{:S(2)}, u32[]{:S(2)}) collective-permute-start(bf16[3,448,256]{2,1,0:T(8,128)(2,1)} %collective-permute-done.4), channel_id=1, source_target_pairs={{1,0},{2,3},{5,4},{6,7},{9,8},{10,11},{13,12},{14,15},{17,16},{18,... | collective-permute-start | bytes 2064392 | tf_op jit(solution)/shard_map/end1_other/ppermute | solution.py:134
  107.8 26.1 %collective-permute-start.15 = (bf16[2,2,448,256]{3,2,1,0:T(8,128)(2,1)}, bf16[2,2,448,256]{3,2,1,0:T(8,128)(2,1)}, u32[]{:S(2)}, u32[]{:S(2)}) collective-permute-start(bf16[2,2,448,256]{3,2,1,0:T(8,128)(2,1)} %pad_maximum_fusion.1.refs_15_.refs_3_), channel_id=1, source_target_pairs={{0,16},{1,17},{2,18},{3,19},{4,20},{5,21},{6,22},{7,23},{8,0},{9,1... | collective-permute-start | bytes 2752520 | tf_op jit(solution)/shard_map/far_meet/ppermute | solution.py:134
  111.5 22.5 %collective-permute-start.16 = (bf16[2,2,448,256]{3,2,1,0:T(8,128)(2,1)}, bf16[2,2,448,256]{3,2,1,0:T(8,128)(2,1)}, u32[]{:S(2)}, u32[]{:S(2)}) collective-permute-start(bf16[2,2,448,256]{3,2,1,0:T(8,128)(2,1)} %pad_maximum_fusion.1.refs_15_.refs_3_), channel_id=1, source_target_pairs={{8,16},{9,17},{10,18},{11,19},{12,20},{13,21},{14,22},{15,23},{16,... | collective-permute-start | bytes 2752520 | tf_op jit(solution)/shard_map/far_corner/ppermute | solution.py:134
  113.3 20.7 %collective-permute-start.11 = (bf16[3,448,256]{2,1,0:T(8,128)(2,1)}, bf16[3,448,256]{2,1,0:T(8,128)(2,1)S(1)}, u32[]{:S(2)}, u32[]{:S(2)}) collective-permute-start(bf16[3,448,256]{2,1,0:T(8,128)(2,1)} %collective-permute-done.10.refs_6_), channel_id=1, source_target_pairs={{1,0},{2,3},{5,4},{6,7},{9,8},{10,11},{13,12},{14,15},{17,16},{18,... | collective-permute-start | bytes 2064392 | tf_op jit(solution)/shard_map/end2_other/ppermute | solution.py:134
  141.1 4.1 %collective-permute-start.20 = (bf16[2,2,2,448,256]{4,3,2,1,0:T(8,128)(2,1)}, bf16[2,2,2,448,256]{4,3,2,1,0:T(8,128)(2,1)S(1)}, u32[]{:S(2)}, u32[]{:S(2)}) collective-permute-start(bf16[2,2,2,448,256]{4,3,2,1,0:T(8,128)(2,1)} %get-tuple-element.49), channel_id=1, source_target_pairs={{0,4},{1,5},{2,6},{3,7},{4,0},{5,1},{6,2},{7,3},{8,12},{9,13},{10,... | collective-permute-start | bytes 5505032 | tf_op jit(solution)/shard_map/out_core/ppermute | solution.py:134
  141.2 9.6 %collective-permute-start.17 = (bf16[528,256]{1,0:T(8,128)(2,1)}, bf16[528,256]{1,0:T(8,128)(2,1)S(1)}, u32[]{:S(2)}, u32[]{:S(2)}) collective-permute-start(bf16[528,256]{1,0:T(8,128)(2,1)} %get-tuple-element.48), channel_id=1, source_target_pairs={{0,16},{1,17},{2,18},{3,19},{4,20},{5,21},{6,22},{7,23},{8,24},{9,... | collective-permute-start | bytes 811016 | tf_op jit(solution)/shard_map/h_ctx/ppermute | solution.py:134
  143.3 9.1 %collective-permute-start.18 = (bf16[528,256]{1,0:T(8,128)(2,1)S(1)}, bf16[528,256]{1,0:T(8,128)(2,1)}, u32[]{:S(2)}, u32[]{:S(2)}) collective-permute-start(bf16[528,256]{1,0:T(8,128)(2,1)S(1)} %get-tuple-element.50.refs_1_), channel_id=1, source_target_pairs={{0,8},{1,9},{2,10},{3,11},{4,12},{5,13},{6,14},{7,15},{8,0},{9,1},... | collective-permute-start | bytes 811016 | tf_op jit(solution)/shard_map/h_y/ppermute | solution.py:134
  143.4 14.4 %collective-permute-start.19 = (bf16[528,256]{1,0:T(8,128)(2,1)}, bf16[528,256]{1,0:T(8,128)(2,1)}, u32[]{:S(2)}, u32[]{:S(2)}) collective-permute-start(bf16[528,256]{1,0:T(8,128)(2,1)} %get-tuple-element.48), channel_id=1, source_target_pairs={{0,24},{1,25},{2,26},{3,27},{4,28},{5,29},{6,30},{7,31},{8,16},{9,... | collective-permute-start | bytes 811016 | tf_op jit(solution)/shard_map/h_diag/ppermute | solution.py:134
  148.8 13.1 %copy-start.9 = (bf16[2,256,896]{2,1,0:T(8,128)(2,1)S(1)}, bf16[2,256,896]{2,1,0:T(8,128)(2,1)}, u32[]{:S(2)}) copy-start(bf16[2,256,896]{2,1,0:T(8,128)(2,1)} %fusion.2.refs_7_) | copy-start | bytes 2752516
  157.8 4.2 %collective-permute-start.21 = (bf16[528,256]{1,0:T(8,128)(2,1)S(1)}, bf16[528,256]{1,0:T(8,128)(2,1)S(1)}, u32[]{:S(2)}, u32[]{:S(2)}) collective-permute-start(bf16[528,256]{1,0:T(8,128)(2,1)S(1)} %get-tuple-element.50.refs_1_), channel_id=1, source_target_pairs={{0,4},{1,5},{2,6},{3,7},{4,0},{5,1},{6,2},{7,3},{8,12},{9,13},{10,... | collective-permute-start | bytes 811016 | tf_op jit(solution)/shard_map/h_core/ppermute | solution.py:134
  157.8 4.2 %collective-permute-start.22 = (bf16[528,256]{1,0:T(8,128)(2,1)S(1)}, bf16[528,256]{1,0:T(8,128)(2,1)S(1)}, u32[]{:S(2)}, u32[]{:S(2)}) collective-permute-start(bf16[528,256]{1,0:T(8,128)(2,1)S(1)} %collective-permute-done.17.refs_2_), channel_id=1, source_target_pairs={{0,4},{1,5},{2,6},{3,7},{4,0},{5,1},{6,2},{7,3},{8,12},{9,13},{10,... | collective-permute-start | bytes 811016 | tf_op jit(solution)/shard_map/h_core/ppermute | solution.py:134
  158.3 3.7 %collective-permute-start.23 = (bf16[528,256]{1,0:T(8,128)(2,1)}, bf16[528,256]{1,0:T(8,128)(2,1)S(1)}, u32[]{:S(2)}, u32[]{:S(2)}) collective-permute-start(bf16[528,256]{1,0:T(8,128)(2,1)} %collective-permute-done.18.refs_3_), channel_id=1, source_target_pairs={{0,4},{1,5},{2,6},{3,7},{4,0},{5,1},{6,2},{7,3},{8,12},{9,13},{10,... | collective-permute-start | bytes 811016 | tf_op jit(solution)/shard_map/h_core/ppermute | solution.py:134
  158.3 3.7 %collective-permute-start.24 = (bf16[528,256]{1,0:T(8,128)(2,1)}, bf16[528,256]{1,0:T(8,128)(2,1)S(1)}, u32[]{:S(2)}, u32[]{:S(2)}) collective-permute-start(bf16[528,256]{1,0:T(8,128)(2,1)} %collective-permute-done.19.refs_4_), channel_id=1, source_target_pairs={{0,4},{1,5},{2,6},{3,7},{4,0},{5,1},{6,2},{7,3},{8,12},{9,13},{10,... | collective-permute-start | bytes 811016 | tf_op jit(solution)/shard_map/h_core/ppermute | solution.py:134
  (19 other events, 47.7 us)

commit v7 on v6

--- a/solution.py
+++ b/solution.py
@@ -584,7 +584,7 @@
     mid2_other = move(after(pair_other, *stage), mid_swap, "mid2_other")
     end1_other = move(after(mid1_other, mid2_other), mid_to_end, "end1_other")
     third_kept = jnp.where(is_end, after(end1_kept, *stage), mid1_kept)
-    second_x = move(after(first_x, third_kept), to_core, "x_core")
+    second_x = move(after(first_x, mid2_kept), to_core, "x_core")
     xs = (own_x, first_x, second_x, dec_x)
     summed = project(scalars, 0, xs, (kept, pair_kept), (other, pair_other), None)
 
@@ -615,9 +615,9 @@
     own_rows, far_rows, passed = attend(
         scalars, xs, (fourth_kept,), (mid2_other, end2_other), summed, prior_state, gain, lengths, near + far, dims
     )
+    h_diag = move(far_rows, to_diagonal, "h_diag")
     h_ctx = move(far_rows, to_ctx, "h_ctx")
     h_y = move(own_rows, to_y, "h_y")
-    h_diag = move(far_rows, to_diagonal, "h_diag")
     mine = [own_rows, h_ctx, h_y, h_diag]
     weights = lay(flags, *near, *far, move(passed, to_core, "out_core"))
     mine = [own_rows, h_ctx, h_y, h_diag]

time: 166 us -> 165 us (level)
  starting transfers between devices: 31.7 us -> 25.8 us
  waiting for transfers between devices: 81 us -> 84.9 us
    ppermute x25, starting transfers between devices: 31.7 us -> 25.8 us  [move(): return lax.ppermute(value, AXES, pairs)]
    ppermute x25, waiting for transfers between devices: 81 us -> 84.9 us  [move(): return lax.ppermute(value, AXES, pairs)]
    unnamed x52 -> x56, local copies, waits for them, and re-layouts: 16.8 us -> 16.8 us
  transfers between devices with their start and end apart: 25 -> 25, of which waited for: 12 -> 10; matrix products, arithmetic and copies ran while one was open for 4% -> 4% of each run, Pallas kernels for 10% -> 10%
where the time goes in v7:
time: 165 us; the launch traced here: 164 us
  waiting for transfers between devices  84.9 us (51%)
  Pallas kernels  27.8 us (17%)
  starting transfers between devices  25.8 us (16%)
  local copies, waits for them, and re-layouts  18.4 us (11%)
  other arithmetic  5.55 us (3%)
    ppermute x25, waiting for transfers between devices, move(): return lax.ppermute(value, AXES, pairs)  84.9 us
    ppermute x25, starting transfers between devices, move(): return lax.ppermute(value, AXES, pairs)  25.8 us
    unnamed x56, local copies, waits for them, and re-layouts  16.8 us
    pallas_call x2, Pallas kernels, project(): pl.pallas_call(lambda *refs: project_kernel(steps, bool(earlier), *refs),...  10 us
    pallas_call x1, Pallas kernels, attend(): pl.pallas_call(lambda *refs: attend_kernel(dims, *refs), grid_spec=pltpu....  7.66 us
    pallas_call x2, Pallas kernels, combine(): pl.pallas_call(lambda *refs: combine_kernel(bool(rest), *refs), grid_spec...  6.25 us
  transfers between devices with their start and end apart: 25, of which 10 were waited for; matrix products, arithmetic and copies ran while one was open for 4% of the time, Pallas kernels for 10%

profile of v7, /device:TPU:0, one launch (start us, length us, event | category | flops | bytes accessed | tf_op | source)
XLA Modules:
  0.0 163.7 jit_solution(17147955891019606997)
XLA Ops:
  0.8 1.3 copy-done.8
  3.8 3.0 %collective-permute-start = (bf16[3,448,256]{2,1,0:T(8,128)(2,1)S(1)}, bf16[3,448,256]{2,1,0:T(8,128)(2,1)}, u32[]{:S(2)}, u32[]{:S(2)}) collective-permute-start(bf16[3,448,256]{2,1,0:T(8,128)(2,1)S(1)} %get-tuple-element.28), channel_id=1, source_target_pairs={{0,16},{1,17},{2,18},{3,19},{4,20},{5,21},{6,22},{7,23},{8,24},{9,... | collective-permute-start | bytes 2064392 | tf_op jit(solution)/shard_map/pre_w/ppermute | solution.py:134
  6.8 1.6 collective-permute-start.2
  8.4 1.7 %collective-permute-start.3 = (bf16[5,448,256]{2,1,0:T(8,128)(2,1)S(1)}, bf16[5,448,256]{2,1,0:T(8,128)(2,1)}, u32[]{:S(2)}, u32[]{:S(2)}) collective-permute-start(bf16[5,448,256]{2,1,0:T(8,128)(2,1)S(1)} %get-tuple-element.34.refs_5_), channel_id=1, source_target_pairs={{1,2},{2,1},{5,6},{6,5},{9,10},{10,9},{13,14},{14,13},{17,18},{18,... | collective-permute-start | bytes 3440648 | tf_op jit(solution)/shard_map/mid1_kept/ppermute | solution.py:134
  10.1 3.1 %copy-done.3 = s32[2,256,3584]{2,1,0:T(8,128)S(1)} copy-done((s32[2,256,3584]{2,1,0:T(8,128)S(1)}, s32[2,256,3584]{2,1,0:T(8,128)}, u32[]{:S(2)}) %copy-start.3) | copy-done | bytes 7340056
  13.3 1.8 %embed.1.refs_1_ = bf16[4,512,896]{2,1,0:T(8,128)(2,1)S(1)} custom-call(s32[512,3584]{1,0:T(8,128)S(1)} %bitcast.20, s32[3584]{0:T(1024)S(1)} %copy-done.26, f32[3584]{0:T(1024)S(1)} %copy-done.25), custom_call_target="tpu_custom_call" | custom-call | tf_op jit(solution)/shard_map/embed/pallas_call | solution.py:246
  15.3 1.6 copy-done.1
  16.9 5.5 %collective-permute-done.refs_7_ = bf16[3,448,256]{2,1,0:T(8,128)(2,1)} collective-permute-done((bf16[3,448,256]{2,1,0:T(8,128)(2,1)S(1)}, bf16[3,448,256]{2,1,0:T(8,128)(2,1)}, u32[]{:S(2)}, u32[]{:S(2)}) %collective-permute-start) | collective-permute-done | bytes 688160 | tf_op jit(solution)/shard_map/pre_w/ppermute | solution.py:134
  22.4 1.7 %collective-permute-start.1 = (bf16[4,256,896]{2,1,0:T(8,128)(2,1)S(1)}, bf16[4,256,896]{2,1,0:T(8,128)(2,1)S(1)}, u32[]{:S(2)}, u32[]{:S(2)}) collective-permute-start(bf16[4,256,896]{2,1,0:T(8,128)(2,1)S(1)} %constant_dynamic-slice_fusion.1), channel_id=1, source_target_pairs={{0,16},{1,17},{2,18},{3,19},{4,20},{5,21},{6,22},{7,23},{8,24},{9,... | collective-permute-start | bytes 5505032 | tf_op jit(solution)/shard_map/x_ctx/ppermute | solution.py:134
  24.1 1.6 collective-permute-start.7
  25.7 1.5 collective-permute-start.8
  27.2 7.9 %collective-permute-done.2.refs_6_ = bf16[5,448,256]{2,1,0:T(8,128)(2,1)} collective-permute-done((bf16[5,448,256]{2,1,0:T(8,128)(2,1)S(1)}, bf16[5,448,256]{2,1,0:T(8,128)(2,1)}, u32[]{:S(2)}, u32[]{:S(2)}) %collective-permute-start.2) | collective-permute-done | bytes 1146912 | tf_op jit(solution)/shard_map/pair_kept/ppermute | solution.py:134
  35.9 12.4 %collective-permute-done.7.refs_8_ = bf16[3,448,256]{2,1,0:T(8,128)(2,1)S(1)} collective-permute-done((bf16[3,448,256]{2,1,0:T(8,128)(2,1)}, bf16[3,448,256]{2,1,0:T(8,128)(2,1)S(1)}, u32[]{:S(2)}, u32[]{:S(2)}) %collective-permute-start.7) | collective-permute-done | bytes 688160 | tf_op jit(solution)/shard_map/pair_other/ppermute | solution.py:134
  48.3 1.3 collective-permute-start.9
  50.9 1.3 collective-permute-start.6
  52.2 11.3 %collective-permute-done.1.refs_2_ = bf16[4,256,896]{2,1,0:T(8,128)(2,1)S(1)} collective-permute-done((bf16[4,256,896]{2,1,0:T(8,128)(2,1)S(1)}, bf16[4,256,896]{2,1,0:T(8,128)(2,1)S(1)}, u32[]{:S(2)}, u32[]{:S(2)}) %collective-permute-start.1) | collective-permute-done | bytes 1835040 | tf_op jit(solution)/shard_map/x_ctx/ppermute | solution.py:134
  63.6 15.2 %collective-permute-done.9 = bf16[5,448,256]{2,1,0:T(8,128)(2,1)S(1)} collective-permute-done((bf16[5,448,256]{2,1,0:T(8,128)(2,1)}, bf16[5,448,256]{2,1,0:T(8,128)(2,1)S(1)}, u32[]{:S(2)}, u32[]{:S(2)}) %collective-permute-start.9) | collective-permute-done | bytes 1146912 | tf_op jit(solution)/shard_map/end1_kept/ppermute | solution.py:134
  82.1 1.3 collective-permute-start.12
  83.4 21.5 %collective-permute-done.6 = bf16[5,448,256]{2,1,0:T(8,128)(2,1)S(1)} collective-permute-done((bf16[5,448,256]{2,1,0:T(8,128)(2,1)S(1)}, bf16[5,448,256]{2,1,0:T(8,128)(2,1)S(1)}, u32[]{:S(2)}, u32[]{:S(2)}) %collective-permute-start.6) | collective-permute-done | bytes 1146912 | tf_op jit(solution)/shard_map/end2_kept/ppermute | solution.py:134
  108.6 1.7 %collective-permute-start.16 = (bf16[2,2,448,256]{3,2,1,0:T(8,128)(2,1)}, bf16[2,2,448,256]{3,2,1,0:T(8,128)(2,1)}, u32[]{:S(2)}, u32[]{:S(2)}) collective-permute-start(bf16[2,2,448,256]{3,2,1,0:T(8,128)(2,1)} %pad_maximum_fusion.1.refs_15_.refs_3_), channel_id=1, source_target_pairs={{8,16},{9,17},{10,18},{11,19},{12,20},{13,21},{14,22},{15,23},{16,... | collective-permute-start | bytes 2752520 | tf_op jit(solution)/shard_map/far_corner/ppermute | solution.py:134
  111.7 2.0 %copy-done.2 = bf16[4,512,896]{2,1,0:T(8,128)(2,1)S(1)} copy-done((bf16[4,512,896]{2,1,0:T(8,128)(2,1)S(1)}, bf16[4,512,896]{2,1,0:T(8,128)(2,1)}, u32[]{:S(2)}) %copy-start.2) | copy-done | bytes 3670040
  116.1 6.1 %project.2.refs_7_ = f32[1040,768]{1,0:T(8,128)S(1)} custom-call(s32[9]{0:T(128)S(1)} %stack.80.scalars.refs_0_, bf16[4,512,896]{2,1,0:T(8,128)(2,1)S(1)} %copy-done.2, bf16[4,256,896]{2,1,0:T(8,128)(2,1)S(1)} %collective-permute-done.1.refs_2_, bf16[4,256,896]{2,1,0:T(8,128)(2,1)} %collective-permute-done.5.refs_3_, ...), custom_call_target="tpu_custom_call" | custom-call | tf_op jit(solution)/shard_map/project/pallas_call | solution.py:305
  122.3 2.8 %fusion.2.refs_7_ = bf16[2,256,896]{2,1,0:T(8,128)(2,1)} fusion(s32[2,256,3584]{2,1,0:T(8,128)} %param.9, s32[]{:T(128)S(6)} %select_n.60, f32[896]{0:T(1024)S(1)} %dynamic_slice.23, s32[896]{0:T(1024)S(1)} %dynamic_slice.22), kind=kLoop, calls=%fused_computation.3 | loop fusion | flops 2293760 | bytes 2759684 | tf_op jit(solution)/shard_map/convert_element_type | solution.py:602
  126.4 3.9 %project.3.refs_8_ = f32[1040,768]{1,0:T(8,128)S(1)} custom-call(s32[9]{0:T(128)S(1)} %stack.80.scalars.refs_0_, bf16[4,512,896]{2,1,0:T(8,128)(2,1)S(1)} %copy-done.2, bf16[4,256,896]{2,1,0:T(8,128)(2,1)S(1)} %collective-permute-done.1.refs_2_, bf16[4,256,896]{2,1,0:T(8,128)(2,1)} %collective-permute-done.5.refs_3_, ...), custom_call_target="tpu_custom_call" | custom-call | tf_op jit(solution)/shard_map/project/pallas_call | solution.py:305
  130.2 2.4 %collective-permute-done.11.refs_7_ = bf16[3,448,256]{2,1,0:T(8,128)(2,1)S(1)} collective-permute-done((bf16[3,448,256]{2,1,0:T(8,128)(2,1)}, bf16[3,448,256]{2,1,0:T(8,128)(2,1)S(1)}, u32[]{:S(2)}, u32[]{:S(2)}) %collective-permute-start.11) | collective-permute-done | bytes 688160 | tf_op jit(solution)/shard_map/end2_other/ppermute | solution.py:134
  132.7 7.7 %attend.1 = (bf16[528,256]{1,0:T(8,128)(2,1)S(1)}, bf16[528,256]{1,0:T(8,128)(2,1)}, bf16[2,2,2,448,256]{4,3,2,1,0:T(8,128)(2,1)}) custom-call(s32[9]{0:T(128)S(1)} %stack.80.scalars.refs_0_, bf16[4,512,896]{2,1,0:T(8,128)(2,1)S(1)} %copy-done.2, bf16[4,256,896]{2,1,0:T(8,128)(2,1)S(1)} %collective-permute-done.1.refs_2_, ...), custom_call_target="tpu_custom_call" | custom-call | flops 2862612480 | bytes 3194880 | tf_op jit(solution)/shard_map/attend/pallas_call | solution.py:420
  141.2 1.3 collective-permute-start.18
  142.5 1.4 collective-permute-start.19
  148.0 2.0 %collective-permute-done.17.refs_2_ = bf16[528,256]{1,0:T(8,128)(2,1)S(1)} collective-permute-done((bf16[528,256]{1,0:T(8,128)(2,1)}, bf16[528,256]{1,0:T(8,128)(2,1)S(1)}, u32[]{:S(2)}, u32[]{:S(2)}) %collective-permute-start.17) | collective-permute-done | bytes 270368 | tf_op jit(solution)/shard_map/h_ctx/ppermute | solution.py:134
  150.0 6.3 %collective-permute-done.19.refs_4_ = bf16[528,256]{1,0:T(8,128)(2,1)} collective-permute-done((bf16[528,256]{1,0:T(8,128)(2,1)}, bf16[528,256]{1,0:T(8,128)(2,1)}, u32[]{:S(2)}, u32[]{:S(2)}) %collective-permute-start.19) | collective-permute-done | bytes 270368 | tf_op jit(solution)/shard_map/h_diag/ppermute | solution.py:134
  157.3 3.1 %combine.2.refs_6_ = f32[528,896]{1,0:T(8,128)S(1)} custom-call(s32[4]{0:T(128)S(1)} %pad_add_fusion.scalars.refs_0_, bf16[528,256]{1,0:T(8,128)(2,1)S(1)} %get-tuple-element.50.refs_1_, bf16[528,256]{1,0:T(8,128)(2,1)S(1)} %collective-permute-done.17.refs_2_, bf16[528,256]{1,0:T(8,128)(2,1)} %collective-permute-done.18.refs_3_, ...), custom_call_target="tpu_custom_call" | custom-call | tf_op jit(solution)/shard_map/combine/pallas_call | solution.py:521
  160.4 3.1 %combine.3 = (bf16[2,256,896]{2,1,0:T(8,128)(2,1)}, bf16[4,2,896]{2,1,0:T(2,128)(2,1)}) custom-call(s32[4]{0:T(128)S(1)} %pad_add_fusion.scalars.refs_0_, bf16[528,256]{1,0:T(8,128)(2,1)S(1)} %collective-permute-done.21.refs_1_, bf16[528,256]{1,0:T(8,128)(2,1)S(1)} %collective-permute-done.22.refs_2_, bf16[528,256]{1,0:T(8,128)(2,1)S(1)} %collective-permute-done.23.refs_3_, ...), custom_call_target="tpu_custom_call" | custom-call | tf_op jit(solution)/shard_map/combine/pallas_call | solution.py:521
  (100 shorter events, 21.9 us)
Async XLA Ops:
  0.6 109.8 %copy-start = (f32[4,128]{1,0:T(4,128)S(1)}, f32[4,128]{1,0:T(4,128)}, u32[]{:S(2)}) copy-start(f32[4,128]{1,0:T(4,128)} %param.15) | copy-start | bytes 6148
  0.6 9.5 %copy-start.26 = (s32[3584]{0:T(1024)S(1)}, s32[3584]{0:T(1024)}, u32[]{:S(2)}) copy-start(s32[3584]{0:T(1024)} %refs_1_.3) | copy-start | bytes 43012
  3.8 45.9 %copy-start.16 = (bf16[5,448,256]{2,1,0:T(8,128)(2,1)}, bf16[5,448,256]{2,1,0:T(8,128)(2,1)S(1)}, u32[]{:S(2)}) copy-start(bf16[5,448,256]{2,1,0:T(8,128)(2,1)S(1)} %get-tuple-element.34.refs_5_) | copy-start | bytes 3440644
  3.8 18.5 %collective-permute-start = (bf16[3,448,256]{2,1,0:T(8,128)(2,1)S(1)}, bf16[3,448,256]{2,1,0:T(8,128)(2,1)}, u32[]{:S(2)}, u32[]{:S(2)}) collective-permute-start(bf16[3,448,256]{2,1,0:T(8,128)(2,1)S(1)} %get-tuple-element.28), channel_id=1, source_target_pairs={{0,16},{1,17},{2,18},{3,19},{4,20},{5,21},{6,22},{7,23},{8,24},{9,... | collective-permute-start | bytes 2064392 | tf_op jit(solution)/shard_map/pre_w/ppermute | solution.py:134
  6.8 28.3 %collective-permute-start.2 = (bf16[5,448,256]{2,1,0:T(8,128)(2,1)S(1)}, bf16[5,448,256]{2,1,0:T(8,128)(2,1)}, u32[]{:S(2)}, u32[]{:S(2)}) collective-permute-start(bf16[5,448,256]{2,1,0:T(8,128)(2,1)S(1)} %get-tuple-element.34.refs_5_), channel_id=1, source_target_pairs={{0,1},{1,0},{2,3},{3,2},{4,5},{5,4},{6,7},{7,6},{8,9},{9,8},{10,11... | collective-permute-start | bytes 3440648 | tf_op jit(solution)/shard_map/pair_kept/ppermute | solution.py:134
  8.4 26.7 %collective-permute-start.3 = (bf16[5,448,256]{2,1,0:T(8,128)(2,1)S(1)}, bf16[5,448,256]{2,1,0:T(8,128)(2,1)}, u32[]{:S(2)}, u32[]{:S(2)}) collective-permute-start(bf16[5,448,256]{2,1,0:T(8,128)(2,1)S(1)} %get-tuple-element.34.refs_5_), channel_id=1, source_target_pairs={{1,2},{2,1},{5,6},{6,5},{9,10},{10,9},{13,14},{14,13},{17,18},{18,... | collective-permute-start | bytes 3440648 | tf_op jit(solution)/shard_map/mid1_kept/ppermute | solution.py:134
  15.1 34.5 %copy-start.24 = (s32[4,2,3584]{2,1,0:T(2,128)S(1)}, s32[4,2,3584]{2,1,0:T(2,128)}, u32[]{:S(2)}) copy-start(s32[4,2,3584]{2,1,0:T(2,128)} %refs_0_) | copy-start | bytes 344068
  22.4 41.2 %collective-permute-start.1 = (bf16[4,256,896]{2,1,0:T(8,128)(2,1)S(1)}, bf16[4,256,896]{2,1,0:T(8,128)(2,1)S(1)}, u32[]{:S(2)}, u32[]{:S(2)}) collective-permute-start(bf16[4,256,896]{2,1,0:T(8,128)(2,1)S(1)} %constant_dynamic-slice_fusion.1), channel_id=1, source_target_pairs={{0,16},{1,17},{2,18},{3,19},{4,20},{5,21},{6,22},{7,23},{8,24},{9,... | collective-permute-start | bytes 5505032 | tf_op jit(solution)/shard_map/x_ctx/ppermute | solution.py:134
  24.1 24.2 %collective-permute-start.7 = (bf16[3,448,256]{2,1,0:T(8,128)(2,1)}, bf16[3,448,256]{2,1,0:T(8,128)(2,1)S(1)}, u32[]{:S(2)}, u32[]{:S(2)}) collective-permute-start(bf16[3,448,256]{2,1,0:T(8,128)(2,1)} %collective-permute-done.refs_7_), channel_id=1, source_target_pairs={{0,1},{1,0},{2,3},{3,2},{4,5},{5,4},{6,7},{7,6},{8,9},{9,8},{10,11... | collective-permute-start | bytes 2064392 | tf_op jit(solution)/shard_map/pair_other/ppermute | solution.py:134
  25.7 22.6 %collective-permute-start.8 = (bf16[3,448,256]{2,1,0:T(8,128)(2,1)}, bf16[3,448,256]{2,1,0:T(8,128)(2,1)}, u32[]{:S(2)}, u32[]{:S(2)}) collective-permute-start(bf16[3,448,256]{2,1,0:T(8,128)(2,1)} %collective-permute-done.refs_7_), channel_id=1, source_target_pairs={{1,2},{2,1},{5,6},{6,5},{9,10},{10,9},{13,14},{14,13},{17,18},{18,... | collective-permute-start | bytes 2064392 | tf_op jit(solution)/shard_map/mid1_other/ppermute | solution.py:134
  35.1 15.8 %collective-permute-start.4 = (bf16[5,448,256]{2,1,0:T(8,128)(2,1)}, bf16[5,448,256]{2,1,0:T(8,128)(2,1)S(1)}, u32[]{:S(2)}, u32[]{:S(2)}) collective-permute-start(bf16[5,448,256]{2,1,0:T(8,128)(2,1)} %collective-permute-done.2.refs_6_), channel_id=1, source_target_pairs={{1,2},{2,1},{5,6},{6,5},{9,10},{10,9},{13,14},{14,13},{17,18},{18,... | collective-permute-start | bytes 3440648 | tf_op jit(solution)/shard_map/mid2_kept/ppermute | solution.py:134
  48.3 30.5 %copy-start.20 = (bf16[3,448,256]{2,1,0:T(8,128)(2,1)}, bf16[3,448,256]{2,1,0:T(8,128)(2,1)S(1)}, u32[]{:S(2)}) copy-start(bf16[3,448,256]{2,1,0:T(8,128)(2,1)S(1)} %collective-permute-done.7.refs_8_) | copy-start | bytes 2064388
  48.3 30.5 %collective-permute-start.9 = (bf16[5,448,256]{2,1,0:T(8,128)(2,1)}, bf16[5,448,256]{2,1,0:T(8,128)(2,1)S(1)}, u32[]{:S(2)}, u32[]{:S(2)}) collective-permute-start(bf16[5,448,256]{2,1,0:T(8,128)(2,1)} %collective-permute-done.3), channel_id=1, source_target_pairs={{1,0},{2,3},{5,4},{6,7},{9,8},{10,11},{13,12},{14,15},{17,16},{18,... | collective-permute-start | bytes 3440648 | tf_op jit(solution)/shard_map/end1_kept/ppermute | solution.py:134
  50.9 54.0 %collective-permute-start.6 = (bf16[5,448,256]{2,1,0:T(8,128)(2,1)S(1)}, bf16[5,448,256]{2,1,0:T(8,128)(2,1)S(1)}, u32[]{:S(2)}, u32[]{:S(2)}) collective-permute-start(bf16[5,448,256]{2,1,0:T(8,128)(2,1)S(1)} %collective-permute-done.4), channel_id=1, source_target_pairs={{1,0},{2,3},{5,4},{6,7},{9,8},{10,11},{13,12},{14,15},{17,16},{18,... | collective-permute-start | bytes 3440648 | tf_op jit(solution)/shard_map/end2_kept/ppermute | solution.py:134
  63.6 48.1 %collective-permute-start.5 = (bf16[4,256,896]{2,1,0:T(8,128)(2,1)S(1)}, bf16[4,256,896]{2,1,0:T(8,128)(2,1)}, u32[]{:S(2)}, u32[]{:S(2)}) collective-permute-start(bf16[4,256,896]{2,1,0:T(8,128)(2,1)S(1)} %collective-permute-done.1.refs_2_), channel_id=1, source_target_pairs={{0,4},{1,5},{2,6},{3,7},{4,0},{5,1},{6,2},{7,3},{8,12},{9,13},{10,... | collective-permute-start | bytes 5505032 | tf_op jit(solution)/shard_map/x_core/ppermute | solution.py:134
  78.8 3.3 %collective-permute-start.10 = (bf16[3,448,256]{2,1,0:T(8,128)(2,1)S(1)}, bf16[3,448,256]{2,1,0:T(8,128)(2,1)S(1)}, u32[]{:S(2)}, u32[]{:S(2)}) collective-permute-start(bf16[3,448,256]{2,1,0:T(8,128)(2,1)S(1)} %collective-permute-done.7.refs_8_), channel_id=1, source_target_pairs={{1,2},{2,1},{5,6},{6,5},{9,10},{10,9},{13,14},{14,13},{17,18},{18,... | collective-permute-start | bytes 2064392 | tf_op jit(solution)/shard_map/mid2_other/ppermute | solution.py:134
  79.6 26.6 %collective-permute-start.13 = (bf16[2,2,448,256]{3,2,1,0:T(8,128)(2,1)S(1)}, bf16[2,2,448,256]{3,2,1,0:T(8,128)(2,1)S(1)}, u32[]{:S(2)}, u32[]{:S(2)}) collective-permute-start(bf16[2,2,448,256]{3,2,1,0:T(8,128)(2,1)S(1)} %pad_maximum_fusion.refs_12_.refs_0_), channel_id=1, source_target_pairs={{0,16},{1,17},{2,18},{3,19},{4,20},{5,21},{6,22},{7,23},{8,0},{9,1... | collective-permute-start | bytes 2752520 | tf_op jit(solution)/shard_map/near_meet/ppermute | solution.py:134
  80.2 26.9 %collective-permute-start.14 = (bf16[2,2,448,256]{3,2,1,0:T(8,128)(2,1)S(1)}, bf16[2,2,448,256]{3,2,1,0:T(8,128)(2,1)S(1)}, u32[]{:S(2)}, u32[]{:S(2)}) collective-permute-start(bf16[2,2,448,256]{3,2,1,0:T(8,128)(2,1)S(1)} %pad_maximum_fusion.refs_12_.refs_0_), channel_id=1, source_target_pairs={{8,16},{9,17},{10,18},{11,19},{12,20},{13,21},{14,22},{15,23},{16,... | collective-permute-start | bytes 2752520 | tf_op jit(solution)/shard_map/near_corner/ppermute | solution.py:134
  82.1 26.5 %copy-start.18 = (bf16[3,448,256]{2,1,0:T(8,128)(2,1)}, bf16[3,448,256]{2,1,0:T(8,128)(2,1)S(1)}, u32[]{:S(2)}) copy-start(bf16[3,448,256]{2,1,0:T(8,128)(2,1)S(1)} %collective-permute-done.10.refs_6_) | copy-start | bytes 2064388
  82.1 43.0 %collective-permute-start.12 = (bf16[3,448,256]{2,1,0:T(8,128)(2,1)}, bf16[3,448,256]{2,1,0:T(8,128)(2,1)}, u32[]{:S(2)}, u32[]{:S(2)}) collective-permute-start(bf16[3,448,256]{2,1,0:T(8,128)(2,1)} %collective-permute-done.8), channel_id=1, source_target_pairs={{1,0},{2,3},{5,4},{6,7},{9,8},{10,11},{13,12},{14,15},{17,16},{18,... | collective-permute-start | bytes 2064392 | tf_op jit(solution)/shard_map/end1_other/ppermute | solution.py:134
  108.1 24.6 %collective-permute-start.15 = (bf16[2,2,448,256]{3,2,1,0:T(8,128)(2,1)}, bf16[2,2,448,256]{3,2,1,0:T(8,128)(2,1)}, u32[]{:S(2)}, u32[]{:S(2)}) collective-permute-start(bf16[2,2,448,256]{3,2,1,0:T(8,128)(2,1)} %pad_maximum_fusion.1.refs_15_.refs_3_), channel_id=1, source_target_pairs={{0,16},{1,17},{2,18},{3,19},{4,20},{5,21},{6,22},{7,23},{8,0},{9,1... | collective-permute-start | bytes 2752520 | tf_op jit(solution)/shard_map/far_meet/ppermute | solution.py:134
  108.6 24.0 %collective-permute-start.16 = (bf16[2,2,448,256]{3,2,1,0:T(8,128)(2,1)}, bf16[2,2,448,256]{3,2,1,0:T(8,128)(2,1)}, u32[]{:S(2)}, u32[]{:S(2)}) collective-permute-start(bf16[2,2,448,256]{3,2,1,0:T(8,128)(2,1)} %pad_maximum_fusion.1.refs_15_.refs_3_), channel_id=1, source_target_pairs={{8,16},{9,17},{10,18},{11,19},{12,20},{13,21},{14,22},{15,23},{16,... | collective-permute-start | bytes 2752520 | tf_op jit(solution)/shard_map/far_corner/ppermute | solution.py:134
  110.4 22.2 %collective-permute-start.11 = (bf16[3,448,256]{2,1,0:T(8,128)(2,1)}, bf16[3,448,256]{2,1,0:T(8,128)(2,1)S(1)}, u32[]{:S(2)}, u32[]{:S(2)}) collective-permute-start(bf16[3,448,256]{2,1,0:T(8,128)(2,1)} %copy-done.18), channel_id=1, source_target_pairs={{1,0},{2,3},{5,4},{6,7},{9,8},{10,11},{13,12},{14,15},{17,16},{18,... | collective-permute-start | bytes 2064392 | tf_op jit(solution)/shard_map/end2_other/ppermute | solution.py:134
  140.3 4.1 %collective-permute-start.20 = (bf16[2,2,2,448,256]{4,3,2,1,0:T(8,128)(2,1)}, bf16[2,2,2,448,256]{4,3,2,1,0:T(8,128)(2,1)S(1)}, u32[]{:S(2)}, u32[]{:S(2)}) collective-permute-start(bf16[2,2,2,448,256]{4,3,2,1,0:T(8,128)(2,1)} %get-tuple-element.49), channel_id=1, source_target_pairs={{0,4},{1,5},{2,6},{3,7},{4,0},{5,1},{6,2},{7,3},{8,12},{9,13},{10,... | collective-permute-start | bytes 5505032 | tf_op jit(solution)/shard_map/out_core/ppermute | solution.py:134
  140.4 9.6 %collective-permute-start.17 = (bf16[528,256]{1,0:T(8,128)(2,1)}, bf16[528,256]{1,0:T(8,128)(2,1)S(1)}, u32[]{:S(2)}, u32[]{:S(2)}) collective-permute-start(bf16[528,256]{1,0:T(8,128)(2,1)} %get-tuple-element.48), channel_id=1, source_target_pairs={{0,16},{1,17},{2,18},{3,19},{4,20},{5,21},{6,22},{7,23},{8,24},{9,... | collective-permute-start | bytes 811016 | tf_op jit(solution)/shard_map/h_ctx/ppermute | solution.py:134
  141.2 8.8 %collective-permute-start.18 = (bf16[528,256]{1,0:T(8,128)(2,1)S(1)}, bf16[528,256]{1,0:T(8,128)(2,1)}, u32[]{:S(2)}, u32[]{:S(2)}) collective-permute-start(bf16[528,256]{1,0:T(8,128)(2,1)S(1)} %get-tuple-element.50.refs_1_), channel_id=1, source_target_pairs={{0,8},{1,9},{2,10},{3,11},{4,12},{5,13},{6,14},{7,15},{8,0},{9,1},... | collective-permute-start | bytes 811016 | tf_op jit(solution)/shard_map/h_y/ppermute | solution.py:134
  142.5 13.7 %collective-permute-start.19 = (bf16[528,256]{1,0:T(8,128)(2,1)}, bf16[528,256]{1,0:T(8,128)(2,1)}, u32[]{:S(2)}, u32[]{:S(2)}) collective-permute-start(bf16[528,256]{1,0:T(8,128)(2,1)} %get-tuple-element.48), channel_id=1, source_target_pairs={{0,24},{1,25},{2,26},{3,27},{4,28},{5,29},{6,30},{7,31},{8,16},{9,... | collective-permute-start | bytes 811016 | tf_op jit(solution)/shard_map/h_diag/ppermute | solution.py:134
  148.0 12.4 %copy-start.9 = (bf16[2,256,896]{2,1,0:T(8,128)(2,1)S(1)}, bf16[2,256,896]{2,1,0:T(8,128)(2,1)}, u32[]{:S(2)}) copy-start(bf16[2,256,896]{2,1,0:T(8,128)(2,1)} %fusion.2.refs_7_) | copy-start | bytes 2752516
  156.2 4.1 %collective-permute-start.21 = (bf16[528,256]{1,0:T(8,128)(2,1)S(1)}, bf16[528,256]{1,0:T(8,128)(2,1)S(1)}, u32[]{:S(2)}, u32[]{:S(2)}) collective-permute-start(bf16[528,256]{1,0:T(8,128)(2,1)S(1)} %get-tuple-element.50.refs_1_), channel_id=1, source_target_pairs={{0,4},{1,5},{2,6},{3,7},{4,0},{5,1},{6,2},{7,3},{8,12},{9,13},{10,... | collective-permute-start | bytes 811016 | tf_op jit(solution)/shard_map/h_core/ppermute | solution.py:134
  156.2 4.2 %collective-permute-start.22 = (bf16[528,256]{1,0:T(8,128)(2,1)S(1)}, bf16[528,256]{1,0:T(8,128)(2,1)S(1)}, u32[]{:S(2)}, u32[]{:S(2)}) collective-permute-start(bf16[528,256]{1,0:T(8,128)(2,1)S(1)} %collective-permute-done.17.refs_2_), channel_id=1, source_target_pairs={{0,4},{1,5},{2,6},{3,7},{4,0},{5,1},{6,2},{7,3},{8,12},{9,13},{10,... | collective-permute-start | bytes 811016 | tf_op jit(solution)/shard_map/h_core/ppermute | solution.py:134
  156.8 3.7 %collective-permute-start.23 = (bf16[528,256]{1,0:T(8,128)(2,1)}, bf16[528,256]{1,0:T(8,128)(2,1)S(1)}, u32[]{:S(2)}, u32[]{:S(2)}) collective-permute-start(bf16[528,256]{1,0:T(8,128)(2,1)} %collective-permute-done.18.refs_3_), channel_id=1, source_target_pairs={{0,4},{1,5},{2,6},{3,7},{4,0},{5,1},{6,2},{7,3},{8,12},{9,13},{10,... | collective-permute-start | bytes 811016 | tf_op jit(solution)/shard_map/h_core/ppermute | solution.py:134
  156.8 3.7 %collective-permute-start.24 = (bf16[528,256]{1,0:T(8,128)(2,1)}, bf16[528,256]{1,0:T(8,128)(2,1)S(1)}, u32[]{:S(2)}, u32[]{:S(2)}) collective-permute-start(bf16[528,256]{1,0:T(8,128)(2,1)} %collective-permute-done.19.refs_4_), channel_id=1, source_target_pairs={{0,4},{1,5},{2,6},{3,7},{4,0},{5,1},{6,2},{7,3},{8,12},{9,13},{10,... | collective-permute-start | bytes 811016 | tf_op jit(solution)/shard_map/h_core/ppermute | solution.py:134
  (21 other events, 70.5 us)

commit v8 on v7

--- a/solution.py
+++ b/solution.py
@@ -591,7 +591,7 @@
     def carry(blocks, name):
         return blocks, move(blocks, meet, name + "_meet"), move(blocks, corner, name + "_corner")
 
-    near = carry(after(near_blocks, third_kept), "near")
+    near = carry(after(near_blocks, first_x), "near")
 
     columns = width // lax.axis_size("tp")
 
@@ -601,7 +601,7 @@
         scale = lax.dynamic_slice_in_dim(in_scale, t * columns, columns, 0)
         return (jnp.where(part >= level, part, 0).astype(jnp.float32) * scale).astype(jnp.bfloat16)
 
-    res, dec_res = gate(after(spikes, second_x)), gate(after(dec_spikes, second_x))
+    res, dec_res = gate(after(spikes, mid2_other)), gate(after(dec_spikes, mid2_other))
     fourth_kept = jnp.where(is_end, end2_kept, mid2_kept)
     far = carry(after(jnp.stack([third_kept[3:], fourth_kept[3:]]), near[1], near[2]), "far")
     stage = (mid2_other, end1_other, summed, res, dec_res)

time: 165 us -> 164 us (level)
  starting transfers between devices: 25.8 us -> 29.2 us
  local copies, waits for them, and re-layouts: 18.4 us -> 16.2 us
  waiting for transfers between devices: 84.9 us -> 82.9 us
    ppermute x25, starting transfers between devices: 25.8 us -> 29.2 us  [move(): return lax.ppermute(value, AXES, pairs)]
    unnamed x56, local copies, waits for them, and re-layouts: 16.8 us -> 14.6 us
    ppermute x25, waiting for transfers between devices: 84.9 us -> 82.9 us  [move(): return lax.ppermute(value, AXES, pairs)]
  transfers between devices with their start and end apart: 25 -> 25, of which waited for: 10 -> 11; matrix products, arithmetic and copies ran while one was open for 4% -> 4% of each run, Pallas kernels for 10% -> 10%
where the time goes in v8:
time: 164 us; the launch traced here: 163 us
  waiting for transfers between devices  82.9 us (51%)
  starting transfers between devices  29.2 us (18%)
  Pallas kernels  27.7 us (17%)
  local copies, waits for them, and re-layouts  16.2 us (10%)
  other arithmetic  5.6 us (3%)
    ppermute x25, waiting for transfers between devices, move(): return lax.ppermute(value, AXES, pairs)  82.9 us
    ppermute x25, starting transfers between devices, move(): return lax.ppermute(value, AXES, pairs)  29.2 us
    unnamed x56, local copies, waits for them, and re-layouts  14.6 us
    pallas_call x2, Pallas kernels, project(): pl.pallas_call(lambda *refs: project_kernel(steps, bool(earlier), *refs),...  9.99 us
    pallas_call x1, Pallas kernels, attend(): pl.pallas_call(lambda *refs: attend_kernel(dims, *refs), grid_spec=pltpu....  7.66 us
    pallas_call x2, Pallas kernels, combine(): pl.pallas_call(lambda *refs: combine_kernel(bool(rest), *refs), grid_spec...  6.25 us
  transfers between devices with their start and end apart: 25, of which 11 were waited for; matrix products, arithmetic and copies ran while one was open for 4% of the time, Pallas kernels for 10%

profile of v8, /device:TPU:0, one launch (start us, length us, event | category | flops | bytes accessed | tf_op | source)
XLA Modules:
  0.0 162.9 jit_solution(15469085856116412843)
XLA Ops:
  0.8 1.3 copy-done.8
  3.8 3.1 %collective-permute-start.2 = (bf16[5,448,256]{2,1,0:T(8,128)(2,1)S(1)}, bf16[5,448,256]{2,1,0:T(8,128)(2,1)}, u32[]{:S(2)}, u32[]{:S(2)}) collective-permute-start(bf16[5,448,256]{2,1,0:T(8,128)(2,1)S(1)} %get-tuple-element.34.refs_5_), channel_id=1, source_target_pairs={{0,1},{1,0},{2,3},{3,2},{4,5},{5,4},{6,7},{7,6},{8,9},{9,8},{10,11... | collective-permute-start | bytes 3440648 | tf_op jit(solution)/shard_map/pair_kept/ppermute | solution.py:134
  6.9 1.7 %collective-permute-start.3 = (bf16[5,448,256]{2,1,0:T(8,128)(2,1)S(1)}, bf16[5,448,256]{2,1,0:T(8,128)(2,1)}, u32[]{:S(2)}, u32[]{:S(2)}) collective-permute-start(bf16[5,448,256]{2,1,0:T(8,128)(2,1)S(1)} %get-tuple-element.34.refs_5_), channel_id=1, source_target_pairs={{1,2},{2,1},{5,6},{6,5},{9,10},{10,9},{13,14},{14,13},{17,18},{18,... | collective-permute-start | bytes 3440648 | tf_op jit(solution)/shard_map/mid1_kept/ppermute | solution.py:134
  8.6 1.5 collective-permute-start
  10.1 3.1 %copy-done.3 = s32[2,256,3584]{2,1,0:T(8,128)S(1)} copy-done((s32[2,256,3584]{2,1,0:T(8,128)S(1)}, s32[2,256,3584]{2,1,0:T(8,128)}, u32[]{:S(2)}) %copy-start.3) | copy-done | bytes 7340056
  13.3 1.8 %embed.1.refs_1_ = bf16[4,512,896]{2,1,0:T(8,128)(2,1)S(1)} custom-call(s32[512,3584]{1,0:T(8,128)S(1)} %bitcast.20, s32[3584]{0:T(1024)S(1)} %copy-done.26, f32[3584]{0:T(1024)S(1)} %copy-done.25), custom_call_target="tpu_custom_call" | custom-call | tf_op jit(solution)/shard_map/embed/pallas_call | solution.py:246
  15.3 1.6 copy-done.1
  16.9 8.8 %collective-permute-done.refs_7_ = bf16[3,448,256]{2,1,0:T(8,128)(2,1)} collective-permute-done((bf16[3,448,256]{2,1,0:T(8,128)(2,1)S(1)}, bf16[3,448,256]{2,1,0:T(8,128)(2,1)}, u32[]{:S(2)}, u32[]{:S(2)}) %collective-permute-start) | collective-permute-done | bytes 688160 | tf_op jit(solution)/shard_map/pre_w/ppermute | solution.py:134
  25.6 3.1 %collective-permute-start.7 = (bf16[3,448,256]{2,1,0:T(8,128)(2,1)}, bf16[3,448,256]{2,1,0:T(8,128)(2,1)S(1)}, u32[]{:S(2)}, u32[]{:S(2)}) collective-permute-start(bf16[3,448,256]{2,1,0:T(8,128)(2,1)} %collective-permute-done.refs_7_), channel_id=1, source_target_pairs={{0,1},{1,0},{2,3},{3,2},{4,5},{5,4},{6,7},{7,6},{8,9},{9,8},{10,11... | collective-permute-start | bytes 2064392 | tf_op jit(solution)/shard_map/pair_other/ppermute | solution.py:134
  28.8 1.5 collective-permute-start.8
  30.3 1.5 collective-permute-start.1
  31.8 1.4 collective-permute-done.2.refs_6_
  33.8 13.1 %collective-permute-done.7.refs_8_ = bf16[3,448,256]{2,1,0:T(8,128)(2,1)S(1)} collective-permute-done((bf16[3,448,256]{2,1,0:T(8,128)(2,1)}, bf16[3,448,256]{2,1,0:T(8,128)(2,1)S(1)}, u32[]{:S(2)}, u32[]{:S(2)}) %collective-permute-start.7) | collective-permute-done | bytes 688160 | tf_op jit(solution)/shard_map/pair_other/ppermute | solution.py:134
  50.9 19.4 %collective-permute-done.1.refs_2_ = bf16[4,256,896]{2,1,0:T(8,128)(2,1)S(1)} collective-permute-done((bf16[4,256,896]{2,1,0:T(8,128)(2,1)S(1)}, bf16[4,256,896]{2,1,0:T(8,128)(2,1)S(1)}, u32[]{:S(2)}, u32[]{:S(2)}) %collective-permute-start.1) | collective-permute-done | bytes 1835040 | tf_op jit(solution)/shard_map/x_ctx/ppermute | solution.py:134
  70.3 7.6 %collective-permute-done.9 = bf16[5,448,256]{2,1,0:T(8,128)(2,1)S(1)} collective-permute-done((bf16[5,448,256]{2,1,0:T(8,128)(2,1)}, bf16[5,448,256]{2,1,0:T(8,128)(2,1)S(1)}, u32[]{:S(2)}, u32[]{:S(2)}) %collective-permute-start.9) | collective-permute-done | bytes 1146912 | tf_op jit(solution)/shard_map/end1_kept/ppermute | solution.py:134
  78.6 1.5 collective-permute-start.13
  83.5 20.2 %collective-permute-done.6 = bf16[5,448,256]{2,1,0:T(8,128)(2,1)S(1)} collective-permute-done((bf16[5,448,256]{2,1,0:T(8,128)(2,1)S(1)}, bf16[5,448,256]{2,1,0:T(8,128)(2,1)S(1)}, u32[]{:S(2)}, u32[]{:S(2)}) %collective-permute-start.6) | collective-permute-done | bytes 1146912 | tf_op jit(solution)/shard_map/end2_kept/ppermute | solution.py:134
  106.9 1.5 collective-permute-start.15
  108.4 1.6 collective-permute-start.16
  110.1 1.4 collective-permute-start.11
  111.6 2.7 %fusion.2.refs_7_ = bf16[2,256,896]{2,1,0:T(8,128)(2,1)} fusion(s32[2,256,3584]{2,1,0:T(8,128)} %param.9, s32[]{:T(128)S(6)} %select_n.60, f32[896]{0:T(1024)S(1)} %dynamic_slice.23, s32[896]{0:T(1024)S(1)} %dynamic_slice.22), kind=kLoop, calls=%fused_computation.3 | loop fusion | flops 2293760 | bytes 2759684 | tf_op jit(solution)/shard_map/convert_element_type | solution.py:602
  114.4 2.0 %copy-done.2 = bf16[4,512,896]{2,1,0:T(8,128)(2,1)S(1)} copy-done((bf16[4,512,896]{2,1,0:T(8,128)(2,1)S(1)}, bf16[4,512,896]{2,1,0:T(8,128)(2,1)}, u32[]{:S(2)}) %copy-start.2) | copy-done | bytes 3670040
  116.4 6.1 %project.2.refs_7_ = f32[1040,768]{1,0:T(8,128)S(1)} custom-call(s32[9]{0:T(128)S(1)} %stack.80.scalars.refs_0_, bf16[4,512,896]{2,1,0:T(8,128)(2,1)S(1)} %copy-done.2, bf16[4,256,896]{2,1,0:T(8,128)(2,1)S(1)} %collective-permute-done.1.refs_2_, bf16[4,256,896]{2,1,0:T(8,128)(2,1)} %collective-permute-done.5.refs_3_, ...), custom_call_target="tpu_custom_call" | custom-call | tf_op jit(solution)/shard_map/project/pallas_call | solution.py:305
  124.0 3.9 %project.3.refs_8_ = f32[1040,768]{1,0:T(8,128)S(1)} custom-call(s32[9]{0:T(128)S(1)} %stack.80.scalars.refs_0_, bf16[4,512,896]{2,1,0:T(8,128)(2,1)S(1)} %copy-done.2, bf16[4,256,896]{2,1,0:T(8,128)(2,1)S(1)} %collective-permute-done.1.refs_2_, bf16[4,256,896]{2,1,0:T(8,128)(2,1)} %collective-permute-done.5.refs_3_, ...), custom_call_target="tpu_custom_call" | custom-call | tf_op jit(solution)/shard_map/project/pallas_call | solution.py:305
  127.9 3.8 %collective-permute-done.11.refs_7_ = bf16[3,448,256]{2,1,0:T(8,128)(2,1)S(1)} collective-permute-done((bf16[3,448,256]{2,1,0:T(8,128)(2,1)}, bf16[3,448,256]{2,1,0:T(8,128)(2,1)S(1)}, u32[]{:S(2)}, u32[]{:S(2)}) %collective-permute-start.11) | collective-permute-done | bytes 688160 | tf_op jit(solution)/shard_map/end2_other/ppermute | solution.py:134
  131.8 7.7 %attend.1 = (bf16[528,256]{1,0:T(8,128)(2,1)S(1)}, bf16[528,256]{1,0:T(8,128)(2,1)}, bf16[2,2,2,448,256]{4,3,2,1,0:T(8,128)(2,1)}) custom-call(s32[9]{0:T(128)S(1)} %stack.80.scalars.refs_0_, bf16[4,512,896]{2,1,0:T(8,128)(2,1)S(1)} %copy-done.2, bf16[4,256,896]{2,1,0:T(8,128)(2,1)S(1)} %collective-permute-done.1.refs_2_, ...), custom_call_target="tpu_custom_call" | custom-call | flops 2862612480 | bytes 3194880 | tf_op jit(solution)/shard_map/attend/pallas_call | solution.py:420
  139.5 1.4 collective-permute-start.17
  140.9 1.7 %collective-permute-start.18 = (bf16[528,256]{1,0:T(8,128)(2,1)S(1)}, bf16[528,256]{1,0:T(8,128)(2,1)}, u32[]{:S(2)}, u32[]{:S(2)}) collective-permute-start(bf16[528,256]{1,0:T(8,128)(2,1)S(1)} %get-tuple-element.50.refs_1_), channel_id=1, source_target_pairs={{0,8},{1,9},{2,10},{3,11},{4,12},{5,13},{6,14},{7,15},{8,0},{9,1},... | collective-permute-start | bytes 811016 | tf_op jit(solution)/shard_map/h_y/ppermute | solution.py:134
  147.1 2.0 %collective-permute-done.17.refs_2_ = bf16[528,256]{1,0:T(8,128)(2,1)S(1)} collective-permute-done((bf16[528,256]{1,0:T(8,128)(2,1)}, bf16[528,256]{1,0:T(8,128)(2,1)S(1)}, u32[]{:S(2)}, u32[]{:S(2)}) %collective-permute-start.17) | collective-permute-done | bytes 270368 | tf_op jit(solution)/shard_map/h_ctx/ppermute | solution.py:134
  149.1 5.4 %collective-permute-done.18.refs_3_ = bf16[528,256]{1,0:T(8,128)(2,1)} collective-permute-done((bf16[528,256]{1,0:T(8,128)(2,1)S(1)}, bf16[528,256]{1,0:T(8,128)(2,1)}, u32[]{:S(2)}, u32[]{:S(2)}) %collective-permute-start.18) | collective-permute-done | bytes 270368 | tf_op jit(solution)/shard_map/h_y/ppermute | solution.py:134
  156.4 3.1 %combine.2.refs_6_ = f32[528,896]{1,0:T(8,128)S(1)} custom-call(s32[4]{0:T(128)S(1)} %pad_add_fusion.scalars.refs_0_, bf16[528,256]{1,0:T(8,128)(2,1)S(1)} %get-tuple-element.50.refs_1_, bf16[528,256]{1,0:T(8,128)(2,1)S(1)} %collective-permute-done.17.refs_2_, bf16[528,256]{1,0:T(8,128)(2,1)} %collective-permute-done.18.refs_3_, ...), custom_call_target="tpu_custom_call" | custom-call | tf_op jit(solution)/shard_map/combine/pallas_call | solution.py:521
  159.6 3.1 %combine.3 = (bf16[2,256,896]{2,1,0:T(8,128)(2,1)}, bf16[4,2,896]{2,1,0:T(2,128)(2,1)}) custom-call(s32[4]{0:T(128)S(1)} %pad_add_fusion.scalars.refs_0_, bf16[528,256]{1,0:T(8,128)(2,1)S(1)} %collective-permute-done.21.refs_1_, bf16[528,256]{1,0:T(8,128)(2,1)S(1)} %collective-permute-done.22.refs_2_, bf16[528,256]{1,0:T(8,128)(2,1)S(1)} %collective-permute-done.23.refs_3_, ...), custom_call_target="tpu_custom_call" | custom-call | tf_op jit(solution)/shard_map/combine/pallas_call | solution.py:521
  (100 shorter events, 21.9 us)
Async XLA Ops:
  0.6 109.5 %copy-start = (f32[4,128]{1,0:T(4,128)S(1)}, f32[4,128]{1,0:T(4,128)}, u32[]{:S(2)}) copy-start(f32[4,128]{1,0:T(4,128)} %param.15) | copy-start | bytes 6148
  0.6 9.5 %copy-start.26 = (s32[3584]{0:T(1024)S(1)}, s32[3584]{0:T(1024)}, u32[]{:S(2)}) copy-start(s32[3584]{0:T(1024)} %refs_1_.3) | copy-start | bytes 43012
  3.8 44.5 %copy-start.16 = (bf16[5,448,256]{2,1,0:T(8,128)(2,1)}, bf16[5,448,256]{2,1,0:T(8,128)(2,1)S(1)}, u32[]{:S(2)}) copy-start(bf16[5,448,256]{2,1,0:T(8,128)(2,1)S(1)} %get-tuple-element.34.refs_5_) | copy-start | bytes 3440644
  3.8 29.3 %collective-permute-start.2 = (bf16[5,448,256]{2,1,0:T(8,128)(2,1)S(1)}, bf16[5,448,256]{2,1,0:T(8,128)(2,1)}, u32[]{:S(2)}, u32[]{:S(2)}) collective-permute-start(bf16[5,448,256]{2,1,0:T(8,128)(2,1)S(1)} %get-tuple-element.34.refs_5_), channel_id=1, source_target_pairs={{0,1},{1,0},{2,3},{3,2},{4,5},{5,4},{6,7},{7,6},{8,9},{9,8},{10,11... | collective-permute-start | bytes 3440648 | tf_op jit(solution)/shard_map/pair_kept/ppermute | solution.py:134
  6.9 26.2 %collective-permute-start.3 = (bf16[5,448,256]{2,1,0:T(8,128)(2,1)S(1)}, bf16[5,448,256]{2,1,0:T(8,128)(2,1)}, u32[]{:S(2)}, u32[]{:S(2)}) collective-permute-start(bf16[5,448,256]{2,1,0:T(8,128)(2,1)S(1)} %get-tuple-element.34.refs_5_), channel_id=1, source_target_pairs={{1,2},{2,1},{5,6},{6,5},{9,10},{10,9},{13,14},{14,13},{17,18},{18,... | collective-permute-start | bytes 3440648 | tf_op jit(solution)/shard_map/mid1_kept/ppermute | solution.py:134
  8.6 17.0 %collective-permute-start = (bf16[3,448,256]{2,1,0:T(8,128)(2,1)S(1)}, bf16[3,448,256]{2,1,0:T(8,128)(2,1)}, u32[]{:S(2)}, u32[]{:S(2)}) collective-permute-start(bf16[3,448,256]{2,1,0:T(8,128)(2,1)S(1)} %get-tuple-element.28), channel_id=1, source_target_pairs={{0,16},{1,17},{2,18},{3,19},{4,20},{5,21},{6,22},{7,23},{8,24},{9,... | collective-permute-start | bytes 2064392 | tf_op jit(solution)/shard_map/pre_w/ppermute | solution.py:134
  15.1 33.1 %copy-start.24 = (s32[4,2,3584]{2,1,0:T(2,128)S(1)}, s32[4,2,3584]{2,1,0:T(2,128)}, u32[]{:S(2)}) copy-start(s32[4,2,3584]{2,1,0:T(2,128)} %refs_0_) | copy-start | bytes 344068
  25.6 21.3 %collective-permute-start.7 = (bf16[3,448,256]{2,1,0:T(8,128)(2,1)}, bf16[3,448,256]{2,1,0:T(8,128)(2,1)S(1)}, u32[]{:S(2)}, u32[]{:S(2)}) collective-permute-start(bf16[3,448,256]{2,1,0:T(8,128)(2,1)} %collective-permute-done.refs_7_), channel_id=1, source_target_pairs={{0,1},{1,0},{2,3},{3,2},{4,5},{5,4},{6,7},{7,6},{8,9},{9,8},{10,11... | collective-permute-start | bytes 2064392 | tf_op jit(solution)/shard_map/pair_other/ppermute | solution.py:134
  28.8 18.2 %collective-permute-start.8 = (bf16[3,448,256]{2,1,0:T(8,128)(2,1)}, bf16[3,448,256]{2,1,0:T(8,128)(2,1)}, u32[]{:S(2)}, u32[]{:S(2)}) collective-permute-start(bf16[3,448,256]{2,1,0:T(8,128)(2,1)} %collective-permute-done.refs_7_), channel_id=1, source_target_pairs={{1,2},{2,1},{5,6},{6,5},{9,10},{10,9},{13,14},{14,13},{17,18},{18,... | collective-permute-start | bytes 2064392 | tf_op jit(solution)/shard_map/mid1_other/ppermute | solution.py:134
  30.3 40.0 %collective-permute-start.1 = (bf16[4,256,896]{2,1,0:T(8,128)(2,1)S(1)}, bf16[4,256,896]{2,1,0:T(8,128)(2,1)S(1)}, u32[]{:S(2)}, u32[]{:S(2)}) collective-permute-start(bf16[4,256,896]{2,1,0:T(8,128)(2,1)S(1)} %constant_dynamic-slice_fusion.1), channel_id=1, source_target_pairs={{0,16},{1,17},{2,18},{3,19},{4,20},{5,21},{6,22},{7,23},{8,24},{9,... | collective-permute-start | bytes 5505032 | tf_op jit(solution)/shard_map/x_ctx/ppermute | solution.py:134
  33.1 16.4 %collective-permute-start.4 = (bf16[5,448,256]{2,1,0:T(8,128)(2,1)}, bf16[5,448,256]{2,1,0:T(8,128)(2,1)S(1)}, u32[]{:S(2)}, u32[]{:S(2)}) collective-permute-start(bf16[5,448,256]{2,1,0:T(8,128)(2,1)} %collective-permute-done.2.refs_6_), channel_id=1, source_target_pairs={{1,2},{2,1},{5,6},{6,5},{9,10},{10,9},{13,14},{14,13},{17,18},{18,... | collective-permute-start | bytes 3440648 | tf_op jit(solution)/shard_map/mid2_kept/ppermute | solution.py:134
  46.9 31.0 %copy-start.20 = (bf16[3,448,256]{2,1,0:T(8,128)(2,1)}, bf16[3,448,256]{2,1,0:T(8,128)(2,1)S(1)}, u32[]{:S(2)}) copy-start(bf16[3,448,256]{2,1,0:T(8,128)(2,1)S(1)} %collective-permute-done.7.refs_8_) | copy-start | bytes 2064388
  46.9 31.0 %collective-permute-start.9 = (bf16[5,448,256]{2,1,0:T(8,128)(2,1)}, bf16[5,448,256]{2,1,0:T(8,128)(2,1)S(1)}, u32[]{:S(2)}, u32[]{:S(2)}) collective-permute-start(bf16[5,448,256]{2,1,0:T(8,128)(2,1)} %collective-permute-done.3), channel_id=1, source_target_pairs={{1,0},{2,3},{5,4},{6,7},{9,8},{10,11},{13,12},{14,15},{17,16},{18,... | collective-permute-start | bytes 3440648 | tf_op jit(solution)/shard_map/end1_kept/ppermute | solution.py:134
  49.6 54.1 %collective-permute-start.6 = (bf16[5,448,256]{2,1,0:T(8,128)(2,1)S(1)}, bf16[5,448,256]{2,1,0:T(8,128)(2,1)S(1)}, u32[]{:S(2)}, u32[]{:S(2)}) collective-permute-start(bf16[5,448,256]{2,1,0:T(8,128)(2,1)S(1)} %collective-permute-done.4), channel_id=1, source_target_pairs={{1,0},{2,3},{5,4},{6,7},{9,8},{10,11},{13,12},{14,15},{17,16},{18,... | collective-permute-start | bytes 3440648 | tf_op jit(solution)/shard_map/end2_kept/ppermute | solution.py:134
  77.9 4.3 %collective-permute-start.10 = (bf16[3,448,256]{2,1,0:T(8,128)(2,1)S(1)}, bf16[3,448,256]{2,1,0:T(8,128)(2,1)S(1)}, u32[]{:S(2)}, u32[]{:S(2)}) collective-permute-start(bf16[3,448,256]{2,1,0:T(8,128)(2,1)S(1)} %collective-permute-done.7.refs_8_), channel_id=1, source_target_pairs={{1,2},{2,1},{5,6},{6,5},{9,10},{10,9},{13,14},{14,13},{17,18},{18,... | collective-permute-start | bytes 2064392 | tf_op jit(solution)/shard_map/mid2_other/ppermute | solution.py:134
  78.6 26.4 %collective-permute-start.13 = (bf16[2,2,448,256]{3,2,1,0:T(8,128)(2,1)S(1)}, bf16[2,2,448,256]{3,2,1,0:T(8,128)(2,1)S(1)}, u32[]{:S(2)}, u32[]{:S(2)}) collective-permute-start(bf16[2,2,448,256]{3,2,1,0:T(8,128)(2,1)S(1)} %pad_maximum_fusion.refs_12_.refs_0_), channel_id=1, source_target_pairs={{0,16},{1,17},{2,18},{3,19},{4,20},{5,21},{6,22},{7,23},{8,0},{9,1... | collective-permute-start | bytes 2752520 | tf_op jit(solution)/shard_map/near_meet/ppermute | solution.py:134
  80.1 25.8 %collective-permute-start.14 = (bf16[2,2,448,256]{3,2,1,0:T(8,128)(2,1)S(1)}, bf16[2,2,448,256]{3,2,1,0:T(8,128)(2,1)S(1)}, u32[]{:S(2)}, u32[]{:S(2)}) collective-permute-start(bf16[2,2,448,256]{3,2,1,0:T(8,128)(2,1)S(1)} %pad_maximum_fusion.refs_12_.refs_0_), channel_id=1, source_target_pairs={{8,16},{9,17},{10,18},{11,19},{12,20},{13,21},{14,22},{15,23},{16,... | collective-permute-start | bytes 2752520 | tf_op jit(solution)/shard_map/near_corner/ppermute | solution.py:134
  80.9 33.5 %collective-permute-start.5 = (bf16[4,256,896]{2,1,0:T(8,128)(2,1)S(1)}, bf16[4,256,896]{2,1,0:T(8,128)(2,1)}, u32[]{:S(2)}, u32[]{:S(2)}) collective-permute-start(bf16[4,256,896]{2,1,0:T(8,128)(2,1)S(1)} %collective-permute-done.1.refs_2_), channel_id=1, source_target_pairs={{0,4},{1,5},{2,6},{3,7},{4,0},{5,1},{6,2},{7,3},{8,12},{9,13},{10,... | collective-permute-start | bytes 5505032 | tf_op jit(solution)/shard_map/x_core/ppermute | solution.py:134
  82.2 26.2 %copy-start.18 = (bf16[3,448,256]{2,1,0:T(8,128)(2,1)}, bf16[3,448,256]{2,1,0:T(8,128)(2,1)S(1)}, u32[]{:S(2)}) copy-start(bf16[3,448,256]{2,1,0:T(8,128)(2,1)S(1)} %collective-permute-done.10.refs_6_) | copy-start | bytes 2064388
  82.2 40.3 %collective-permute-start.12 = (bf16[3,448,256]{2,1,0:T(8,128)(2,1)}, bf16[3,448,256]{2,1,0:T(8,128)(2,1)}, u32[]{:S(2)}, u32[]{:S(2)}) collective-permute-start(bf16[3,448,256]{2,1,0:T(8,128)(2,1)} %collective-permute-done.8), channel_id=1, source_target_pairs={{1,0},{2,3},{5,4},{6,7},{9,8},{10,11},{13,12},{14,15},{17,16},{18,... | collective-permute-start | bytes 2064392 | tf_op jit(solution)/shard_map/end1_other/ppermute | solution.py:134
  106.9 24.8 %collective-permute-start.15 = (bf16[2,2,448,256]{3,2,1,0:T(8,128)(2,1)}, bf16[2,2,448,256]{3,2,1,0:T(8,128)(2,1)}, u32[]{:S(2)}, u32[]{:S(2)}) collective-permute-start(bf16[2,2,448,256]{3,2,1,0:T(8,128)(2,1)} %pad_maximum_fusion.1.refs_15_.refs_3_), channel_id=1, source_target_pairs={{0,16},{1,17},{2,18},{3,19},{4,20},{5,21},{6,22},{7,23},{8,0},{9,1... | collective-permute-start | bytes 2752520 | tf_op jit(solution)/shard_map/far_meet/ppermute | solution.py:134
  108.4 23.3 %collective-permute-start.16 = (bf16[2,2,448,256]{3,2,1,0:T(8,128)(2,1)}, bf16[2,2,448,256]{3,2,1,0:T(8,128)(2,1)}, u32[]{:S(2)}, u32[]{:S(2)}) collective-permute-start(bf16[2,2,448,256]{3,2,1,0:T(8,128)(2,1)} %pad_maximum_fusion.1.refs_15_.refs_3_), channel_id=1, source_target_pairs={{8,16},{9,17},{10,18},{11,19},{12,20},{13,21},{14,22},{15,23},{16,... | collective-permute-start | bytes 2752520 | tf_op jit(solution)/shard_map/far_corner/ppermute | solution.py:134
  110.1 21.6 %collective-permute-start.11 = (bf16[3,448,256]{2,1,0:T(8,128)(2,1)}, bf16[3,448,256]{2,1,0:T(8,128)(2,1)S(1)}, u32[]{:S(2)}, u32[]{:S(2)}) collective-permute-start(bf16[3,448,256]{2,1,0:T(8,128)(2,1)} %copy-done.18), channel_id=1, source_target_pairs={{1,0},{2,3},{5,4},{6,7},{9,8},{10,11},{13,12},{14,15},{17,16},{18,... | collective-permute-start | bytes 2064392 | tf_op jit(solution)/shard_map/end2_other/ppermute | solution.py:134
  139.4 4.1 %collective-permute-start.20 = (bf16[2,2,2,448,256]{4,3,2,1,0:T(8,128)(2,1)}, bf16[2,2,2,448,256]{4,3,2,1,0:T(8,128)(2,1)S(1)}, u32[]{:S(2)}, u32[]{:S(2)}) collective-permute-start(bf16[2,2,2,448,256]{4,3,2,1,0:T(8,128)(2,1)} %get-tuple-element.49), channel_id=1, source_target_pairs={{0,4},{1,5},{2,6},{3,7},{4,0},{5,1},{6,2},{7,3},{8,12},{9,13},{10,... | collective-permute-start | bytes 5505032 | tf_op jit(solution)/shard_map/out_core/ppermute | solution.py:134
  139.5 9.6 %collective-permute-start.17 = (bf16[528,256]{1,0:T(8,128)(2,1)}, bf16[528,256]{1,0:T(8,128)(2,1)S(1)}, u32[]{:S(2)}, u32[]{:S(2)}) collective-permute-start(bf16[528,256]{1,0:T(8,128)(2,1)} %get-tuple-element.48), channel_id=1, source_target_pairs={{0,16},{1,17},{2,18},{3,19},{4,20},{5,21},{6,22},{7,23},{8,24},{9,... | collective-permute-start | bytes 811016 | tf_op jit(solution)/shard_map/h_ctx/ppermute | solution.py:134
  140.9 13.5 %collective-permute-start.18 = (bf16[528,256]{1,0:T(8,128)(2,1)S(1)}, bf16[528,256]{1,0:T(8,128)(2,1)}, u32[]{:S(2)}, u32[]{:S(2)}) collective-permute-start(bf16[528,256]{1,0:T(8,128)(2,1)S(1)} %get-tuple-element.50.refs_1_), channel_id=1, source_target_pairs={{0,8},{1,9},{2,10},{3,11},{4,12},{5,13},{6,14},{7,15},{8,0},{9,1},... | collective-permute-start | bytes 811016 | tf_op jit(solution)/shard_map/h_y/ppermute | solution.py:134
  142.6 12.8 %collective-permute-start.19 = (bf16[528,256]{1,0:T(8,128)(2,1)}, bf16[528,256]{1,0:T(8,128)(2,1)}, u32[]{:S(2)}, u32[]{:S(2)}) collective-permute-start(bf16[528,256]{1,0:T(8,128)(2,1)} %get-tuple-element.48), channel_id=1, source_target_pairs={{0,24},{1,25},{2,26},{3,27},{4,28},{5,29},{6,30},{7,31},{8,16},{9,... | collective-permute-start | bytes 811016 | tf_op jit(solution)/shard_map/h_diag/ppermute | solution.py:134
  147.1 12.5 %copy-start.9 = (bf16[2,256,896]{2,1,0:T(8,128)(2,1)S(1)}, bf16[2,256,896]{2,1,0:T(8,128)(2,1)}, u32[]{:S(2)}) copy-start(bf16[2,256,896]{2,1,0:T(8,128)(2,1)} %fusion.2.refs_7_) | copy-start | bytes 2752516
  155.4 4.1 %collective-permute-start.21 = (bf16[528,256]{1,0:T(8,128)(2,1)S(1)}, bf16[528,256]{1,0:T(8,128)(2,1)S(1)}, u32[]{:S(2)}, u32[]{:S(2)}) collective-permute-start(bf16[528,256]{1,0:T(8,128)(2,1)S(1)} %get-tuple-element.50.refs_1_), channel_id=1, source_target_pairs={{0,4},{1,5},{2,6},{3,7},{4,0},{5,1},{6,2},{7,3},{8,12},{9,13},{10,... | collective-permute-start | bytes 811016 | tf_op jit(solution)/shard_map/h_core/ppermute | solution.py:134
  155.4 4.2 %collective-permute-start.22 = (bf16[528,256]{1,0:T(8,128)(2,1)S(1)}, bf16[528,256]{1,0:T(8,128)(2,1)S(1)}, u32[]{:S(2)}, u32[]{:S(2)}) collective-permute-start(bf16[528,256]{1,0:T(8,128)(2,1)S(1)} %collective-permute-done.17.refs_2_), channel_id=1, source_target_pairs={{0,4},{1,5},{2,6},{3,7},{4,0},{5,1},{6,2},{7,3},{8,12},{9,13},{10,... | collective-permute-start | bytes 811016 | tf_op jit(solution)/shard_map/h_core/ppermute | solution.py:134
  155.9 3.7 %collective-permute-start.23 = (bf16[528,256]{1,0:T(8,128)(2,1)}, bf16[528,256]{1,0:T(8,128)(2,1)S(1)}, u32[]{:S(2)}, u32[]{:S(2)}) collective-permute-start(bf16[528,256]{1,0:T(8,128)(2,1)} %collective-permute-done.18.refs_3_), channel_id=1, source_target_pairs={{0,4},{1,5},{2,6},{3,7},{4,0},{5,1},{6,2},{7,3},{8,12},{9,13},{10,... | collective-permute-start | bytes 811016 | tf_op jit(solution)/shard_map/h_core/ppermute | solution.py:134
  155.9 3.7 %collective-permute-start.24 = (bf16[528,256]{1,0:T(8,128)(2,1)}, bf16[528,256]{1,0:T(8,128)(2,1)S(1)}, u32[]{:S(2)}, u32[]{:S(2)}) collective-permute-start(bf16[528,256]{1,0:T(8,128)(2,1)} %collective-permute-done.19.refs_4_), channel_id=1, source_target_pairs={{0,4},{1,5},{2,6},{3,7},{4,0},{5,1},{6,2},{7,3},{8,12},{9,13},{10,... | collective-permute-start | bytes 811016 | tf_op jit(solution)/shard_map/h_core/ppermute | solution.py:134
  (21 other events, 82.7 us)
